TPU v7x, 256 devices: a whole 4x4x8 slice. The times are simulated.
256 devices in a mesh: band: 8 (over x, core), pos: 32 (over y, z).
Axes of the slice: x: 4, y: 4, z: 8, core: 2. Of those that a mesh axis runs over, the one named last changes fastest.
Arguments:
- wigner: float32 [8, 512, 4096], P('band', 'pos'), may hold values from -6 to 6
- past_iterates: float32 [4, 8, 512, 4096], P(None, 'band', 'pos'), may hold values from -6 to 6
- past_residuals: float32 [4, 8, 512, 4096], P(None, 'band', 'pos'), may hold values from -3 to 3
- velocity: float32 [512, 4096], P('pos'), may hold values from 0.5 to 2
- out_rate: float32 [8, 4096], P('band'), may hold values from 0.0009765625 to 1
- inflow: float32 [8, 4096], P('band'), may hold values from -6 to 6
- offsets: int32 [4096], replicated, may hold values from 1 to 16
- directions: int32 [32], replicated, may hold values from 0 to 1
- coupling: int32 [8], replicated, may hold values from 0 to 7, as said below
Outputs:
- mixed: float32 [8, 512, 4096], P('band', 'pos')
- residual: float32 [8, 512, 4096], P('band', 'pos')
Inputs may be any that keep to these rules, and one draw needn't show every extreme that they name: directions: 1 marks blocks whose carriers move toward lower positions. coupling is a permutation of the 8 subbands.
All inputs are finite; a program needn't handle non-finite values.
Results may differ from a plain program's by a relative error of at most 0.00009.
Values sent between devices are 32-bit elements; how exact they have to be, the bound alone decides.
No kernel may reach another device: no remote copies, remote signals or barrier semaphores. Data moves between devices by JAX's collectives and lax.ppermute only.
A program may use at most 128 MiB of HBM per device.

v0:
```python
import functools

import jax
import jax.numpy as jnp
from jax import lax
from jax.experimental import pallas as pl
from jax.experimental.pallas import tpu as pltpu
from jax.sharding import Mesh
from jax.sharding import PartitionSpec as P

POS = ("pos_0", "pos_1")
BAND = ("band_0", "band_1")

MIX_STEP = 0.5
RIDGE_SCALE = 0.0001
LANES = 128
ROWS = 8
HIST = 4
PAIRS = [(i, j) for i in range(HIST) for j in range(i, HIST)]

VMEM = pl.BlockSpec(memory_space=pltpu.VMEM)
SMEM = pl.BlockSpec(memory_space=pltpu.SMEM)


def call(kernel, outs, in_specs, flops, nbytes):
    return pl.pallas_call(
        kernel,
        out_shape=outs,
        in_specs=in_specs,
        out_specs=jax.tree.map(lambda _: VMEM, outs),
        compiler_params=pltpu.CompilerParams(vmem_limit_bytes=24 * 2**20),
        cost_estimate=pl.CostEstimate(flops=flops, bytes_accessed=nbytes, transcendentals=0),
    )


def f32(*shape):
    return jax.ShapeDtypeStruct(shape, jnp.float32)


def tile(kb):
    return slice(kb * LANES, (kb + 1) * LANES)


def pick(x, index, axis):
    return jnp.take_along_axis(x, index, axis=axis, mode="promise_in_bounds")


def iota(axis):
    return lax.broadcasted_iota(jnp.int32, (ROWS, LANES), axis)


def spread_kernel(offsets, wigner, spread):
    cells, moments = wigner.shape
    tiles = moments // LANES
    per = spread.shape[2] // LANES
    lane = iota(1)
    zero = jnp.zeros((ROWS, LANES), jnp.float32)
    for kb in range(tiles):
        off = jnp.broadcast_to(offsets[:, tile(kb)], (ROWS, LANES))
        up, down = lane + off, lane - off
        up_in, down_in = up & (LANES - 1), down & (LANES - 1)
        for h in range(cells // ROWS):
            rows = slice(h * ROWS, (h + 1) * ROWS)
            here = wigner[rows, tile(kb)]
            nxt = pick(wigner[rows, tile(kb + 1)], up_in, 1) if kb + 1 < tiles else zero
            prv = pick(wigner[rows, tile(kb - 1)], down_in, 1) if kb else zero
            above = jnp.where(up < LANES, pick(here, up_in, 1), nxt)
            below = jnp.where(down >= 0, pick(here, down_in, 1), prv)
            spread[kb // per, rows, tile(kb % per)] = 0.5 * (above + below)


def route_kernel(coupling, held, routed):
    for s in range(routed.shape[0]):
        routed[s] = held[coupling[s]]


def scan_tile(back, a, b):
    row = iota(0)
    away = jnp.where(back, ROWS - 1 - row, row)
    a = [jnp.where(back, a[1], a[0]), jnp.where(back, a[0], a[1])]
    if b is not None:
        b = [jnp.where(back, b[1], b[0]), jnp.where(back, b[0], b[1])]
    for d in (1, 2, 4):
        source = jnp.where(back, row + d, row - d) & (ROWS - 1)
        keep = away >= d
        for h in range(2):
            if b is not None:
                b[h] = a[h] * jnp.where(keep, pick(b[h], source, 0), 0.0) + b[h]
            a[h] = a[h] * jnp.where(keep, pick(a[h], source, 0), 1.0)
    last = jnp.where(back, 0, ROWS - 1) + jnp.zeros_like(row)
    if b is not None:
        b[1] = a[1] * pick(b[0], last, 0) + b[1]
    a[1] = a[1] * pick(a[0], last, 0)
    ends = [pick(a[1], last, 0)]
    if b is not None:
        ends.append(pick(b[1], last, 0))
        b = [jnp.where(back, b[1], b[0]), jnp.where(back, b[0], b[1])]
    a = [jnp.where(back, a[1], a[0]), jnp.where(back, a[0], a[1])]
    return a, b, ends


def coefficients(velocity, out_rate, kb, h):
    v = velocity[h * ROWS : (h + 1) * ROWS, tile(kb)]
    r = jnp.broadcast_to(out_rate[:, tile(kb)], (ROWS, LANES))
    return v, r, 1.0 / (v + r)


def flag(directions, index):
    return jnp.full((ROWS, LANES), directions[index], jnp.int32) == 1


def down(x):
    return jnp.sum(x, axis=0, keepdims=True)


def early_kernel(directions, velocity, out_rate, past_iterates, past_residuals, sums, blends, gram):
    tiles = velocity.shape[1] // LANES
    halves = range(2)
    acc = [jnp.zeros((ROWS, LANES), jnp.float32) for _ in PAIRS]
    for kb in range(tiles):
        back = flag(directions, kb)
        slope = []
        for h in halves:
            v, _, inv = coefficients(velocity, out_rate, kb, h)
            slope.append(v * inv)
        reach, _, ends = scan_tile(back, slope, None)
        past = [[past_residuals[j, h * ROWS : (h + 1) * ROWS, tile(kb)] for h in halves] for j in range(HIST)]
        for j in range(HIST):
            for h in halves:
                rows = slice(h * ROWS, (h + 1) * ROWS)
                blends[j, rows, tile(kb)] = past_iterates[j, rows, tile(kb)] + MIX_STEP * past[j][h]
        for n, (i, j) in enumerate(PAIRS):
            acc[n] = acc[n] + (past[i][0] * past[j][0] + past[i][1] * past[j][1])
        sums[kb, 0:1, :] = ends[0][0:1]
        sums[kb, 1:2, :] = jnp.zeros((1, LANES), jnp.float32)
        for j in range(HIST):
            sums[kb, 2 + j : 3 + j, :] = down(past[j][0] * reach[0] + past[j][1] * reach[1])
        sums[kb, 6:7, :] = down(reach[0] * reach[0] + reach[1] * reach[1])
        sums[kb, 7:8, :] = jnp.zeros((1, LANES), jnp.float32)
    gram[...] = jnp.zeros(gram.shape, jnp.float32)
    for n in range(len(PAIRS)):
        gram[6 + n : 7 + n, :] = down(acc[n])


def local_kernel(
    directions, spread, partner, velocity, out_rate, wigner, past_residuals, early_sums, early_gram, reach_out, rest, sums, gram
):
    tiles = velocity.shape[1] // LANES
    per = spread.shape[2] // LANES
    halves = range(2)
    acc = [jnp.zeros((ROWS, LANES), jnp.float32) for _ in range(HIST + 1)]
    for kb in range(tiles):
        back = flag(directions, kb)
        slope, offset = [], []
        for h in halves:
            rows = slice(h * ROWS, (h + 1) * ROWS)
            v, r, inv = coefficients(velocity, out_rate, kb, h)
            gain = r * 0.5 * (spread[kb // per, rows, tile(kb % per)] + partner[kb // per, rows, tile(kb % per)])
            slope.append(v * inv)
            offset.append(gain * inv)
        reach, run, ends = scan_tile(back, slope, offset)
        left = []
        for h in halves:
            rows = slice(h * ROWS, (h + 1) * ROWS)
            left.append(run[h] - wigner[rows, tile(kb)])
            rest[rows, tile(kb)] = left[h]
            reach_out[rows, tile(kb)] = reach[h]
        for j in range(HIST):
            for h in halves:
                acc[j] = acc[j] + past_residuals[j, h * ROWS : (h + 1) * ROWS, tile(kb)] * left[h]
        acc[HIST] = acc[HIST] + (left[0] * left[0] + left[1] * left[1])
        crossed = down(reach[0] * left[0] + reach[1] * left[1])
        row = iota(0)
        early = early_sums[kb]
        sums[kb] = jnp.where(row == 1, ends[1], jnp.where(row == 7, jnp.broadcast_to(crossed, (ROWS, LANES)), early))
    gram[...] = early_gram[...]
    for n in range(HIST + 1):
        gram[1 + n : 2 + n, :] = down(acc[n])


def carry_kernel(directions, where_at, inflow, sums, gram, message):
    blocks = sums.shape[0]
    at = where_at[0]
    back = directions[at]
    start = pl.multiple_of(at * LANES, LANES)
    carry = inflow[:, pl.ds(start, LANES)]
    row = iota(0)
    acc = jnp.zeros((ROWS, LANES), jnp.float32)
    for step in range(blocks):
        p = jnp.where(back == 1, blocks - 1 - step, step)
        part = sums[p]
        wide = jnp.broadcast_to(carry, (ROWS, LANES))
        message[p, 0:1, :] = carry
        acc = acc + part * jnp.where(row == 6, wide * wide, jnp.where(row == 7, 2.0 * wide, wide))
        carry = part[0:1] * carry + part[1:2]
    terms = jnp.concatenate([acc[2:6], acc[6:7] + acc[7:8]], axis=0) + gram[1:6]
    for p in range(blocks):
        message[p, 1:6, :] = terms
        message[p, 6:, :] = gram[6:]


def finish_kernel(message, reach, rest, wigner, residual, base, gram):
    tiles = wigner.shape[1] // LANES
    total = message[0]
    for kb in range(tiles):
        if kb:
            total = total + message[kb]
        carry = jnp.broadcast_to(message[kb, 0:1, :], (wigner.shape[0], LANES))
        found = rest[:, tile(kb)] + reach[:, tile(kb)] * carry
        residual[:, tile(kb)] = found
        base[:, tile(kb)] = wigner[:, tile(kb)] + MIX_STEP * found
    gram[...] = total


def mixing_weights(entry):
    count = HIST + 1
    scale = sum(entry(i, i) for i in range(count)) / count
    factor = {}
    for i in range(count):
        for j in range(i + 1):
            value = entry(j, i)
            if i == j:
                value = value + RIDGE_SCALE * scale
            for k in range(j):
                value = value - factor[i, k] * factor[j, k]
            factor[i, j] = jnp.sqrt(value) if i == j else value / factor[j, j]
    forward = []
    for row in range(count):
        partial = jnp.ones_like(scale)
        for inner in range(row):
            partial = partial - factor[row, inner] * forward[inner]
        forward.append(partial / factor[row, row])
    backward = [None] * count
    for row in reversed(range(count)):
        partial = forward[row]
        for inner in range(row + 1, count):
            partial = partial - factor[inner, row] * backward[inner]
        backward[row] = partial / factor[row, row]
    total = sum(backward)
    return [z / total for z in backward]


def mix_kernel(gram_0, gram_1, gram_2, gram_3, blends, base, mixed):
    cells, moments = base.shape
    gram = (gram_0[...] + gram_1[...]) + (gram_2[...] + gram_3[...])
    gram = jnp.broadcast_to(jnp.sum(gram, axis=1, keepdims=True), gram.shape)

    def entry(i, j):
        row = 1 + i if j == HIST else 6 + PAIRS.index((i, j))
        return gram[row : row + 1, :]

    weights = [jnp.broadcast_to(w, (cells, LANES)) for w in mixing_weights(entry)]
    for kb in range(moments // LANES):
        total = weights[HIST] * base[:, tile(kb)]
        for j in range(HIST):
            total = total + weights[j] * blends[j, :, tile(kb)]
        mixed[:, tile(kb)] = total


def body(wigner, past_iterates, past_residuals, velocity, out_rate, inflow, offsets, directions, coupling):
    _, cells, moments = wigner.shape
    bands = lax.axis_size(BAND)
    blocks = lax.axis_size(POS)
    where_at = lax.axis_index(POS).astype(jnp.int32).reshape(1)
    wigner = wigner.reshape(cells, moments)
    past_iterates = past_iterates.reshape(HIST, cells, moments)
    past_residuals = past_residuals.reshape(HIST, cells, moments)
    offsets = offsets.reshape(1, moments)
    size = 4 * cells * moments
    share = f32(bands, cells, moments // bands)

    spread = call(spread_kernel, share, [VMEM] * 2, 10 * size, 2 * size)(offsets, wigner)
    held = lax.all_to_all(spread, BAND, 0, 0, tiled=True)
    early_sums, blends, early_gram = call(
        early_kernel,
        (f32(blocks, ROWS, LANES), f32(HIST, cells, moments), f32(16, LANES)),
        [SMEM] + [VMEM] * 4,
        20 * size,
        13 * size,
    )(directions, velocity, out_rate, past_iterates, past_residuals)
    routed = call(route_kernel, share, [SMEM, VMEM], size, 2 * size)(coupling, held)
    partner = lax.all_to_all(routed, BAND, 0, 0, tiled=True)
    reach, rest, sums, gram = call(
        local_kernel,
        (f32(cells, moments), f32(cells, moments), f32(blocks, ROWS, LANES), f32(16, LANES)),
        [SMEM] + [VMEM] * 8,
        20 * size,
        12 * size,
    )(directions, spread, partner, velocity, out_rate, wigner, past_residuals, early_sums, early_gram)
    sums = lax.all_to_all(sums, POS, 0, 0, tiled=True)
    message = call(carry_kernel, f32(blocks, 16, LANES), [SMEM] * 2 + [VMEM] * 3, size, 2 * size)(
        directions, where_at, inflow, sums, gram
    )
    message = lax.all_to_all(message, POS, 0, 0, tiled=True)
    residual, base, gram = call(
        finish_kernel, (f32(cells, moments), f32(cells, moments), f32(16, LANES)), [VMEM] * 4, size, 6 * size
    )(message, reach, rest, wigner)
    gram = gram + lax.ppermute(gram, BAND[1], [(0, 1), (1, 0)])
    chips = lax.axis_size(BAND[0])
    others = [lax.ppermute(gram, BAND[0], [(i, (i + d) % chips) for i in range(chips)]) for d in range(1, chips)]
    mixed = call(mix_kernel, f32(cells, moments), [VMEM] * 6, 3 * size, 6 * size)(gram, *others, blends, base)
    return mixed[None], residual[None]


def solution(mesh):
    finer = Mesh(mesh.devices.reshape(4, 2, 4, 8), ("band_0", "band_1", "pos_0", "pos_1"))
    in_specs = (
        P(BAND, POS, None),
        P(None, BAND, POS, None),
        P(None, BAND, POS, None),
        P(POS, None),
        P(BAND, None),
        P(BAND, None),
        P(),
        P(),
        P(),
    )
    out_specs = (P(BAND, POS, None), P(BAND, POS, None))
    return jax.shard_map(body, mesh=finer, in_specs=in_specs, out_specs=out_specs, check_vma=False)
```

profile of v0, /device:TPU:1, one launch (start us, length us, event | category | flops | bytes accessed | tf_op | source)
XLA Modules:
  0.0 78.9 jit_solution(10663392591868763449)
XLA Ops:
  0.6 0.0 copy-start.1
  0.6 0.9 %copy-done.1 = f32[1,16,4096]{2,1,0:T(8,128)S(1)} copy-done((f32[1,16,4096]{2,1,0:T(8,128)S(1)}, f32[1,16,4096]{2,1,0:T(8,128)}, u32[]{:S(2)}) %copy-start.1) | copy-done | bytes 262168
  1.6 0.0 copy-start.9
  1.6 0.7 copy-done.9
  2.3 0.0 copy-start
  2.3 0.6 shard_map.104.spread
  2.9 0.0 copy-start.18
  3.0 12.1 %all_to_all.20.held = f32[8,16,512]{2,1,0:T(8,128)S(1)} all-to-all(f32[8,16,512]{2,1,0:T(8,128)S(1)} %shard_map.104.spread), channel_id=1, replica_groups=mesh['band_0'=4,'band_1'=2,'pos_0'=4,'pos_1'=8] {'band_0','band_1'}, dimensions={0} | all-to-all | bytes 524288 | tf_op jit(solution)/shard_map/all_to_all | solution.py:273
  15.1 0.0 copy-done.18
  15.1 1.3 %shard_map.105 = f32[8,16,512]{2,1,0:T(8,128)} custom-call(s32[8]{0:T(128)S(1)} %copy-done.18, f32[8,16,512]{2,1,0:T(8,128)S(1)} %all_to_all.20.held), custom_call_target="tpu_custom_call" | custom-call | flops 262144 | bytes 524288 | tf_op jit(solution)/shard_map/pallas_call | solution.py:281
  16.4 4.5 %all-to-all-start.1 = ((f32[8,16,512]{2,1,0:T(8,128)}), f32[8,16,512]{2,1,0:T(8,128)S(1)}, u32[]{:S(2)}, u32[]{:S(2)}) async-start(f32[8,16,512]{2,1,0:T(8,128)} %shard_map.105), calls=%async_computation.1 | async-start | bytes 524288 | tf_op jit(solution)/shard_map/all_to_all | solution.py:282
  20.9 0.0 copy-done
  20.9 0.0 copy-done.4
  20.9 0.0 copy-done.8
  20.9 0.6 copy-done.15
  21.5 1.2 %copy-done.3 = f32[4,1,16,4096]{3,2,1,0:T(8,128)S(1)} copy-done((f32[4,1,16,4096]{3,2,1,0:T(8,128)S(1)}, f32[4,1,16,4096]{3,2,1,0:T(8,128)}, u32[]{:S(2)}) %copy-start.3) | copy-done | bytes 1048600
  22.7 1.3 %shard_map.106 = (f32[32,8,128]{2,1,0:T(8,128)S(1)}, f32[4,16,4096]{2,1,0:T(8,128)S(1)}, f32[16,128]{1,0:T(8,128)S(1)}) custom-call(s32[32]{0:T(128)S(1)} %copy-done.15, f32[16,4096]{1,0:T(8,128)S(1)} %copy-done.4, f32[1,4096]{1,0:T(1,128)S(1)} %copy-done.8, f32[4,16,4096]{2,1,0:T(8,128)S(1)} %bitcast.12, f32[4,16,4096]{2,1,0:T(8,128)S(1)} %bitcast.7), custom_call_target="tpu_custom_call" | custom-call | flops 5242880 | bytes 3407872 | tf_op jit(solution)/shard_map/pallas_call | solution.py:274
  24.0 0.0 copy-start.11
  24.0 0.6 copy-done.11
  24.6 2.8 %all-to-all-done.1.partner = f32[8,16,512]{2,1,0:T(8,128)S(1)} async-done(((f32[8,16,512]{2,1,0:T(8,128)}), f32[8,16,512]{2,1,0:T(8,128)S(1)}, u32[]{:S(2)}, u32[]{:S(2)}) %all-to-all-start.1) | async-done | bytes 262176 | tf_op jit(solution)/shard_map/all_to_all | solution.py:282
  27.4 0.0 copy-done.2
  27.4 0.7 copy-done.16
  28.0 0.7 copy-done.12
  28.7 1.1 %shard_map.107 = (f32[16,4096]{1,0:T(8,128)S(1)}, f32[16,4096]{1,0:T(8,128)S(1)}, f32[32,8,128]{2,1,0:T(8,128)S(1)}, f32[16,128]{1,0:T(8,128)S(1)}) custom-call(s32[32]{0:T(128)S(1)} %copy-done.16, f32[8,16,512]{2,1,0:T(8,128)S(1)} %shard_map.104.spread, f32[8,16,512]{2,1,0:T(8,128)S(1)} %all-to-all-done.1.partner, f32[16,4096]{1,0:T(8,128)S(1)} %copy-done.4, ...), custom_call_target="tpu_custom_call" | custom-call | flops 5242880 | bytes 3145728 | tf_op jit(solution)/shard_map/pallas_call | solution.py:283
  29.8 0.0 copy-start.5
  29.9 0.7 copy-done.5
  30.6 0.7 copy-done.7
  31.2 0.6 copy-done.13
  31.8 11.3 %all-to-all-start.2 = ((f32[32,8,128]{2,1,0:T(8,128)}), f32[32,8,128]{2,1,0:T(8,128)S(1)}, u32[]{:S(2)}, u32[]{:S(2)}) async-start(f32[32,8,128]{2,1,0:T(8,128)} %copy-done.7), calls=%async_computation.2 | async-start | bytes 262144 | tf_op jit(solution)/shard_map/all_to_all | solution.py:290
  43.1 0.0 copy-start.10
  43.1 9.1 %all-to-all-done.2.sums = f32[32,8,128]{2,1,0:T(8,128)S(1)} async-done(((f32[32,8,128]{2,1,0:T(8,128)}), f32[32,8,128]{2,1,0:T(8,128)S(1)}, u32[]{:S(2)}, u32[]{:S(2)}) %all-to-all-start.2) | async-done | bytes 131104 | tf_op jit(solution)/shard_map/all_to_all | solution.py:290
  52.3 0.0 copy-done.14
  52.3 0.0 copy-done.10
  52.3 0.6 copy-done.17
  52.9 0.6 shard_map.108
  53.6 0.0 copy-start.6
  53.6 13.3 %all_to_all.21.message = f32[32,16,128]{2,1,0:T(8,128)S(1)} all-to-all(f32[32,16,128]{2,1,0:T(8,128)S(1)} %shard_map.108), channel_id=1, replica_groups=mesh['band_0'=4,'band_1'=2,'pos_0'=4,'pos_1'=8] {'pos_0','pos_1'}, dimensions={0} | all-to-all | bytes 524288 | tf_op jit(solution)/shard_map/all_to_all | solution.py:294
  66.9 0.0 copy-done.6
  66.9 0.8 shard_map.109
  67.7 4.5 %collective-permute-start = (f32[16,128]{1,0:T(8,128)S(1)}, f32[16,128]{1,0:T(8,128)S(1)}, u32[]{:S(2)}, u32[]{:S(2)}) collective-permute-start(f32[16,128]{1,0:T(8,128)S(1)} %get-tuple-element.18), channel_id=1, source_target_pairs={{0,32},{32,0},{1,33},{33,1},{2,34},{34,2},{3,35},{35,3},{4,36},{36... | collective-permute-start | bytes 24584 | tf_op jit(solution)/shard_map/ppermute | solution.py:298
  72.2 0.8 %collective-permute-done = f32[16,128]{1,0:T(8,128)S(1)} collective-permute-done((f32[16,128]{1,0:T(8,128)S(1)}, f32[16,128]{1,0:T(8,128)S(1)}, u32[]{:S(2)}, u32[]{:S(2)}) %collective-permute-start) | collective-permute-done | bytes 8224 | tf_op jit(solution)/shard_map/ppermute | solution.py:298
  73.0 0.3 collective-permute-start.1
  73.3 1.8 %collective-permute-start.2 = (f32[16,128]{1,0:T(8,128)S(1)}, f32[16,128]{1,0:T(8,128)S(1)}, u32[]{:S(2)}, u32[]{:S(2)}) collective-permute-start(f32[16,128]{1,0:T(8,128)S(1)} %add.7.gram_0), channel_id=1, source_target_pairs={{0,128},{64,192},{128,0},{192,64},{1,129},{65,193},{129,1},{193,65... | collective-permute-start | bytes 24584 | tf_op jit(solution)/shard_map/ppermute | solution.py:300
  75.1 0.6 collective-permute-start.3
  75.7 1.0 %collective-permute-done.1.gram_1 = f32[16,128]{1,0:T(8,128)S(1)} collective-permute-done((f32[16,128]{1,0:T(8,128)S(1)}, f32[16,128]{1,0:T(8,128)S(1)}, u32[]{:S(2)}, u32[]{:S(2)}) %collective-permute-start.1) | collective-permute-done | bytes 8224 | tf_op jit(solution)/shard_map/ppermute | solution.py:300
  76.7 0.6 collective-permute-done.2.gram_2
  77.3 0.6 collective-permute-done.3.gram_3
  77.9 1.0 %shard_map.110 = f32[16,4096]{1,0:T(8,128)} custom-call(f32[16,128]{1,0:T(8,128)S(1)} %add.7.gram_0, f32[16,128]{1,0:T(8,128)S(1)} %collective-permute-done.1.gram_1, f32[16,128]{1,0:T(8,128)S(1)} %collective-permute-done.2.gram_2, f32[16,128]{1,0:T(8,128)S(1)} %collective-permute-done.3.gram_3, f32[4,16,4096]{2,1,0:T(8,128)S(1)} %get-tuple-element.19.blends, ...), custom_call_target="tpu_custom_call" | custom-call | flops 786432 | bytes 1572864 | tf_op jit(solution)/shard_map/pallas_call | solution.py:301
  (12 shorter events, 0.0 us)
Async XLA Ops:
  0.6 1.0 %copy-start.1 = (f32[1,16,4096]{2,1,0:T(8,128)S(1)}, f32[1,16,4096]{2,1,0:T(8,128)}, u32[]{:S(2)}) copy-start(f32[1,16,4096]{2,1,0:T(8,128)} %param.9) | copy-start | bytes 786436
  1.6 0.7 copy-start.9
  2.3 18.6 %copy-start = (f32[4,1,16,4096]{3,2,1,0:T(8,128)S(1)}, f32[4,1,16,4096]{3,2,1,0:T(8,128)}, u32[]{:S(2)}) copy-start(f32[4,1,16,4096]{3,2,1,0:T(8,128)} %param.11) | copy-start | bytes 3145732
  2.9 12.2 %copy-start.18 = (s32[8]{0:T(128)S(1)}, s32[8]{0:T(128)}, u32[]{:S(2)}) copy-start(s32[8]{0:T(128)} %coupling.1) | copy-start | bytes 100
  16.4 4.5 %copy-start.4 = (f32[16,4096]{1,0:T(8,128)S(1)}, f32[16,4096]{1,0:T(8,128)}, u32[]{:S(2)}) copy-start(f32[16,4096]{1,0:T(8,128)} %velocity.3) | copy-start | bytes 786436
  16.4 4.5 %copy-start.8 = (f32[1,4096]{1,0:T(1,128)S(1)}, f32[1,4096]{1,0:T(1,128)}, u32[]{:S(2)}) copy-start(f32[1,4096]{1,0:T(1,128)} %out_rate.3) | copy-start | bytes 49156
  16.4 11.0 %all-to-all-start.1 = ((f32[8,16,512]{2,1,0:T(8,128)}), f32[8,16,512]{2,1,0:T(8,128)S(1)}, u32[]{:S(2)}, u32[]{:S(2)}) async-start(f32[8,16,512]{2,1,0:T(8,128)} %shard_map.105), calls=%async_computation.1 | async-start | bytes 524288 | tf_op jit(solution)/shard_map/all_to_all | solution.py:282
  20.9 0.7 copy-start.15
  21.5 1.2 %copy-start.3 = (f32[4,1,16,4096]{3,2,1,0:T(8,128)S(1)}, f32[4,1,16,4096]{3,2,1,0:T(8,128)}, u32[]{:S(2)}) copy-start(f32[4,1,16,4096]{3,2,1,0:T(8,128)} %param.10) | copy-start | bytes 3145732
  22.7 4.6 %copy-start.2 = (f32[1,16,4096]{2,1,0:T(8,128)S(1)}, f32[1,16,4096]{2,1,0:T(8,128)}, u32[]{:S(2)}) copy-start(f32[1,16,4096]{2,1,0:T(8,128)} %param.9) | copy-start | bytes 786436
  24.0 0.6 copy-start.11
  27.4 0.7 copy-start.16
  28.0 0.7 copy-start.12
  29.8 0.7 copy-start.5
  30.6 0.7 copy-start.7
  31.2 0.6 copy-start.13
  31.8 20.5 %copy-start.14 = (f32[16,128]{1,0:T(8,128)S(1)}, f32[16,128]{1,0:T(8,128)}, u32[]{:S(2)}) copy-start(f32[16,128]{1,0:T(8,128)} %copy-done.13) | copy-start | bytes 24580
  31.8 20.5 %all-to-all-start.2 = ((f32[32,8,128]{2,1,0:T(8,128)}), f32[32,8,128]{2,1,0:T(8,128)S(1)}, u32[]{:S(2)}, u32[]{:S(2)}) async-start(f32[32,8,128]{2,1,0:T(8,128)} %copy-done.7), calls=%async_computation.2 | async-start | bytes 262144 | tf_op jit(solution)/shard_map/all_to_all | solution.py:290
  43.1 9.2 %copy-start.10 = (f32[1,4096]{1,0:T(1,128)S(1)}, f32[1,4096]{1,0:T(1,128)}, u32[]{:S(2)}) copy-start(f32[1,4096]{1,0:T(1,128)} %inflow.1) | copy-start | bytes 49156
  52.3 0.7 copy-start.17
  53.6 13.4 %copy-start.6 = (f32[16,4096]{1,0:T(8,128)S(1)}, f32[16,4096]{1,0:T(8,128)}, u32[]{:S(2)}) copy-start(f32[16,4096]{1,0:T(8,128)} %copy-done.5) | copy-start | bytes 786436
  67.7 5.3 %collective-permute-start = (f32[16,128]{1,0:T(8,128)S(1)}, f32[16,128]{1,0:T(8,128)S(1)}, u32[]{:S(2)}, u32[]{:S(2)}) collective-permute-start(f32[16,128]{1,0:T(8,128)S(1)} %get-tuple-element.18), channel_id=1, source_target_pairs={{0,32},{32,0},{1,33},{33,1},{2,34},{34,2},{3,35},{35,3},{4,36},{36... | collective-permute-start | bytes 24584 | tf_op jit(solution)/shard_map/ppermute | solution.py:298
  73.0 3.7 %collective-permute-start.1 = (f32[16,128]{1,0:T(8,128)S(1)}, f32[16,128]{1,0:T(8,128)S(1)}, u32[]{:S(2)}, u32[]{:S(2)}) collective-permute-start(f32[16,128]{1,0:T(8,128)S(1)} %add.7.gram_0), channel_id=1, source_target_pairs={{0,64},{64,128},{128,192},{192,0},{1,65},{65,129},{129,193},{193,1... | collective-permute-start | bytes 24584 | tf_op jit(solution)/shard_map/ppermute | solution.py:300
  73.3 4.0 %collective-permute-start.2 = (f32[16,128]{1,0:T(8,128)S(1)}, f32[16,128]{1,0:T(8,128)S(1)}, u32[]{:S(2)}, u32[]{:S(2)}) collective-permute-start(f32[16,128]{1,0:T(8,128)S(1)} %add.7.gram_0), channel_id=1, source_target_pairs={{0,128},{64,192},{128,0},{192,64},{1,129},{65,193},{129,1},{193,65... | collective-permute-start | bytes 24584 | tf_op jit(solution)/shard_map/ppermute | solution.py:300
  75.1 2.8 %collective-permute-start.3 = (f32[16,128]{1,0:T(8,128)S(1)}, f32[16,128]{1,0:T(8,128)S(1)}, u32[]{:S(2)}, u32[]{:S(2)}) collective-permute-start(f32[16,128]{1,0:T(8,128)S(1)} %add.7.gram_0), channel_id=1, source_target_pairs={{0,192},{64,0},{128,64},{192,128},{1,193},{65,1},{129,65},{193,129... | collective-permute-start | bytes 24584 | tf_op jit(solution)/shard_map/ppermute | solution.py:300
where the time goes:
time: 79.7 us; the launch traced here: 78.9 us
  blocking collectives  25.5 us (32%)
  starting transfers between devices  23 us (29%)
  waiting for transfers between devices  14.9 us (19%)
  local copies, waits for them, and re-layouts  8.1 us (10%)
  Pallas kernels  6.67 us (8%)
    all_to_all x1, blocking collectives, body(): message = lax.all_to_all(message, POS, 0, 0, tiled=True)  13.3 us
    all_to_all x1, blocking collectives, body(): held = lax.all_to_all(spread, BAND, 0, 0, tiled=True)  12.1 us
    all_to_all x1, starting transfers between devices, body(): sums = lax.all_to_all(sums, POS, 0, 0, tiled=True)  11.3 us
    all_to_all x1, waiting for transfers between devices, body(): sums = lax.all_to_all(sums, POS, 0, 0, tiled=True)  9.15 us
    unnamed x38, local copies, waits for them, and re-layouts  8.1 us
    ppermute x1, starting transfers between devices, body(): gram = gram + lax.ppermute(gram, BAND[1], [(0, 1), (1, 0)])  4.5 us
    all_to_all x1, starting transfers between devices, body(): partner = lax.all_to_all(routed, BAND, 0, 0, tiled=True)  4.49 us
    all_to_all x1, waiting for transfers between devices, body(): partner = lax.all_to_all(routed, BAND, 0, 0, tiled=True)  2.78 us
  transfers between devices with their start and end apart: 6, of which 6 were waited for; matrix products, arithmetic and copies ran while one was open for 0% of the time, Pallas kernels for 2%

commit v1 on v0

v1 whole, which is shorter than its diff:
```python
import functools

import jax
import jax.numpy as jnp
from jax import lax
from jax.experimental import pallas as pl
from jax.experimental.pallas import tpu as pltpu
from jax.sharding import Mesh
from jax.sharding import PartitionSpec as P

POS = ("pos_0", "pos_1")
BAND = ("band_0", "band_1")
ALL = BAND + POS

MIX_STEP = 0.5
RIDGE_SCALE = 0.0001
LANES = 128
GROUP = 16
ROWS = 8
HIST = 4
PAIRS = [(i, j) for i in range(HIST) for j in range(i, HIST)]

VMEM = pl.BlockSpec(memory_space=pltpu.VMEM)
SMEM = pl.BlockSpec(memory_space=pltpu.SMEM)
HBM = pl.BlockSpec(memory_space=pltpu.HBM)


def call(kernel, outs, in_specs, flops, nbytes, scratch=(), mib=24):
    return pl.pallas_call(
        kernel,
        out_shape=outs,
        in_specs=in_specs,
        out_specs=jax.tree.map(lambda _: VMEM, outs),
        scratch_shapes=list(scratch),
        compiler_params=pltpu.CompilerParams(vmem_limit_bytes=mib * 2**20),
        cost_estimate=pl.CostEstimate(flops=flops, bytes_accessed=nbytes, transcendentals=0),
    )


def f32(*shape):
    return jax.ShapeDtypeStruct(shape, jnp.float32)


def tile(kb):
    return slice(kb * LANES, (kb + 1) * LANES)


def pick(x, index, axis):
    return jnp.take_along_axis(x, index, axis=axis, mode="promise_in_bounds")


def iota(axis):
    return lax.broadcasted_iota(jnp.int32, (ROWS, LANES), axis)


def scan_tile(back, a, b):
    row = iota(0)
    away = jnp.where(back, ROWS - 1 - row, row)
    a = [jnp.where(back, a[1], a[0]), jnp.where(back, a[0], a[1])]
    if b is not None:
        b = [jnp.where(back, b[1], b[0]), jnp.where(back, b[0], b[1])]
    for d in (1, 2, 4):
        source = jnp.where(back, row + d, row - d) & (ROWS - 1)
        keep = away >= d
        for h in range(2):
            if b is not None:
                b[h] = a[h] * jnp.where(keep, pick(b[h], source, 0), 0.0) + b[h]
            a[h] = a[h] * jnp.where(keep, pick(a[h], source, 0), 1.0)
    last = jnp.where(back, 0, ROWS - 1) + jnp.zeros_like(row)
    if b is not None:
        b[1] = a[1] * pick(b[0], last, 0) + b[1]
    a[1] = a[1] * pick(a[0], last, 0)
    ends = [pick(a[1], last, 0)]
    if b is not None:
        ends.append(pick(b[1], last, 0))
        b = [jnp.where(back, b[1], b[0]), jnp.where(back, b[0], b[1])]
    a = [jnp.where(back, a[1], a[0]), jnp.where(back, a[0], a[1])]
    return a, b, ends


def coefficients(velocity, out_rate, kb, h):
    v = velocity[h * ROWS : (h + 1) * ROWS, tile(kb)]
    r = jnp.broadcast_to(out_rate[:, tile(kb)], (ROWS, LANES))
    return v, r, 1.0 / (v + r)


def flag(directions, index):
    return jnp.full((ROWS, LANES), directions[index], jnp.int32) == 1


def down(x):
    return jnp.sum(x, axis=0, keepdims=True)


def half(h):
    return slice(h * ROWS, (h + 1) * ROWS)


def open_kernel(directions, *refs):
    sources, message, held, arrived = refs[:6], refs[6], refs[7:13], refs[13]
    copies = [pltpu.make_async_copy(a, b, arrived.at[n]) for n, (a, b) in enumerate(zip(sources, held))]
    for copy in copies:
        copy.start()
    offsets, wigner, velocity, out_rate, inflow, past_residuals = held
    tiles = wigner.shape[1] // LANES
    per = message.shape[2] // LANES
    lane = iota(1)
    zero = jnp.zeros((ROWS, LANES), jnp.float32)
    copies[0].wait()
    copies[1].wait()
    for kb in range(tiles):
        off = jnp.broadcast_to(offsets[:, tile(kb)], (ROWS, LANES))
        up, below_at = lane + off, lane - off
        up_in, down_in = up & (LANES - 1), below_at & (LANES - 1)
        for h in range(2):
            here = wigner[half(h), tile(kb)]
            nxt = pick(wigner[half(h), tile(kb + 1)], up_in, 1) if kb + 1 < tiles else zero
            prv = pick(wigner[half(h), tile(kb - 1)], down_in, 1) if kb else zero
            above = jnp.where(up < LANES, pick(here, up_in, 1), nxt)
            below = jnp.where(below_at >= 0, pick(here, down_in, 1), prv)
            message[kb // per, half(h), tile(kb % per)] = 0.5 * (above + below)
    for copy in copies[2:]:
        copy.wait()
    for kb in range(tiles):
        back = flag(directions, kb)
        slope = []
        for h in range(2):
            v, _, inv = coefficients(velocity, out_rate, kb, h)
            slope.append(v * inv)
        reach, _, _ = scan_tile(back, slope, None)

        def put(row, value):
            message[kb // per, 2 * ROWS + row : 2 * ROWS + row + 1, tile(kb % per)] = value

        for j in range(HIST):
            put(j, down(sum(past_residuals[j, half(h), tile(kb)] * reach[h] for h in range(2))))
        put(4, down(sum(reach[h] * reach[h] for h in range(2))))
        put(5, down(sum(reach[h] * wigner[half(h), tile(kb)] for h in range(2))))
        put(6, out_rate[:, tile(kb)])
        put(7, inflow[:, tile(kb)])


def history_kernel(past_iterates, past_residuals, blends, gram):
    tiles = past_residuals.shape[2] // LANES
    acc = [jnp.zeros((ROWS, LANES), jnp.float32) for _ in PAIRS]
    for kb in range(tiles):
        for h in range(2):
            past = [past_residuals[j, half(h), tile(kb)] for j in range(HIST)]
            for j in range(HIST):
                blends[j, half(h), tile(kb)] = past_iterates[j, half(h), tile(kb)] + MIX_STEP * past[j]
            for n, (i, j) in enumerate(PAIRS):
                acc[n] = acc[n] + past[i] * past[j]
    gram[...] = jnp.zeros(gram.shape, jnp.float32)
    for n in range(len(PAIRS)):
        gram[6 + n : 7 + n, :] = down(acc[n])


def at_contact(ids, blocks, back, slope, inflow):
    row = iota(0)
    place = jnp.full((ROWS, LANES), ids[1], jnp.int32)
    first = (place == 0) & (row == 0) & jnp.logical_not(back)
    final = (place == blocks - 1) & (row == ROWS - 1) & back
    wide = jnp.broadcast_to(inflow, (ROWS, LANES))
    return [jnp.where(first, slope[0] * wide, 0.0), jnp.where(final, slope[1] * wide, 0.0)]


def fold_kernel(directions, coupling, ids, held, velocity, message, *shares):
    bands = held.shape[0]
    blocks = message.shape[0]
    per = held.shape[2] // LANES
    row, lane = iota(0), iota(1)
    for d in range(bands):
        s = ids[0] ^ d
        shares[d][...] = held[s, 0 : 2 * ROWS, :] + held[coupling[s], 0 : 2 * ROWS, :]
    for kt in range(per):
        kb = ids[0] * per + kt
        back = flag(directions, kb)
        columns = pl.ds(pl.multiple_of(kb * LANES, LANES), LANES)
        parts = []
        for s in range(bands):
            tail = held[s, 2 * ROWS :, tile(kt)]
            rate = jnp.broadcast_to(tail[6:7], (ROWS, LANES))
            slope, offset = [], []
            for h in range(2):
                v = velocity[half(h), columns]
                inv = 1.0 / (v + rate)
                both = held[s, half(h), tile(kt)] + held[coupling[s], half(h), tile(kt)]
                slope.append(v * inv)
                offset.append(rate * 0.5 * both * inv)
            edge = at_contact(ids, blocks, back, slope, tail[7:8])
            offset = [offset[h] + edge[h] for h in range(2)]
            reach, run, ends = scan_tile(back, slope, offset)
            crossed = jnp.broadcast_to(down(reach[0] * run[0] + reach[1] * run[1]), (ROWS, LANES)) - tail
            parts.append(
                jnp.where(row == 5, crossed, jnp.where(row == 6, ends[0], jnp.where(row == 7, ends[1], tail)))
            )
        for bit in range(3):
            step = 1 << bit
            high = ((lane >> (4 + bit)) & 1) == 1
            swapped = list(parts)
            for s in range(bands):
                if not s & step:
                    swapped[s] = jnp.where(high, pltpu.roll(parts[s + step], GROUP * step, 1), parts[s])
                    swapped[s + step] = jnp.where(high, parts[s + step], pltpu.roll(parts[s], LANES - GROUP * step, 1))
            parts = swapped
        for g in range(bands):
            message[kt * bands + g] = parts[g]


def settle_kernel(directions, ids, *refs):
    shares = refs[:8]
    velocity, out_rate, inflow, wigner, past_residuals, early, marks, reach_out, rest, gram = refs[8:]
    per = shares[0].shape[1] // LANES
    blocks = velocity.shape[1] // LANES
    acc = [jnp.zeros((ROWS, LANES), jnp.float32) for _ in range(HIST + 1)]
    for d in range(len(shares)):
        for kt in range(per):
            kb = (ids[0] ^ d) * per + kt
            back = flag(directions, kb)
            columns = pl.ds(pl.multiple_of(kb * LANES, LANES), LANES)
            rate = jnp.broadcast_to(out_rate[:, columns], (ROWS, LANES))
            slope, offset = [], []
            for h in range(2):
                v = velocity[half(h), columns]
                inv = 1.0 / (v + rate)
                slope.append(v * inv)
                offset.append(rate * 0.5 * shares[d][half(h), tile(kt)] * inv)
            edge = at_contact(ids, blocks, back, slope, inflow[:, columns])
            offset = [offset[h] + edge[h] for h in range(2)]
            reach, run, _ = scan_tile(back, slope, offset)
            for h in range(2):
                left = run[h] - wigner[half(h), columns]
                rest[half(h), columns] = left
                reach_out[half(h), columns] = reach[h]
                for j in range(HIST):
                    acc[j] = acc[j] + past_residuals[j, half(h), columns] * left
                acc[HIST] = acc[HIST] + left * left
    gram[...] = early[...]
    for n in range(HIST + 1):
        gram[n : n + 1, :] = down(acc[n])
    marks[...] = jnp.full((ROWS, LANES), directions[ids[0] * per + ids[1] // ROWS], jnp.int32)


def carry_kernel(marks, sums, gram, message, forth, counter):
    blocks = sums.shape[0]
    row, lane = iota(0), iota(1)
    back = marks[...] == 1
    acc = jnp.zeros((ROWS, LANES), jnp.float32)
    carry = jnp.zeros((1, LANES), jnp.float32)
    for step in range(blocks):
        part = jnp.where(back, sums[blocks - 1 - step], sums[step])
        wide = jnp.broadcast_to(carry, (ROWS, LANES))
        forth[step : step + 1, :] = carry
        counter[blocks - 1 - step : blocks - step, :] = carry
        acc = acc + part * jnp.where(row == 4, wide * wide, jnp.where(row == 5, 2.0 * wide, wide))
        carry = part[6:7] * carry + part[7:8]
    terms = [gram[half(0), :] + jnp.where(row < 6, acc, 0.0), gram[half(1), :]]
    line = jnp.zeros((ROWS, LANES), jnp.float32)
    for h in range(2):
        whole = jnp.broadcast_to(jnp.sum(terms[h], axis=1, keepdims=True), (ROWS, LANES))
        line = line + jnp.where(lane == GROUP + h * ROWS + row, whole, 0.0)
    line = jnp.broadcast_to(down(line), (ROWS, LANES))
    for q in range(blocks // ROWS):
        carries = jnp.where(back, counter[half(q), :], forth[half(q), :])
        for s in range(LANES // GROUP):
            turned = pltpu.roll(carries, LANES - GROUP * s, 1) if s else carries
            message[s * blocks + q * ROWS : s * blocks + (q + 1) * ROWS, :] = jnp.where(lane < GROUP, turned, line)


def mixing_weights(entry):
    count = HIST + 1
    scale = sum(entry(i, i) for i in range(count)) / count
    factor = {}
    for i in range(count):
        for j in range(i + 1):
            value = entry(j, i)
            if i == j:
                value = value + RIDGE_SCALE * scale
            for k in range(j):
                value = value - factor[i, k] * factor[j, k]
            factor[i, j] = jnp.sqrt(value) if i == j else value / factor[j, j]
    forward = []
    for row in range(count):
        partial = jnp.ones_like(scale)
        for inner in range(row):
            partial = partial - factor[row, inner] * forward[inner]
        forward.append(partial / factor[row, row])
    backward = [None] * count
    for row in reversed(range(count)):
        partial = forward[row]
        for inner in range(row + 1, count):
            partial = partial - factor[inner, row] * backward[inner]
        backward[row] = partial / factor[row, row]
    total = sum(backward)
    return [z / total for z in backward]


def finish_kernel(message, reach, rest, wigner, blends, residual, mixed):
    tiles = wigner.shape[1] // LANES
    row, lane = iota(0), iota(1)
    total = message[half(0), :]
    for kb in range(1, tiles):
        total = total + message[half(kb), :]
    total = jnp.broadcast_to(down(total), (ROWS, LANES))

    def term(n):
        return pick(total, jnp.full((ROWS, LANES), GROUP + n, jnp.int32), 1)

    def entry(i, j):
        if j == HIST:
            return term(4) + term(5) if i == HIST else term(i)
        return term(6 + PAIRS.index((i, j)))

    weights = mixing_weights(entry)
    for kb in range(tiles):
        spots = pick(message[half(kb), :], lane & (GROUP - 1), 1)
        carry = jnp.broadcast_to(down(jnp.where((lane >> 4) == row, spots, 0.0)), (ROWS, LANES))
        for h in range(2):
            found = rest[half(h), tile(kb)] + reach[half(h), tile(kb)] * carry
            residual[half(h), tile(kb)] = found
            value = weights[HIST] * (wigner[half(h), tile(kb)] + MIX_STEP * found)
            for j in range(HIST):
                value = value + weights[j] * blends[j, half(h), tile(kb)]
            mixed[half(h), tile(kb)] = value


def body(wigner, past_iterates, past_residuals, velocity, out_rate, inflow, offsets, directions, coupling):
    _, cells, moments = wigner.shape
    bands = lax.axis_size(BAND)
    blocks = lax.axis_size(POS)
    ids = jnp.stack([lax.axis_index(BAND), lax.axis_index(POS)]).astype(jnp.int32)
    wigner = wigner.reshape(cells, moments)
    past_iterates = past_iterates.reshape(HIST, cells, moments)
    past_residuals = past_residuals.reshape(HIST, cells, moments)
    offsets = offsets.reshape(1, moments)
    size = 4 * cells * moments
    share = moments // bands

    sources = (offsets, wigner, velocity, out_rate, inflow, past_residuals)
    message = call(
        open_kernel,
        f32(bands, cells + ROWS, share),
        [SMEM] + [HBM] * 6,
        20 * size,
        8 * size,
        [pltpu.VMEM(x.shape, x.dtype) for x in sources] + [pltpu.SemaphoreType.DMA((6,))],
        mib=60,
    )(directions, *sources)
    held = lax.all_to_all(message, BAND, 0, 0, tiled=True)
    blends, early = call(
        history_kernel, (f32(HIST, cells, moments), f32(16, LANES)), [VMEM] * 2, 8 * size, 12 * size
    )(past_iterates, past_residuals)
    sums, *shares = call(
        fold_kernel,
        (f32(blocks, ROWS, LANES),) + (f32(cells, share),) * bands,
        [SMEM] * 3 + [VMEM] * 2,
        20 * size,
        5 * size,
    )(directions, coupling, ids, held, velocity)
    sums = lax.all_to_all(sums, POS, 0, 0, tiled=True)
    shares = [shares[0]] + [
        lax.ppermute(shares[d], BAND, [(i, i ^ d) for i in range(bands)]) for d in range(1, bands)
    ]
    marks, reach, rest, gram = call(
        settle_kernel,
        (jax.ShapeDtypeStruct((ROWS, LANES), jnp.int32), f32(cells, moments), f32(cells, moments), f32(16, LANES)),
        [SMEM] * 2 + [VMEM] * 14,
        20 * size,
        10 * size,
    )(directions, ids, *shares, velocity, out_rate, inflow, wigner, past_residuals, early)
    message = call(
        carry_kernel,
        f32(bands * blocks, LANES),
        [VMEM] * 3,
        size,
        size,
        [pltpu.VMEM((blocks, LANES), jnp.float32)] * 2,
    )(marks, sums, gram)
    message = lax.all_to_all(message, ALL, 0, 0, tiled=True)
    residual, mixed = call(
        finish_kernel, (f32(cells, moments), f32(cells, moments)), [VMEM] * 5, 8 * size, 10 * size
    )(message, reach, rest, wigner, blends)
    return mixed[None], residual[None]


def solution(mesh):
    finer = Mesh(mesh.devices.reshape(4, 2, 4, 8), ("band_0", "band_1", "pos_0", "pos_1"))
    in_specs = (
        P(BAND, POS, None),
        P(None, BAND, POS, None),
        P(None, BAND, POS, None),
        P(POS, None),
        P(BAND, None),
        P(BAND, None),
        P(),
        P(),
        P(),
    )
    out_specs = (P(BAND, POS, None), P(BAND, POS, None))
    return jax.shard_map(body, mesh=finer, in_specs=in_specs, out_specs=out_specs, check_vma=False)
```

time: 79.7 us -> 70.7 us (0.89)
  local copies, waits for them, and re-layouts: 8.1 us -> 1.02 us
  waiting for transfers between devices: 14.9 us -> 9.28 us
  starting transfers between devices: 23 us -> 26.3 us
  Pallas kernels: 6.67 us -> 8.19 us
  blocking collectives: 25.5 us -> 24.7 us
    all_to_all x1, waiting for transfers between devices: 9.15 us -> 0.01 us  [body(): sums = lax.all_to_all(sums, POS, 0, 0, tiled=True)]
    unnamed x38 -> x20, local copies, waits for them, and re-layouts: 8.1 us -> 1.02 us
    all_to_all x1, waiting for transfers between devices: 2.78 us -> 8.02 us  [body(): held = lax.all_to_all(message, BAND, 0, 0, tiled=True)]
    all_to_all x1, starting transfers between devices: 4.49 us -> 6.74 us  [body(): held = lax.all_to_all(message, BAND, 0, 0, tiled=True)]
    ppermute x4 -> x7, starting transfers between devices: 7.2 us -> 9.18 us  [body(): lax.ppermute(shares[d], BAND, [(i, i ^ d) for i in range(bands)])]
    ppermute x4 -> x7, waiting for transfers between devices: 2.99 us -> 1.26 us  [body(): lax.ppermute(shares[d], BAND, [(i, i ^ d) for i in range(bands)])]
    pallas_call x7 -> x6, Pallas kernels: 6.67 us -> 8.19 us  [the longest x1 3.7 us: body(): call(open_kernel, f32(bands, cells + ROWS, share), [SMEM] + [HBM] * 6, 20...]
    all_to_all x1, starting transfers between devices: 11.3 us -> 10.4 us  [body(): sums = lax.all_to_all(sums, POS, 0, 0, tiled=True)]
  transfers between devices with their start and end apart: 6 -> 9, of which waited for: 6 -> 3; matrix products, arithmetic and copies ran while one was open for 0% -> 0% of each run, Pallas kernels for 2% -> 2%
where the time goes in v1:
time: 70.7 us; the launch traced here: 70.3 us
  starting transfers between devices  26.3 us (37%)
  blocking collectives  24.7 us (35%)
  waiting for transfers between devices  9.28 us (13%)
  Pallas kernels  8.19 us (12%)
  local copies, waits for them, and re-layouts  1.02 us (1%)
  between operations  0.76 us (1%)
    all_to_all x1, blocking collectives, body(): message = lax.all_to_all(message, ALL, 0, 0, tiled=True)  24.7 us
    all_to_all x1, starting transfers between devices, body(): sums = lax.all_to_all(sums, POS, 0, 0, tiled=True)  10.4 us
    ppermute x7, starting transfers between devices, body(): lax.ppermute(shares[d], BAND, [(i, i ^ d) for i in range(bands)])  9.18 us
    all_to_all x1, waiting for transfers between devices, body(): held = lax.all_to_all(message, BAND, 0, 0, tiled=True)  8.02 us
    all_to_all x1, starting transfers between devices, body(): held = lax.all_to_all(message, BAND, 0, 0, tiled=True)  6.74 us
    pallas_call x1, Pallas kernels, body(): call(open_kernel, f32(bands, cells + ROWS, share), [SMEM] + [HBM] * 6, 20...  3.7 us
    pallas_call x1, Pallas kernels, body(): call(fold_kernel, (f32(blocks, ROWS, LANES),) + (f32(cells, share),) * ba...  1.83 us
  transfers between devices with their start and end apart: 9, of which 3 were waited for; matrix products, arithmetic and copies ran while one was open for 0% of the time, Pallas kernels for 2%

profile of v1, /device:TPU:1, one launch (start us, length us, event | category | flops | bytes accessed | tf_op | source)
XLA Modules:
  0.0 70.3 jit_solution(10244699327532701891)
XLA Ops:
  0.6 0.0 copy-start.2
  0.6 0.0 copy-start.8
  0.7 0.0 copy-start.9
  0.7 0.0 copy-start.3
  0.7 3.7 %shard_map.104 = f32[8,24,512]{2,1,0:T(8,128)} custom-call(s32[32]{0:T(128)} %directions.5, s32[1,4096]{1,0:T(1,128)} %bitcast.21, f32[16,4096]{1,0:T(8,128)} %bitcast.15, f32[16,4096]{1,0:T(8,128)} %refs_8_.1, f32[1,4096]{1,0:T(1,128)} %refs_9_.1, f32[1,4096]{1,0:T(1,128)} %refs_10_.1, f32[4,16,4096]{2,1,0:T(8,128)} %bitcast.12), custom_call_target="tpu_custom_call" | custom-call | flops 5242880 | bytes 2097152 | tf_op jit(solution)/shard_map/pallas_call | solution.py:340
  4.4 0.0 copy-start
  4.4 6.7 %all-to-all-start = ((f32[8,24,512]{2,1,0:T(8,128)}), f32[8,24,512]{2,1,0:T(8,128)S(1)}, u32[]{:S(2)}, u32[]{:S(2)}) async-start(f32[8,24,512]{2,1,0:T(8,128)} %shard_map.104), calls=%async_computation | async-start | bytes 786432 | tf_op jit(solution)/shard_map/all_to_all | solution.py:349
  11.1 0.1 pad_add_fusion.ids
  11.2 8.0 %all-to-all-done.held = f32[8,24,512]{2,1,0:T(8,128)S(1)} async-done(((f32[8,24,512]{2,1,0:T(8,128)}), f32[8,24,512]{2,1,0:T(8,128)S(1)}, u32[]{:S(2)}, u32[]{:S(2)}) %all-to-all-start) | async-done | bytes 393248 | tf_op jit(solution)/shard_map/all_to_all | solution.py:349
  19.2 0.0 copy-done.2
  19.2 0.0 copy-done.8
  19.2 0.0 copy-done.9
  19.2 1.8 %shard_map.105 = (f32[32,8,128]{2,1,0:T(8,128)}, f32[16,512]{1,0:T(8,128)S(1)}, f32[16,512]{1,0:T(8,128)S(1)}, f32[16,512]{1,0:T(8,128)S(1)}, f32[16,512]{1,0:T(...) custom-call(s32[32]{0:T(128)S(1)} %copy-done.8, ...), custom_call_target="tpu_custom_call" | custom-call | flops 5242880 | bytes 1310720 | tf_op jit(solution)/shard_map/pallas_call | solution.py:353
  21.1 10.4 %all-to-all-start.1 = ((f32[32,8,128]{2,1,0:T(8,128)}), f32[32,8,128]{2,1,0:T(8,128)S(1)}, u32[]{:S(2)}, u32[]{:S(2)}) async-start(f32[32,8,128]{2,1,0:T(8,128)} %get-tuple-element.29), calls=%async_computation.1 | async-start | bytes 262144 | tf_op jit(solution)/shard_map/all_to_all | solution.py:360
  31.5 1.2 %collective-permute-start = (f32[16,512]{1,0:T(8,128)S(1)}, f32[16,512]{1,0:T(8,128)S(1)}, u32[]{:S(2)}, u32[]{:S(2)}) collective-permute-start(f32[16,512]{1,0:T(8,128)S(1)} %get-tuple-element.20), channel_id=1, source_target_pairs={{0,32},{32,0},{64,96},{96,64},{128,160},{160,128},{192,224},{224,1... | collective-permute-start | bytes 98312 | tf_op jit(solution)/shard_map/ppermute | solution.py:362
  32.7 0.3 collective-permute-start.1
  33.0 1.4 %collective-permute-start.2 = (f32[16,512]{1,0:T(8,128)S(1)}, f32[16,512]{1,0:T(8,128)S(1)}, u32[]{:S(2)}, u32[]{:S(2)}) collective-permute-start(f32[16,512]{1,0:T(8,128)S(1)} %get-tuple-element.22), channel_id=1, source_target_pairs={{0,96},{32,64},{64,32},{96,0},{128,224},{160,192},{192,160},{224,1... | collective-permute-start | bytes 98312 | tf_op jit(solution)/shard_map/ppermute | solution.py:362
  34.4 0.4 collective-permute-start.3
  34.9 2.9 %collective-permute-start.4 = (f32[16,512]{1,0:T(8,128)S(1)}, f32[16,512]{1,0:T(8,128)S(1)}, u32[]{:S(2)}, u32[]{:S(2)}) collective-permute-start(f32[16,512]{1,0:T(8,128)S(1)} %get-tuple-element.24), channel_id=1, source_target_pairs={{0,160},{32,128},{64,224},{96,192},{128,32},{160,0},{192,96},{224,... | collective-permute-start | bytes 98312 | tf_op jit(solution)/shard_map/ppermute | solution.py:362
  37.7 0.0 collective-permute-done.refs_1_
  37.7 0.9 %collective-permute-start.5 = (f32[16,512]{1,0:T(8,128)S(1)}, f32[16,512]{1,0:T(8,128)S(1)}, u32[]{:S(2)}, u32[]{:S(2)}) collective-permute-start(f32[16,512]{1,0:T(8,128)S(1)} %get-tuple-element.25), channel_id=1, source_target_pairs={{0,192},{32,224},{64,128},{96,160},{128,64},{160,96},{192,0},{224,... | collective-permute-start | bytes 98312 | tf_op jit(solution)/shard_map/ppermute | solution.py:362
  38.6 0.0 collective-permute-done.1.refs_2_
  38.6 2.0 %collective-permute-start.6 = (f32[16,512]{1,0:T(8,128)S(1)}, f32[16,512]{1,0:T(8,128)S(1)}, u32[]{:S(2)}, u32[]{:S(2)}) collective-permute-start(f32[16,512]{1,0:T(8,128)S(1)} %get-tuple-element.26), channel_id=1, source_target_pairs={{0,224},{32,192},{64,160},{96,128},{128,96},{160,64},{192,32},{224... | collective-permute-start | bytes 98312 | tf_op jit(solution)/shard_map/ppermute | solution.py:362
  40.7 0.0 copy-done.3
  40.7 0.0 copy-done
  40.7 0.0 copy-start.1
  40.7 0.0 copy-start.6
  40.7 0.0 copy-start.7
  40.7 0.3 shard_map.106
  40.9 0.0 copy-start.4
  41.0 1.0 %copy-done.4 = f32[4,16,4096]{2,1,0:T(8,128)} copy-done((f32[4,16,4096]{2,1,0:T(8,128)}, f32[4,16,4096]{2,1,0:T(8,128)S(1)}, u32[]{:S(2)}) %copy-start.4) | copy-done | bytes 1048600
  41.9 0.0 collective-permute-done.2.refs_3_
  41.9 0.0 collective-permute-done.3.refs_4_
  41.9 0.0 collective-permute-done.4.refs_5_
  41.9 0.1 collective-permute-done.5.refs_6_
  42.0 1.2 %collective-permute-done.6.refs_7_ = f32[16,512]{1,0:T(8,128)S(1)} collective-permute-done((f32[16,512]{1,0:T(8,128)S(1)}, f32[16,512]{1,0:T(8,128)S(1)}, u32[]{:S(2)}, u32[]{:S(2)}) %collective-permute-start.6) | collective-permute-done | bytes 32800 | tf_op jit(solution)/shard_map/ppermute | solution.py:362
  43.2 0.0 copy-done.1
  43.2 0.0 copy-done.6
  43.2 0.0 copy-done.7
  43.2 0.0 copy-start.5
  43.2 1.2 %shard_map.107 = (s32[8,128]{1,0:T(8,128)S(1)}, f32[16,4096]{1,0:T(8,128)S(1)}, f32[16,4096]{1,0:T(8,128)S(1)}, f32[16,128]{1,0:T(8,128)S(1)}) custom-call(s32[32]{0:T(128)S(1)} %copy-done.8, s32[2]{0:T(128)S(1)} %pad_add_fusion.ids, f32[16,512]{1,0:T(8,128)S(1)} %get-tuple-element.19.refs_0_, f32[16,512]{1,0:T(8,128)S(1)} %collective-permute-done.refs_1_, ...), custom_call_target="tpu_custom_call" | custom-call | flops 5242880 | bytes 2621440 | tf_op jit(solution)/shard_map/pallas_call | solution.py:364
  44.4 0.0 all-to-all-done.1.sums
  44.4 0.2 shard_map.108
  44.6 24.7 %all_to_all.21 = f32[256,1,128]{2,1,0:T(1,128)S(1)} all-to-all(f32[256,1,128]{2,1,0:T(1,128)S(1)} %bitcast.19), channel_id=1, replica_groups=mesh['band_0'=4,'band_1'=2,'pos_0'=4,'pos_1'=8] {'band_0','band_1','pos_..., dimensions={0} | all-to-all | bytes 262144 | tf_op jit(solution)/shard_map/all_to_all | solution.py:379
  69.3 0.0 copy-done.5
  69.3 1.0 %shard_map.109 = (f32[16,4096]{1,0:T(8,128)}, f32[16,4096]{1,0:T(8,128)}) custom-call(f32[256,128]{1,0:T(8,128)S(1)} %bitcast.20, f32[16,4096]{1,0:T(8,128)S(1)} %get-tuple-element.31.reach, f32[16,4096]{1,0:T(8,128)S(1)} %get-tuple-element.32.rest, f32[16,4096]{1,0:T(8,128)S(1)} %bitcast.17, f32[4,16,4096]{2,1,0:T(8,128)S(1)} %copy-done.5), custom_call_target="tpu_custom_call" | custom-call | flops 2097152 | bytes 2621440 | tf_op jit(solution)/shard_map/pallas_call | solution.py:380
Async XLA Ops:
  0.6 18.6 %copy-start.2 = (f32[16,4096]{1,0:T(8,128)S(1)}, f32[16,4096]{1,0:T(8,128)}, u32[]{:S(2)}) copy-start(f32[16,4096]{1,0:T(8,128)} %refs_8_.1) | copy-start | bytes 786436
  0.6 18.6 %copy-start.8 = (s32[32]{0:T(128)S(1)}, s32[32]{0:T(128)}, u32[]{:S(2)}) copy-start(s32[32]{0:T(128)} %directions.5) | copy-start | bytes 388
  0.7 18.6 %copy-start.9 = (s32[8]{0:T(128)S(1)}, s32[8]{0:T(128)}, u32[]{:S(2)}) copy-start(s32[8]{0:T(128)} %coupling.1) | copy-start | bytes 100
  0.7 40.0 %copy-start.3 = (f32[4,1,16,4096]{3,2,1,0:T(8,128)S(1)}, f32[4,1,16,4096]{3,2,1,0:T(8,128)}, u32[]{:S(2)}) copy-start(f32[4,1,16,4096]{3,2,1,0:T(8,128)} %param.10) | copy-start | bytes 3145732
  4.4 36.3 %copy-start = (f32[4,1,16,4096]{3,2,1,0:T(8,128)S(1)}, f32[4,1,16,4096]{3,2,1,0:T(8,128)}, u32[]{:S(2)}) copy-start(f32[4,1,16,4096]{3,2,1,0:T(8,128)} %param.11) | copy-start | bytes 3145732
  4.4 14.8 %all-to-all-start = ((f32[8,24,512]{2,1,0:T(8,128)}), f32[8,24,512]{2,1,0:T(8,128)S(1)}, u32[]{:S(2)}, u32[]{:S(2)}) async-start(f32[8,24,512]{2,1,0:T(8,128)} %shard_map.104), calls=%async_computation | async-start | bytes 786432 | tf_op jit(solution)/shard_map/all_to_all | solution.py:349
  21.1 23.3 %all-to-all-start.1 = ((f32[32,8,128]{2,1,0:T(8,128)}), f32[32,8,128]{2,1,0:T(8,128)S(1)}, u32[]{:S(2)}, u32[]{:S(2)}) async-start(f32[32,8,128]{2,1,0:T(8,128)} %get-tuple-element.29), calls=%async_computation.1 | async-start | bytes 262144 | tf_op jit(solution)/shard_map/all_to_all | solution.py:360
  31.5 6.3 %collective-permute-start = (f32[16,512]{1,0:T(8,128)S(1)}, f32[16,512]{1,0:T(8,128)S(1)}, u32[]{:S(2)}, u32[]{:S(2)}) collective-permute-start(f32[16,512]{1,0:T(8,128)S(1)} %get-tuple-element.20), channel_id=1, source_target_pairs={{0,32},{32,0},{64,96},{96,64},{128,160},{160,128},{192,224},{224,1... | collective-permute-start | bytes 98312 | tf_op jit(solution)/shard_map/ppermute | solution.py:362
  32.7 5.9 %collective-permute-start.1 = (f32[16,512]{1,0:T(8,128)S(1)}, f32[16,512]{1,0:T(8,128)S(1)}, u32[]{:S(2)}, u32[]{:S(2)}) collective-permute-start(f32[16,512]{1,0:T(8,128)S(1)} %get-tuple-element.21), channel_id=1, source_target_pairs={{0,64},{32,96},{64,0},{96,32},{128,192},{160,224},{192,128},{224,1... | collective-permute-start | bytes 98312 | tf_op jit(solution)/shard_map/ppermute | solution.py:362
  33.0 8.9 %collective-permute-start.2 = (f32[16,512]{1,0:T(8,128)S(1)}, f32[16,512]{1,0:T(8,128)S(1)}, u32[]{:S(2)}, u32[]{:S(2)}) collective-permute-start(f32[16,512]{1,0:T(8,128)S(1)} %get-tuple-element.22), channel_id=1, source_target_pairs={{0,96},{32,64},{64,32},{96,0},{128,224},{160,192},{192,160},{224,1... | collective-permute-start | bytes 98312 | tf_op jit(solution)/shard_map/ppermute | solution.py:362
  34.4 7.5 %collective-permute-start.3 = (f32[16,512]{1,0:T(8,128)S(1)}, f32[16,512]{1,0:T(8,128)S(1)}, u32[]{:S(2)}, u32[]{:S(2)}) collective-permute-start(f32[16,512]{1,0:T(8,128)S(1)} %get-tuple-element.23), channel_id=1, source_target_pairs={{0,128},{32,160},{64,192},{96,224},{128,0},{160,32},{192,64},{224,... | collective-permute-start | bytes 98312 | tf_op jit(solution)/shard_map/ppermute | solution.py:362
  34.9 7.1 %collective-permute-start.4 = (f32[16,512]{1,0:T(8,128)S(1)}, f32[16,512]{1,0:T(8,128)S(1)}, u32[]{:S(2)}, u32[]{:S(2)}) collective-permute-start(f32[16,512]{1,0:T(8,128)S(1)} %get-tuple-element.24), channel_id=1, source_target_pairs={{0,160},{32,128},{64,224},{96,192},{128,32},{160,0},{192,96},{224,... | collective-permute-start | bytes 98312 | tf_op jit(solution)/shard_map/ppermute | solution.py:362
  37.7 4.3 %collective-permute-start.5 = (f32[16,512]{1,0:T(8,128)S(1)}, f32[16,512]{1,0:T(8,128)S(1)}, u32[]{:S(2)}, u32[]{:S(2)}) collective-permute-start(f32[16,512]{1,0:T(8,128)S(1)} %get-tuple-element.25), channel_id=1, source_target_pairs={{0,192},{32,224},{64,128},{96,160},{128,64},{160,96},{192,0},{224,... | collective-permute-start | bytes 98312 | tf_op jit(solution)/shard_map/ppermute | solution.py:362
  38.6 4.6 %collective-permute-start.6 = (f32[16,512]{1,0:T(8,128)S(1)}, f32[16,512]{1,0:T(8,128)S(1)}, u32[]{:S(2)}, u32[]{:S(2)}) collective-permute-start(f32[16,512]{1,0:T(8,128)S(1)} %get-tuple-element.26), channel_id=1, source_target_pairs={{0,224},{32,192},{64,160},{96,128},{128,96},{160,64},{192,32},{224... | collective-permute-start | bytes 98312 | tf_op jit(solution)/shard_map/ppermute | solution.py:362
  40.7 2.5 %copy-start.1 = (f32[1,16,4096]{2,1,0:T(8,128)S(1)}, f32[1,16,4096]{2,1,0:T(8,128)}, u32[]{:S(2)}) copy-start(f32[1,16,4096]{2,1,0:T(8,128)} %param.9) | copy-start | bytes 786436
  40.7 2.5 %copy-start.6 = (f32[1,4096]{1,0:T(1,128)S(1)}, f32[1,4096]{1,0:T(1,128)}, u32[]{:S(2)}) copy-start(f32[1,4096]{1,0:T(1,128)} %refs_9_.1) | copy-start | bytes 49156
  40.7 2.5 %copy-start.7 = (f32[1,4096]{1,0:T(1,128)S(1)}, f32[1,4096]{1,0:T(1,128)}, u32[]{:S(2)}) copy-start(f32[1,4096]{1,0:T(1,128)} %refs_10_.1) | copy-start | bytes 49156
  40.9 1.0 %copy-start.4 = (f32[4,16,4096]{2,1,0:T(8,128)}, f32[4,16,4096]{2,1,0:T(8,128)S(1)}, u32[]{:S(2)}) copy-start(f32[4,16,4096]{2,1,0:T(8,128)S(1)} %get-tuple-element.33.blends) | copy-start | bytes 3145732
  43.2 26.1 %copy-start.5 = (f32[4,16,4096]{2,1,0:T(8,128)S(1)}, f32[4,16,4096]{2,1,0:T(8,128)}, u32[]{:S(2)}) copy-start(f32[4,16,4096]{2,1,0:T(8,128)} %copy-done.4) | copy-start | bytes 3145732

commit v2 on v1

--- a/solution.py
+++ b/solution.py
@@ -21,16 +21,15 @@
 PAIRS = [(i, j) for i in range(HIST) for j in range(i, HIST)]
 
 VMEM = pl.BlockSpec(memory_space=pltpu.VMEM)
-SMEM = pl.BlockSpec(memory_space=pltpu.SMEM)
 HBM = pl.BlockSpec(memory_space=pltpu.HBM)
 
 
-def call(kernel, outs, in_specs, flops, nbytes, scratch=(), mib=24):
+def call(kernel, outs, in_specs, flops, nbytes, scratch=(), mib=24, out_specs=None):
     return pl.pallas_call(
         kernel,
         out_shape=outs,
         in_specs=in_specs,
-        out_specs=jax.tree.map(lambda _: VMEM, outs),
+        out_specs=jax.tree.map(lambda _: VMEM, outs) if out_specs is None else out_specs,
         scratch_shapes=list(scratch),
         compiler_params=pltpu.CompilerParams(vmem_limit_bytes=mib * 2**20),
         cost_estimate=pl.CostEstimate(flops=flops, bytes_accessed=nbytes, transcendentals=0),
@@ -84,8 +83,8 @@
     return v, r, 1.0 / (v + r)
 
 
-def flag(directions, index):
-    return jnp.full((ROWS, LANES), directions[index], jnp.int32) == 1
+def flag(notes, index):
+    return jnp.broadcast_to(notes[pl.ds(index, 1), :], (ROWS, LANES)) == 1
 
 
 def down(x):
@@ -96,15 +95,29 @@
     return slice(h * ROWS, (h + 1) * ROWS)
 
 
-def open_kernel(directions, *refs):
-    sources, message, held, arrived = refs[:6], refs[6], refs[7:13], refs[13]
+def added_rows(parts):
+    row = iota(0)
+    parts = parts + [jnp.zeros((ROWS, LANES), jnp.float32)] * (ROWS - len(parts))
+    for d in (4, 2, 1):
+        low = (row & d) == 0
+        count = len(parts) // 2
+        parts = [
+            jnp.where(low, parts[n], parts[n + count])
+            + pick(jnp.where(low, parts[n + count], parts[n]), row ^ d, 0)
+            for n in range(count)
+        ]
+    return parts[0]
+
+
+def open_kernel(*refs):
+    sources, message, notes, held, ready, arrived, gone = refs[:8], refs[8], refs[9], refs[10:18], *refs[18:]
     copies = [pltpu.make_async_copy(a, b, arrived.at[n]) for n, (a, b) in enumerate(zip(sources, held))]
     for copy in copies:
         copy.start()
-    offsets, wigner, velocity, out_rate, inflow, past_residuals = held
+    offsets, wigner, directions, coupling, velocity, out_rate, inflow, past_residuals = held
     tiles = wigner.shape[1] // LANES
     per = message.shape[2] // LANES
-    lane = iota(1)
+    row, lane = iota(0), iota(1)
     zero = jnp.zeros((ROWS, LANES), jnp.float32)
     copies[0].wait()
     copies[1].wait()
@@ -118,36 +131,43 @@
             prv = pick(wigner[half(h), tile(kb - 1)], down_in, 1) if kb else zero
             above = jnp.where(up < LANES, pick(here, up_in, 1), nxt)
             below = jnp.where(below_at >= 0, pick(here, down_in, 1), prv)
-            message[kb // per, half(h), tile(kb % per)] = 0.5 * (above + below)
+            ready[kb // per, half(h), tile(kb % per)] = 0.5 * (above + below)
     for copy in copies[2:]:
         copy.wait()
+    out = [pltpu.make_async_copy(ready.at[b], message.at[b], gone.at[b]) for b in range(message.shape[0])]
     for kb in range(tiles):
-        back = flag(directions, kb)
+        back = jnp.full((ROWS, LANES), directions[kb], jnp.int32) == 1
         slope = []
         for h in range(2):
             v, _, inv = coefficients(velocity, out_rate, kb, h)
             slope.append(v * inv)
         reach, _, _ = scan_tile(back, slope, None)
-
-        def put(row, value):
-            message[kb // per, 2 * ROWS + row : 2 * ROWS + row + 1, tile(kb % per)] = value
-
-        for j in range(HIST):
-            put(j, down(sum(past_residuals[j, half(h), tile(kb)] * reach[h] for h in range(2))))
-        put(4, down(sum(reach[h] * reach[h] for h in range(2))))
-        put(5, down(sum(reach[h] * wigner[half(h), tile(kb)] for h in range(2))))
-        put(6, out_rate[:, tile(kb)])
-        put(7, inflow[:, tile(kb)])
-
-
-def history_kernel(past_iterates, past_residuals, blends, gram):
+        parts = [sum(past_residuals[j, half(h), tile(kb)] * reach[h] for h in range(2)) for j in range(HIST)]
+        parts.append(sum(reach[h] * reach[h] for h in range(2)))
+        parts.append(sum(reach[h] * wigner[half(h), tile(kb)] for h in range(2)))
+        rate = jnp.broadcast_to(out_rate[:, tile(kb)], (ROWS, LANES))
+        enters = jnp.broadcast_to(inflow[:, tile(kb)], (ROWS, LANES))
+        ready[kb // per, 2 * ROWS :, tile(kb % per)] = jnp.where(
+            row == 6, rate, jnp.where(row == 7, enters, added_rows(parts))
+        )
+        if kb % per == per - 1:
+            out[kb // per].start()
+    known = [directions[n] for n in range(tiles)] + [coupling[n] for n in range(coupling.shape[0])]
+    for q in range(len(known) // ROWS):
+        rows = jnp.zeros((ROWS, LANES), jnp.int32)
+        for n in range(ROWS):
+            rows = jnp.where(row == n, known[q * ROWS + n], rows)
+        notes[half(q), :] = rows
+    for copy in out:
+        copy.wait()
+
+
+def history_kernel(past_residuals, gram):
     tiles = past_residuals.shape[2] // LANES
     acc = [jnp.zeros((ROWS, LANES), jnp.float32) for _ in PAIRS]
     for kb in range(tiles):
         for h in range(2):
             past = [past_residuals[j, half(h), tile(kb)] for j in range(HIST)]
-            for j in range(HIST):
-                blends[j, half(h), tile(kb)] = past_iterates[j, half(h), tile(kb)] + MIX_STEP * past[j]
             for n, (i, j) in enumerate(PAIRS):
                 acc[n] = acc[n] + past[i] * past[j]
     gram[...] = jnp.zeros(gram.shape, jnp.float32)
@@ -155,39 +175,51 @@
         gram[6 + n : 7 + n, :] = down(acc[n])
 
 
-def at_contact(ids, blocks, back, slope, inflow):
+def at_contact(blocks, back, slope, inflow):
     row = iota(0)
-    place = jnp.full((ROWS, LANES), ids[1], jnp.int32)
+    place = jnp.full((ROWS, LANES), lax.axis_index(POS), jnp.int32)
     first = (place == 0) & (row == 0) & jnp.logical_not(back)
     final = (place == blocks - 1) & (row == ROWS - 1) & back
     wide = jnp.broadcast_to(inflow, (ROWS, LANES))
     return [jnp.where(first, slope[0] * wide, 0.0), jnp.where(final, slope[1] * wide, 0.0)]
 
 
-def fold_kernel(directions, coupling, ids, held, velocity, message, *shares):
+def fold_kernel(notes, held, velocity, message, *refs):
     bands = held.shape[0]
+    shares, both, ready, gone = refs[:bands], *refs[bands:]
     blocks = message.shape[0]
     per = held.shape[2] // LANES
     row, lane = iota(0), iota(1)
-    for d in range(bands):
-        s = ids[0] ^ d
-        shares[d][...] = held[s, 0 : 2 * ROWS, :] + held[coupling[s], 0 : 2 * ROWS, :]
+    band = lax.axis_index(BAND)
+    first = blocks
+    chosen = [jnp.broadcast_to(notes[first + s : first + s + 1, :], (ROWS, LANES)) for s in range(bands)]
+    out = [
+        pltpu.make_async_copy(
+            ready.at[pl.ds(kt * bands, bands)], message.at[pl.ds(kt * bands, bands)], gone.at[kt]
+        )
+        for kt in range(per)
+    ]
     for kt in range(per):
-        kb = ids[0] * per + kt
-        back = flag(directions, kb)
+        kb = band * per + kt
+        back = flag(notes, kb)
         columns = pl.ds(pl.multiple_of(kb * LANES, LANES), LANES)
+        speeds = [velocity[half(h), columns] for h in range(2)]
+        spread = [[held[s, half(h), tile(kt)] for h in range(2)] for s in range(bands)]
         parts = []
         for s in range(bands):
             tail = held[s, 2 * ROWS :, tile(kt)]
             rate = jnp.broadcast_to(tail[6:7], (ROWS, LANES))
             slope, offset = [], []
             for h in range(2):
-                v = velocity[half(h), columns]
-                inv = 1.0 / (v + rate)
-                both = held[s, half(h), tile(kt)] + held[coupling[s], half(h), tile(kt)]
-                slope.append(v * inv)
-                offset.append(rate * 0.5 * both * inv)
-            edge = at_contact(ids, blocks, back, slope, tail[7:8])
+                partner = spread[0][h]
+                for t in range(1, bands):
+                    partner = jnp.where(chosen[s] == t, spread[t][h], partner)
+                pair = spread[s][h] + partner
+                both[s, half(h), tile(kt)] = pair
+                inv = 1.0 / (speeds[h] + rate)
+                slope.append(speeds[h] * inv)
+                offset.append(rate * 0.5 * pair * inv)
+            edge = at_contact(blocks, back, slope, tail[7:8])
             offset = [offset[h] + edge[h] for h in range(2)]
             reach, run, ends = scan_tile(back, slope, offset)
             crossed = jnp.broadcast_to(down(reach[0] * run[0] + reach[1] * run[1]), (ROWS, LANES)) - tail
@@ -204,19 +236,25 @@
                     swapped[s + step] = jnp.where(high, parts[s + step], pltpu.roll(parts[s], LANES - GROUP * step, 1))
             parts = swapped
         for g in range(bands):
-            message[kt * bands + g] = parts[g]
-
-
-def settle_kernel(directions, ids, *refs):
+            ready[kt * bands + g] = parts[g]
+        out[kt].start()
+    for d in range(bands):
+        shares[d][...] = both[band ^ d]
+    for copy in out:
+        copy.wait()
+
+
+def settle_kernel(notes, *refs):
     shares = refs[:8]
-    velocity, out_rate, inflow, wigner, past_residuals, early, marks, reach_out, rest, gram = refs[8:]
+    velocity, out_rate, inflow, wigner, past_residuals, early, reach_out, rest, gram = refs[8:]
     per = shares[0].shape[1] // LANES
     blocks = velocity.shape[1] // LANES
+    band = lax.axis_index(BAND)
     acc = [jnp.zeros((ROWS, LANES), jnp.float32) for _ in range(HIST + 1)]
     for d in range(len(shares)):
         for kt in range(per):
-            kb = (ids[0] ^ d) * per + kt
-            back = flag(directions, kb)
+            kb = (band ^ d) * per + kt
+            back = flag(notes, kb)
             columns = pl.ds(pl.multiple_of(kb * LANES, LANES), LANES)
             rate = jnp.broadcast_to(out_rate[:, columns], (ROWS, LANES))
             slope, offset = [], []
@@ -225,7 +263,7 @@
                 inv = 1.0 / (v + rate)
                 slope.append(v * inv)
                 offset.append(rate * 0.5 * shares[d][half(h), tile(kt)] * inv)
-            edge = at_contact(ids, blocks, back, slope, inflow[:, columns])
+            edge = at_contact(blocks, back, slope, inflow[:, columns])
             offset = [offset[h] + edge[h] for h in range(2)]
             reach, run, _ = scan_tile(back, slope, offset)
             for h in range(2):
@@ -235,16 +273,15 @@
                 for j in range(HIST):
                     acc[j] = acc[j] + past_residuals[j, half(h), columns] * left
                 acc[HIST] = acc[HIST] + left * left
-    gram[...] = early[...]
-    for n in range(HIST + 1):
-        gram[n : n + 1, :] = down(acc[n])
-    marks[...] = jnp.full((ROWS, LANES), directions[ids[0] * per + ids[1] // ROWS], jnp.int32)
-
-
-def carry_kernel(marks, sums, gram, message, forth, counter):
+    gram[half(0), :] = added_rows(acc)
+    gram[half(1), :] = early[half(1), :]
+    gram[6:8, :] = early[6:8, :]
+
+
+def carry_kernel(notes, sums, gram, message, forth, counter):
     blocks = sums.shape[0]
     row, lane = iota(0), iota(1)
-    back = marks[...] == 1
+    back = flag(notes, lax.axis_index(BAND) * (blocks // ROWS) + lax.axis_index(POS) // ROWS)
     acc = jnp.zeros((ROWS, LANES), jnp.float32)
     carry = jnp.zeros((1, LANES), jnp.float32)
     for step in range(blocks):
@@ -295,9 +332,16 @@
     return [z / total for z in backward]
 
 
-def finish_kernel(message, reach, rest, wigner, blends, residual, mixed):
-    tiles = wigner.shape[1] // LANES
+def finish_kernel(message, reach, rest, wigner, past_iterates, past_residuals, residual, mixed, found, mixes, gone):
+    cells, moments = wigner.shape
+    tiles = moments // LANES
+    pieces = 4
     row, lane = iota(0), iota(1)
+    out = []
+    for n, (source, target) in enumerate(((found, residual), (mixes, mixed))):
+        for q in range(pieces):
+            columns = pl.ds(q * (moments // pieces), moments // pieces)
+            out.append(pltpu.make_async_copy(source.at[:, columns], target.at[:, columns], gone.at[n * pieces + q]))
     total = message[half(0), :]
     for kb in range(1, tiles):
         total = total + message[half(kb), :]
@@ -311,63 +355,72 @@
             return term(4) + term(5) if i == HIST else term(i)
         return term(6 + PAIRS.index((i, j)))
 
-    weights = mixing_weights(entry)
     for kb in range(tiles):
         spots = pick(message[half(kb), :], lane & (GROUP - 1), 1)
         carry = jnp.broadcast_to(down(jnp.where((lane >> 4) == row, spots, 0.0)), (ROWS, LANES))
         for h in range(2):
-            found = rest[half(h), tile(kb)] + reach[half(h), tile(kb)] * carry
-            residual[half(h), tile(kb)] = found
-            value = weights[HIST] * (wigner[half(h), tile(kb)] + MIX_STEP * found)
+            found[half(h), tile(kb)] = rest[half(h), tile(kb)] + reach[half(h), tile(kb)] * carry
+        if (kb + 1) % (tiles // pieces) == 0:
+            out[kb // (tiles // pieces)].start()
+    weights = mixing_weights(entry)
+    for kb in range(tiles):
+        for h in range(2):
+            value = weights[HIST] * (wigner[half(h), tile(kb)] + MIX_STEP * found[half(h), tile(kb)])
             for j in range(HIST):
-                value = value + weights[j] * blends[j, half(h), tile(kb)]
-            mixed[half(h), tile(kb)] = value
+                earlier = past_iterates[j, half(h), tile(kb)] + MIX_STEP * past_residuals[j, half(h), tile(kb)]
+                value = value + weights[j] * earlier
+            mixes[half(h), tile(kb)] = value
+        if (kb + 1) % (tiles // pieces) == 0:
+            out[pieces + kb // (tiles // pieces)].start()
+    for copy in out:
+        copy.wait()
 
 
 def body(wigner, past_iterates, past_residuals, velocity, out_rate, inflow, offsets, directions, coupling):
     _, cells, moments = wigner.shape
     bands = lax.axis_size(BAND)
     blocks = lax.axis_size(POS)
-    ids = jnp.stack([lax.axis_index(BAND), lax.axis_index(POS)]).astype(jnp.int32)
     wigner = wigner.reshape(cells, moments)
     past_iterates = past_iterates.reshape(HIST, cells, moments)
     past_residuals = past_residuals.reshape(HIST, cells, moments)
     offsets = offsets.reshape(1, moments)
     size = 4 * cells * moments
     share = moments // bands
-
-    sources = (offsets, wigner, velocity, out_rate, inflow, past_residuals)
-    message = call(
+    field = f32(cells, moments)
+    dma = pltpu.SemaphoreType.DMA
+
+    sources = (offsets, wigner, directions, coupling, velocity, out_rate, inflow, past_residuals)
+    opened = f32(bands, cells + ROWS, share)
+    message, notes = call(
         open_kernel,
-        f32(bands, cells + ROWS, share),
-        [SMEM] + [HBM] * 6,
+        (opened, jax.ShapeDtypeStruct((blocks + bands, LANES), jnp.int32)),
+        [HBM] * 8,
         20 * size,
         8 * size,
-        [pltpu.VMEM(x.shape, x.dtype) for x in sources] + [pltpu.SemaphoreType.DMA((6,))],
-        mib=60,
-    )(directions, *sources)
+        [(pltpu.SMEM if x.ndim == 1 else pltpu.VMEM)(x.shape, x.dtype) for x in sources]
+        + [pltpu.VMEM(opened.shape, jnp.float32), dma((8,)), dma((bands,))],
+        60,
+        (HBM, VMEM),
+    )(*sources)
     held = lax.all_to_all(message, BAND, 0, 0, tiled=True)
-    blends, early = call(
-        history_kernel, (f32(HIST, cells, moments), f32(16, LANES)), [VMEM] * 2, 8 * size, 12 * size
-    )(past_iterates, past_residuals)
+    early = call(history_kernel, f32(16, LANES), [VMEM], 8 * size, 4 * size)(past_residuals)
+    held, early = lax.optimization_barrier((held, early))
     sums, *shares = call(
         fold_kernel,
         (f32(blocks, ROWS, LANES),) + (f32(cells, share),) * bands,
-        [SMEM] * 3 + [VMEM] * 2,
+        [VMEM] * 3,
         20 * size,
         5 * size,
-    )(directions, coupling, ids, held, velocity)
+        [pltpu.VMEM((bands, cells, share), jnp.float32), pltpu.VMEM((blocks, ROWS, LANES), jnp.float32), dma((4,))],
+        out_specs=(HBM,) + (VMEM,) * bands,
+    )(notes, held, velocity)
     sums = lax.all_to_all(sums, POS, 0, 0, tiled=True)
     shares = [shares[0]] + [
         lax.ppermute(shares[d], BAND, [(i, i ^ d) for i in range(bands)]) for d in range(1, bands)
     ]
-    marks, reach, rest, gram = call(
-        settle_kernel,
-        (jax.ShapeDtypeStruct((ROWS, LANES), jnp.int32), f32(cells, moments), f32(cells, moments), f32(16, LANES)),
-        [SMEM] * 2 + [VMEM] * 14,
-        20 * size,
-        10 * size,
-    )(directions, ids, *shares, velocity, out_rate, inflow, wigner, past_residuals, early)
+    reach, rest, gram = call(
+        settle_kernel, (field, field, f32(16, LANES)), [VMEM] * 15, 20 * size, 10 * size
+    )(notes, *shares, velocity, out_rate, inflow, wigner, past_residuals, early)
     message = call(
         carry_kernel,
         f32(bands * blocks, LANES),
@@ -375,11 +428,17 @@
         size,
         size,
         [pltpu.VMEM((blocks, LANES), jnp.float32)] * 2,
-    )(marks, sums, gram)
+    )(notes, sums, gram)
     message = lax.all_to_all(message, ALL, 0, 0, tiled=True)
     residual, mixed = call(
-        finish_kernel, (f32(cells, moments), f32(cells, moments)), [VMEM] * 5, 8 * size, 10 * size
-    )(message, reach, rest, wigner, blends)
+        finish_kernel,
+        (field, field),
+        [VMEM] * 6,
+        8 * size,
+        14 * size,
+        [pltpu.VMEM((cells, moments), jnp.float32)] * 2 + [dma((8,))],
+        out_specs=(HBM, HBM),
+    )(message, reach, rest, wigner, past_iterates, past_residuals)
     return mixed[None], residual[None]
 
 

time: 70.7 us -> 69.6 us (0.984)
  waiting for transfers between devices: 9.28 us -> 10.4 us
  Pallas kernels: 8.19 us -> 7.16 us
  local copies, waits for them, and re-layouts: 1.02 us -> 0.03 us
    ppermute x7, waiting for transfers between devices: 1.26 us -> 2.54 us  [body(): lax.ppermute(shares[d], BAND, [(i, i ^ d) for i in range(bands)])]
    unnamed x20 -> x14, local copies, waits for them, and re-layouts: 1.02 us -> 0.03 us
  transfers between devices with their start and end apart: 9 -> 9, of which waited for: 3 -> 3; matrix products, arithmetic and copies ran while one was open for 0% -> 0% of each run, Pallas kernels for 2% -> 1%
where the time goes in v2:
time: 69.6 us; the launch traced here: 69.3 us
  starting transfers between devices  26.3 us (38%)
  blocking collectives  24.7 us (35%)
  waiting for transfers between devices  10.4 us (15%)
  Pallas kernels  7.16 us (10%)
  between operations  0.73 us (1%)
    all_to_all x1, blocking collectives, body(): message = lax.all_to_all(message, ALL, 0, 0, tiled=True)  24.7 us
    all_to_all x1, starting transfers between devices, body(): sums = lax.all_to_all(sums, POS, 0, 0, tiled=True)  10.5 us
    ppermute x7, starting transfers between devices, body(): lax.ppermute(shares[d], BAND, [(i, i ^ d) for i in range(bands)])  9.18 us
    all_to_all x1, waiting for transfers between devices, body(): held = lax.all_to_all(message, BAND, 0, 0, tiled=True)  7.85 us
    all_to_all x1, starting transfers between devices, body(): held = lax.all_to_all(message, BAND, 0, 0, tiled=True)  6.61 us
    pallas_call x1, Pallas kernels, body(): call(open_kernel, (opened, jax.ShapeDtypeStruct((blocks + bands, LANES),...  3.56 us
    ppermute x7, waiting for transfers between devices, body(): lax.ppermute(shares[d], BAND, [(i, i ^ d) for i in range(bands)])  2.54 us
    pallas_call x1, Pallas kernels, body(): call(fold_kernel, (f32(blocks, ROWS, LANES),) + (f32(cells, share),) * ba...  1.39 us
  transfers between devices with their start and end apart: 9, of which 3 were waited for; matrix products, arithmetic and copies ran while one was open for 0% of the time, Pallas kernels for 1%

profile of v2, /device:TPU:1, one launch (start us, length us, event | category | flops | bytes accessed | tf_op | source)
XLA Modules:
  0.0 69.3 jit_solution(7914920432195881499)
XLA Ops:
  0.6 0.0 copy-start
  0.6 3.6 %shard_map.104 = (f32[8,24,512]{2,1,0:T(8,128)}, s32[40,128]{1,0:T(8,128)}) custom-call(s32[1,4096]{1,0:T(1,128)} %bitcast.20, f32[16,4096]{1,0:T(8,128)} %bitcast.14, s32[32]{0:T(128)} %refs_2_.1, s32[8]{0:T(128)} %refs_3_.1, f32[16,4096]{1,0:T(8,128)} %refs_8_.1, f32[1,4096]{1,0:T(1,128)} %refs_9_.1, f32[1,4096]{1,0:T(1,128)} %refs_10_.1, ...), custom_call_target="tpu_custom_call" | custom-call | flops 5242880 | bytes 2097152 | tf_op jit(solution)/shard_map/pallas_call | solution.py:394
  4.2 6.6 %all-to-all-start = ((f32[8,24,512]{2,1,0:T(8,128)}), f32[8,24,512]{2,1,0:T(8,128)S(1)}, u32[]{:S(2)}, u32[]{:S(2)}) async-start(f32[8,24,512]{2,1,0:T(8,128)} %get-tuple-element.21), calls=%async_computation | async-start | bytes 786432 | tf_op jit(solution)/shard_map/all_to_all | solution.py:405
  10.8 0.0 copy-done
  10.8 0.0 copy-start.2
  10.8 0.0 copy-start.4
  10.8 0.2 shard_map.105.refs_13_
  11.1 7.8 %all-to-all-done.held = f32[8,24,512]{2,1,0:T(8,128)S(1)} async-done(((f32[8,24,512]{2,1,0:T(8,128)}), f32[8,24,512]{2,1,0:T(8,128)S(1)}, u32[]{:S(2)}, u32[]{:S(2)}) %all-to-all-start) | async-done | bytes 393248 | tf_op jit(solution)/shard_map/all_to_all | solution.py:405
  18.9 0.0 copy-done.2
  18.9 0.0 copy-done.4
  18.9 0.0 copy-start.6
  18.9 1.4 %shard_map.106 = (f32[32,8,128]{2,1,0:T(8,128)}, f32[16,512]{1,0:T(8,128)S(1)}, f32[16,512]{1,0:T(8,128)S(1)}, f32[16,512]{1,0:T(8,128)S(1)}, f32[16,512]{1,0:T(...) custom-call(s32[40,128]{1,0:T(8,128)S(1)} %copy-done.4, ...), custom_call_target="tpu_custom_call" | custom-call | flops 5242880 | bytes 1310720 | tf_op jit(solution)/shard_map/pallas_call | solution.py:408
  20.3 0.0 copy-start.1
  20.3 0.0 copy-start.5
  20.3 10.5 %all-to-all-start.1 = ((f32[32,8,128]{2,1,0:T(8,128)}), f32[32,8,128]{2,1,0:T(8,128)S(1)}, u32[]{:S(2)}, u32[]{:S(2)}) async-start(f32[32,8,128]{2,1,0:T(8,128)} %get-tuple-element.23), calls=%async_computation.1 | async-start | bytes 262144 | tf_op jit(solution)/shard_map/all_to_all | solution.py:417
  30.9 1.2 %collective-permute-start = (f32[16,512]{1,0:T(8,128)S(1)}, f32[16,512]{1,0:T(8,128)S(1)}, u32[]{:S(2)}, u32[]{:S(2)}) collective-permute-start(f32[16,512]{1,0:T(8,128)S(1)} %get-tuple-element.25), channel_id=1, source_target_pairs={{0,32},{32,0},{64,96},{96,64},{128,160},{160,128},{192,224},{224,1... | collective-permute-start | bytes 98312 | tf_op jit(solution)/shard_map/ppermute | solution.py:419
  32.1 0.3 collective-permute-start.1
  32.4 1.4 %collective-permute-start.2 = (f32[16,512]{1,0:T(8,128)S(1)}, f32[16,512]{1,0:T(8,128)S(1)}, u32[]{:S(2)}, u32[]{:S(2)}) collective-permute-start(f32[16,512]{1,0:T(8,128)S(1)} %get-tuple-element.27), channel_id=1, source_target_pairs={{0,96},{32,64},{64,32},{96,0},{128,224},{160,192},{192,160},{224,1... | collective-permute-start | bytes 98312 | tf_op jit(solution)/shard_map/ppermute | solution.py:419
  33.9 0.4 collective-permute-start.3
  34.3 2.9 %collective-permute-start.4 = (f32[16,512]{1,0:T(8,128)S(1)}, f32[16,512]{1,0:T(8,128)S(1)}, u32[]{:S(2)}, u32[]{:S(2)}) collective-permute-start(f32[16,512]{1,0:T(8,128)S(1)} %get-tuple-element.29), channel_id=1, source_target_pairs={{0,160},{32,128},{64,224},{96,192},{128,32},{160,0},{192,96},{224,... | collective-permute-start | bytes 98312 | tf_op jit(solution)/shard_map/ppermute | solution.py:419
  37.2 0.0 collective-permute-done.refs_1_
  37.2 0.9 %collective-permute-start.5 = (f32[16,512]{1,0:T(8,128)S(1)}, f32[16,512]{1,0:T(8,128)S(1)}, u32[]{:S(2)}, u32[]{:S(2)}) collective-permute-start(f32[16,512]{1,0:T(8,128)S(1)} %get-tuple-element.30), channel_id=1, source_target_pairs={{0,192},{32,224},{64,128},{96,160},{128,64},{160,96},{192,0},{224,... | collective-permute-start | bytes 98312 | tf_op jit(solution)/shard_map/ppermute | solution.py:419
  38.0 0.0 collective-permute-done.1.refs_2_
  38.1 2.0 %collective-permute-start.6 = (f32[16,512]{1,0:T(8,128)S(1)}, f32[16,512]{1,0:T(8,128)S(1)}, u32[]{:S(2)}, u32[]{:S(2)}) collective-permute-start(f32[16,512]{1,0:T(8,128)S(1)} %get-tuple-element.31), channel_id=1, source_target_pairs={{0,224},{32,192},{64,160},{96,128},{128,96},{160,64},{192,32},{224... | collective-permute-start | bytes 98312 | tf_op jit(solution)/shard_map/ppermute | solution.py:419
  40.1 0.0 collective-permute-done.2.refs_3_
  40.1 0.0 collective-permute-done.3.refs_4_
  40.1 0.0 collective-permute-done.4.refs_5_
  40.1 1.3 %collective-permute-done.5.refs_6_ = f32[16,512]{1,0:T(8,128)S(1)} collective-permute-done((f32[16,512]{1,0:T(8,128)S(1)}, f32[16,512]{1,0:T(8,128)S(1)}, u32[]{:S(2)}, u32[]{:S(2)}) %collective-permute-start.5) | collective-permute-done | bytes 32800 | tf_op jit(solution)/shard_map/ppermute | solution.py:419
  41.4 1.2 %collective-permute-done.6.refs_7_ = f32[16,512]{1,0:T(8,128)S(1)} collective-permute-done((f32[16,512]{1,0:T(8,128)S(1)}, f32[16,512]{1,0:T(8,128)S(1)}, u32[]{:S(2)}, u32[]{:S(2)}) %collective-permute-start.6) | collective-permute-done | bytes 32800 | tf_op jit(solution)/shard_map/ppermute | solution.py:419
  42.6 0.0 copy-done.6
  42.6 0.0 copy-done.1
  42.6 0.0 copy-done.5
  42.6 0.0 copy-start.3
  42.6 0.7 shard_map.107
  43.3 0.0 all-to-all-done.1.sums
  43.3 0.2 shard_map.108
  43.5 24.7 %all_to_all.21 = f32[256,1,128]{2,1,0:T(1,128)S(1)} all-to-all(f32[256,1,128]{2,1,0:T(1,128)S(1)} %bitcast.19), channel_id=1, replica_groups=mesh['band_0'=4,'band_1'=2,'pos_0'=4,'pos_1'=8] {'band_0','band_1','pos_..., dimensions={0} | all-to-all | bytes 262144 | tf_op jit(solution)/shard_map/all_to_all | solution.py:432
  68.2 0.0 copy-done.3
  68.2 1.1 %shard_map.109 = (f32[16,4096]{1,0:T(8,128)}, f32[16,4096]{1,0:T(8,128)}) custom-call(f32[256,128]{1,0:T(8,128)S(1)} %bitcast.18, f32[16,4096]{1,0:T(8,128)S(1)} %get-tuple-element.34.reach, f32[16,4096]{1,0:T(8,128)S(1)} %get-tuple-element.35.rest, f32[16,4096]{1,0:T(8,128)S(1)} %bitcast.16, f32[4,16,4096]{2,1,0:T(8,128)S(1)} %bitcast.17, ...), custom_call_target="tpu_custom_call" | custom-call | flops 2097152 | bytes 3670016 | tf_op jit(solution)/shard_map/pallas_call | solution.py:433
Async XLA Ops:
  0.6 10.2 %copy-start = (f32[4,1,16,4096]{3,2,1,0:T(8,128)S(1)}, f32[4,1,16,4096]{3,2,1,0:T(8,128)}, u32[]{:S(2)}) copy-start(f32[4,1,16,4096]{3,2,1,0:T(8,128)} %param.11) | copy-start | bytes 3145732
  4.2 14.7 %all-to-all-start = ((f32[8,24,512]{2,1,0:T(8,128)}), f32[8,24,512]{2,1,0:T(8,128)S(1)}, u32[]{:S(2)}, u32[]{:S(2)}) async-start(f32[8,24,512]{2,1,0:T(8,128)} %get-tuple-element.21), calls=%async_computation | async-start | bytes 786432 | tf_op jit(solution)/shard_map/all_to_all | solution.py:405
  10.8 8.1 %copy-start.2 = (f32[16,4096]{1,0:T(8,128)S(1)}, f32[16,4096]{1,0:T(8,128)}, u32[]{:S(2)}) copy-start(f32[16,4096]{1,0:T(8,128)} %refs_8_.1) | copy-start | bytes 786436
  10.8 8.1 %copy-start.4 = (s32[40,128]{1,0:T(8,128)S(1)}, s32[40,128]{1,0:T(8,128)}, u32[]{:S(2)}) copy-start(s32[40,128]{1,0:T(8,128)} %get-tuple-element.20.notes) | copy-start | bytes 61444
  18.9 23.7 %copy-start.6 = (f32[1,4096]{1,0:T(1,128)S(1)}, f32[1,4096]{1,0:T(1,128)}, u32[]{:S(2)}) copy-start(f32[1,4096]{1,0:T(1,128)} %refs_10_.1) | copy-start | bytes 49156
  20.3 22.3 %copy-start.1 = (f32[1,16,4096]{2,1,0:T(8,128)S(1)}, f32[1,16,4096]{2,1,0:T(8,128)}, u32[]{:S(2)}) copy-start(f32[1,16,4096]{2,1,0:T(8,128)} %param.9) | copy-start | bytes 786436
  20.3 22.3 %copy-start.5 = (f32[1,4096]{1,0:T(1,128)S(1)}, f32[1,4096]{1,0:T(1,128)}, u32[]{:S(2)}) copy-start(f32[1,4096]{1,0:T(1,128)} %refs_9_.1) | copy-start | bytes 49156
  20.3 23.0 %all-to-all-start.1 = ((f32[32,8,128]{2,1,0:T(8,128)}), f32[32,8,128]{2,1,0:T(8,128)S(1)}, u32[]{:S(2)}, u32[]{:S(2)}) async-start(f32[32,8,128]{2,1,0:T(8,128)} %get-tuple-element.23), calls=%async_computation.1 | async-start | bytes 262144 | tf_op jit(solution)/shard_map/all_to_all | solution.py:417
  30.9 6.3 %collective-permute-start = (f32[16,512]{1,0:T(8,128)S(1)}, f32[16,512]{1,0:T(8,128)S(1)}, u32[]{:S(2)}, u32[]{:S(2)}) collective-permute-start(f32[16,512]{1,0:T(8,128)S(1)} %get-tuple-element.25), channel_id=1, source_target_pairs={{0,32},{32,0},{64,96},{96,64},{128,160},{160,128},{192,224},{224,1... | collective-permute-start | bytes 98312 | tf_op jit(solution)/shard_map/ppermute | solution.py:419
  32.1 5.9 %collective-permute-start.1 = (f32[16,512]{1,0:T(8,128)S(1)}, f32[16,512]{1,0:T(8,128)S(1)}, u32[]{:S(2)}, u32[]{:S(2)}) collective-permute-start(f32[16,512]{1,0:T(8,128)S(1)} %get-tuple-element.26), channel_id=1, source_target_pairs={{0,64},{32,96},{64,0},{96,32},{128,192},{160,224},{192,128},{224,1... | collective-permute-start | bytes 98312 | tf_op jit(solution)/shard_map/ppermute | solution.py:419
  32.4 7.6 %collective-permute-start.2 = (f32[16,512]{1,0:T(8,128)S(1)}, f32[16,512]{1,0:T(8,128)S(1)}, u32[]{:S(2)}, u32[]{:S(2)}) collective-permute-start(f32[16,512]{1,0:T(8,128)S(1)} %get-tuple-element.27), channel_id=1, source_target_pairs={{0,96},{32,64},{64,32},{96,0},{128,224},{160,192},{192,160},{224,1... | collective-permute-start | bytes 98312 | tf_op jit(solution)/shard_map/ppermute | solution.py:419
  33.9 6.2 %collective-permute-start.3 = (f32[16,512]{1,0:T(8,128)S(1)}, f32[16,512]{1,0:T(8,128)S(1)}, u32[]{:S(2)}, u32[]{:S(2)}) collective-permute-start(f32[16,512]{1,0:T(8,128)S(1)} %get-tuple-element.28), channel_id=1, source_target_pairs={{0,128},{32,160},{64,192},{96,224},{128,0},{160,32},{192,64},{224,... | collective-permute-start | bytes 98312 | tf_op jit(solution)/shard_map/ppermute | solution.py:419
  34.3 5.8 %collective-permute-start.4 = (f32[16,512]{1,0:T(8,128)S(1)}, f32[16,512]{1,0:T(8,128)S(1)}, u32[]{:S(2)}, u32[]{:S(2)}) collective-permute-start(f32[16,512]{1,0:T(8,128)S(1)} %get-tuple-element.29), channel_id=1, source_target_pairs={{0,160},{32,128},{64,224},{96,192},{128,32},{160,0},{192,96},{224,... | collective-permute-start | bytes 98312 | tf_op jit(solution)/shard_map/ppermute | solution.py:419
  37.2 4.3 %collective-permute-start.5 = (f32[16,512]{1,0:T(8,128)S(1)}, f32[16,512]{1,0:T(8,128)S(1)}, u32[]{:S(2)}, u32[]{:S(2)}) collective-permute-start(f32[16,512]{1,0:T(8,128)S(1)} %get-tuple-element.30), channel_id=1, source_target_pairs={{0,192},{32,224},{64,128},{96,160},{128,64},{160,96},{192,0},{224,... | collective-permute-start | bytes 98312 | tf_op jit(solution)/shard_map/ppermute | solution.py:419
  38.1 4.6 %collective-permute-start.6 = (f32[16,512]{1,0:T(8,128)S(1)}, f32[16,512]{1,0:T(8,128)S(1)}, u32[]{:S(2)}, u32[]{:S(2)}) collective-permute-start(f32[16,512]{1,0:T(8,128)S(1)} %get-tuple-element.31), channel_id=1, source_target_pairs={{0,224},{32,192},{64,160},{96,128},{128,96},{160,64},{192,32},{224... | collective-permute-start | bytes 98312 | tf_op jit(solution)/shard_map/ppermute | solution.py:419
  42.6 25.6 %copy-start.3 = (f32[4,1,16,4096]{3,2,1,0:T(8,128)S(1)}, f32[4,1,16,4096]{3,2,1,0:T(8,128)}, u32[]{:S(2)}) copy-start(f32[4,1,16,4096]{3,2,1,0:T(8,128)} %param.10) | copy-start | bytes 3145732

commit v3 on v2

--- a/solution.py
+++ b/solution.py
@@ -186,7 +186,7 @@
 
 def fold_kernel(notes, held, velocity, message, *refs):
     bands = held.shape[0]
-    shares, both, ready, gone = refs[:bands], *refs[bands:]
+    own, other, both, ready, gone = refs
     blocks = message.shape[0]
     per = held.shape[2] // LANES
     row, lane = iota(0), iota(1)
@@ -238,20 +238,21 @@
         for g in range(bands):
             ready[kt * bands + g] = parts[g]
         out[kt].start()
-    for d in range(bands):
-        shares[d][...] = both[band ^ d]
+    for d in range(bands // 2):
+        own[d] = both[band ^ (2 * d)]
+        other[d] = both[band ^ (2 * d + 1)]
     for copy in out:
         copy.wait()
 
 
 def settle_kernel(notes, *refs):
-    shares = refs[:8]
-    velocity, out_rate, inflow, wigner, past_residuals, early, reach_out, rest, gram = refs[8:]
-    per = shares[0].shape[1] // LANES
+    shares = refs[:-9]
+    velocity, out_rate, inflow, wigner, past_residuals, early, reach_out, rest, gram = refs[-9:]
+    per = rest.shape[2] // LANES
     blocks = velocity.shape[1] // LANES
     band = lax.axis_index(BAND)
     acc = [jnp.zeros((ROWS, LANES), jnp.float32) for _ in range(HIST + 1)]
-    for d in range(len(shares)):
+    for d in range(2 * len(shares)):
         for kt in range(per):
             kb = (band ^ d) * per + kt
             back = flag(notes, kb)
@@ -262,25 +263,24 @@
                 v = velocity[half(h), columns]
                 inv = 1.0 / (v + rate)
                 slope.append(v * inv)
-                offset.append(rate * 0.5 * shares[d][half(h), tile(kt)] * inv)
+                offset.append(rate * 0.5 * shares[d // 2][d % 2, half(h), tile(kt)] * inv)
             edge = at_contact(blocks, back, slope, inflow[:, columns])
             offset = [offset[h] + edge[h] for h in range(2)]
             reach, run, _ = scan_tile(back, slope, offset)
             for h in range(2):
                 left = run[h] - wigner[half(h), columns]
-                rest[half(h), columns] = left
-                reach_out[half(h), columns] = reach[h]
+                rest[d, half(h), tile(kt)] = left
+                reach_out[d, half(h), tile(kt)] = reach[h]
                 for j in range(HIST):
                     acc[j] = acc[j] + past_residuals[j, half(h), columns] * left
                 acc[HIST] = acc[HIST] + left * left
-    gram[half(0), :] = added_rows(acc)
+    gram[half(0), :] = early[half(0), :] + added_rows(acc)
     gram[half(1), :] = early[half(1), :]
-    gram[6:8, :] = early[6:8, :]
-
-
-def carry_kernel(notes, sums, gram, message, forth, counter):
+
+
+def carry_kernel(notes, sums, carries, terms, forth, counter):
     blocks = sums.shape[0]
-    row, lane = iota(0), iota(1)
+    row = iota(0)
     back = flag(notes, lax.axis_index(BAND) * (blocks // ROWS) + lax.axis_index(POS) // ROWS)
     acc = jnp.zeros((ROWS, LANES), jnp.float32)
     carry = jnp.zeros((1, LANES), jnp.float32)
@@ -291,16 +291,23 @@
         counter[blocks - 1 - step : blocks - step, :] = carry
         acc = acc + part * jnp.where(row == 4, wide * wide, jnp.where(row == 5, 2.0 * wide, wide))
         carry = part[6:7] * carry + part[7:8]
-    terms = [gram[half(0), :] + jnp.where(row < 6, acc, 0.0), gram[half(1), :]]
+    for q in range(blocks // ROWS):
+        carries[half(q), :] = jnp.where(back, counter[half(q), :], forth[half(q), :])
+    terms[...] = jnp.where(row < 6, acc, 0.0)
+
+
+def message_kernel(carries, terms, gram, message):
+    blocks = carries.shape[0]
+    row, lane = iota(0), iota(1)
+    whole = [gram[half(0), :] + terms[...], gram[half(1), :]]
     line = jnp.zeros((ROWS, LANES), jnp.float32)
     for h in range(2):
-        whole = jnp.broadcast_to(jnp.sum(terms[h], axis=1, keepdims=True), (ROWS, LANES))
-        line = line + jnp.where(lane == GROUP + h * ROWS + row, whole, 0.0)
+        total = jnp.broadcast_to(jnp.sum(whole[h], axis=1, keepdims=True), (ROWS, LANES))
+        line = line + jnp.where(lane == GROUP + h * ROWS + row, total, 0.0)
     line = jnp.broadcast_to(down(line), (ROWS, LANES))
     for q in range(blocks // ROWS):
-        carries = jnp.where(back, counter[half(q), :], forth[half(q), :])
         for s in range(LANES // GROUP):
-            turned = pltpu.roll(carries, LANES - GROUP * s, 1) if s else carries
+            turned = pltpu.roll(carries[half(q), :], LANES - GROUP * s, 1) if s else carries[half(q), :]
             message[s * blocks + q * ROWS : s * blocks + (q + 1) * ROWS, :] = jnp.where(lane < GROUP, turned, line)
 
 
@@ -332,8 +339,12 @@
     return [z / total for z in backward]
 
 
-def finish_kernel(message, reach, rest, wigner, past_iterates, past_residuals, residual, mixed, found, mixes, gone):
+def finish_kernel(message, *refs):
+    reach, rest, wigner, past_iterates, past_residuals, residual, mixed, found, mixes, gone = refs
     cells, moments = wigner.shape
+    bands, _, share = rest.shape
+    per = share // LANES
+    band = lax.axis_index(BAND)
     tiles = moments // LANES
     pieces = 4
     row, lane = iota(0), iota(1)
@@ -355,13 +366,17 @@
             return term(4) + term(5) if i == HIST else term(i)
         return term(6 + PAIRS.index((i, j)))
 
-    for kb in range(tiles):
-        spots = pick(message[half(kb), :], lane & (GROUP - 1), 1)
-        carry = jnp.broadcast_to(down(jnp.where((lane >> 4) == row, spots, 0.0)), (ROWS, LANES))
-        for h in range(2):
-            found[half(h), tile(kb)] = rest[half(h), tile(kb)] + reach[half(h), tile(kb)] * carry
-        if (kb + 1) % (tiles // pieces) == 0:
-            out[kb // (tiles // pieces)].start()
+    for d in range(bands):
+        for kt in range(per):
+            kb = (band ^ d) * per + kt
+            rows = message[pl.ds(pl.multiple_of(kb * ROWS, ROWS), ROWS), :]
+            spots = pick(rows, lane & (GROUP - 1), 1)
+            carry = jnp.broadcast_to(down(jnp.where((lane >> 4) == row, spots, 0.0)), (ROWS, LANES))
+            for h in range(2):
+                at = (d, half(h), tile(kt))
+                found[half(h), pl.ds(pl.multiple_of(kb * LANES, LANES), LANES)] = rest[at] + reach[at] * carry
+    for copy in out[:pieces]:
+        copy.start()
     weights = mixing_weights(entry)
     for kb in range(tiles):
         for h in range(2):
@@ -405,30 +420,40 @@
     held = lax.all_to_all(message, BAND, 0, 0, tiled=True)
     early = call(history_kernel, f32(16, LANES), [VMEM], 8 * size, 4 * size)(past_residuals)
     held, early = lax.optimization_barrier((held, early))
-    sums, *shares = call(
+    chips = lax.axis_size(BAND[0])
+    part = f32(chips, cells, share)
+    sums, own, other = call(
         fold_kernel,
-        (f32(blocks, ROWS, LANES),) + (f32(cells, share),) * bands,
+        (f32(blocks, ROWS, LANES), part, part),
         [VMEM] * 3,
         20 * size,
         5 * size,
         [pltpu.VMEM((bands, cells, share), jnp.float32), pltpu.VMEM((blocks, ROWS, LANES), jnp.float32), dma((4,))],
-        out_specs=(HBM,) + (VMEM,) * bands,
+        out_specs=(HBM, VMEM, VMEM),
     )(notes, held, velocity)
     sums = lax.all_to_all(sums, POS, 0, 0, tiled=True)
-    shares = [shares[0]] + [
-        lax.ppermute(shares[d], BAND, [(i, i ^ d) for i in range(bands)]) for d in range(1, bands)
+    other = lax.ppermute(other, BAND[1], [(0, 1), (1, 0)])
+    across = [jnp.stack([own[d], other[d]]) for d in range(chips)]
+    across = across[:1] + [
+        lax.ppermute(across[d], BAND[0], [(i, i ^ d) for i in range(chips)]) for d in range(1, chips)
     ]
+    local = (velocity, out_rate, inflow, wigner, past_residuals)
     reach, rest, gram = call(
-        settle_kernel, (field, field, f32(16, LANES)), [VMEM] * 15, 20 * size, 10 * size
-    )(notes, *shares, velocity, out_rate, inflow, wigner, past_residuals, early)
-    message = call(
-        carry_kernel,
-        f32(bands * blocks, LANES),
-        [VMEM] * 3,
+        settle_kernel,
+        (f32(bands, cells, share), f32(bands, cells, share), f32(16, LANES)),
+        [VMEM] * (chips + 7),
         size,
         size,
+    )(notes, *across, *local, early)
+    carries, terms = call(
+        carry_kernel,
+        (f32(blocks, LANES), f32(ROWS, LANES)),
+        [VMEM] * 2,
+        size,
+        256 * size,
         [pltpu.VMEM((blocks, LANES), jnp.float32)] * 2,
-    )(notes, sums, gram)
+    )(notes, sums)
+    message = call(message_kernel, f32(bands * blocks, LANES), [VMEM] * 3, size, size)(carries, terms, gram)
     message = lax.all_to_all(message, ALL, 0, 0, tiled=True)
     residual, mixed = call(
         finish_kernel,

time: 69.6 us -> 68.1 us (0.978)
  starting transfers between devices: 26.3 us -> 22.2 us
  waiting for transfers between devices: 10.4 us -> 11.9 us
  blocking collectives: 24.7 us -> 25.8 us
    ppermute x7 -> x4, starting transfers between devices: 9.18 us -> 5.18 us  [the longest x3 3.95 us: body(): lax.ppermute(across[d], BAND[0], [(i, i ^ d) for i in range(chips)])]
    ppermute x7 -> x4, waiting for transfers between devices: 2.54 us -> 4.08 us  [the longest x3 3.11 us: body(): lax.ppermute(across[d], BAND[0], [(i, i ^ d) for i in range(chips)])]
    all_to_all x1, blocking collectives: 24.7 us -> 25.8 us  [body(): message = lax.all_to_all(message, ALL, 0, 0, tiled=True)]
    pallas_call x3 -> x4, Pallas kernels: 2.26 us -> 2.15 us  [the longest x1 1.39 us: body(): call(fold_kernel, (f32(blocks, ROWS, LANES), part, part), [VMEM] * 3, 20...]
  transfers between devices with their start and end apart: 9 -> 6, of which waited for: 3 -> 4; matrix products, arithmetic and copies ran while one was open for 0% -> 0% of each run, Pallas kernels for 1% -> 1%
where the time goes in v3:
time: 68.1 us; the launch traced here: 67.9 us
  blocking collectives  25.8 us (38%)
  starting transfers between devices  22.2 us (33%)
  waiting for transfers between devices  11.9 us (17%)
  Pallas kernels  7.08 us (10%)
  between operations  0.74 us (1%)
    all_to_all x1, blocking collectives, body(): message = lax.all_to_all(message, ALL, 0, 0, tiled=True)  25.8 us
    all_to_all x1, starting transfers between devices, body(): sums = lax.all_to_all(sums, POS, 0, 0, tiled=True)  10.4 us
    all_to_all x1, waiting for transfers between devices, body(): held = lax.all_to_all(message, BAND, 0, 0, tiled=True)  7.84 us
    all_to_all x1, starting transfers between devices, body(): held = lax.all_to_all(message, BAND, 0, 0, tiled=True)  6.61 us
    ppermute x3, starting transfers between devices, body(): lax.ppermute(across[d], BAND[0], [(i, i ^ d) for i in range(chips)])  3.95 us
    pallas_call x1, Pallas kernels, body(): call(open_kernel, (opened, jax.ShapeDtypeStruct((blocks + bands, LANES),...  3.56 us
    ppermute x3, waiting for transfers between devices, body(): lax.ppermute(across[d], BAND[0], [(i, i ^ d) for i in range(chips)])  3.11 us
    pallas_call x1, Pallas kernels, body(): call(fold_kernel, (f32(blocks, ROWS, LANES), part, part), [VMEM] * 3, 20...  1.39 us
  transfers between devices with their start and end apart: 6, of which 4 were waited for; matrix products, arithmetic and copies ran while one was open for 0% of the time, Pallas kernels for 1%

profile of v3, /device:TPU:1, one launch (start us, length us, event | category | flops | bytes accessed | tf_op | source)
XLA Modules:
  0.0 67.9 jit_solution(10893016492786296445)
XLA Ops:
  0.6 0.0 copy-start
  0.6 3.6 %shard_map.104 = (f32[8,24,512]{2,1,0:T(8,128)}, s32[40,128]{1,0:T(8,128)}) custom-call(s32[1,4096]{1,0:T(1,128)} %bitcast.20, f32[16,4096]{1,0:T(8,128)} %bitcast.14, s32[32]{0:T(128)} %refs_2_.1, s32[8]{0:T(128)} %refs_3_.1, f32[16,4096]{1,0:T(8,128)} %refs_4_.3, f32[1,4096]{1,0:T(1,128)} %refs_5_.3, f32[1,4096]{1,0:T(1,128)} %refs_6_.3, ...), custom_call_target="tpu_custom_call" | custom-call | flops 5242880 | bytes 2097152 | tf_op jit(solution)/shard_map/pallas_call | solution.py:409
  4.2 6.6 %all-to-all-start = ((f32[8,24,512]{2,1,0:T(8,128)}), f32[8,24,512]{2,1,0:T(8,128)S(1)}, u32[]{:S(2)}, u32[]{:S(2)}) async-start(f32[8,24,512]{2,1,0:T(8,128)} %get-tuple-element.17), calls=%async_computation | async-start | bytes 786432 | tf_op jit(solution)/shard_map/all_to_all | solution.py:420
  10.8 0.0 copy-done
  10.8 0.0 copy-start.2
  10.8 0.0 copy-start.4
  10.8 0.2 shard_map.105.refs_9_
  11.1 7.8 %all-to-all-done.held = f32[8,24,512]{2,1,0:T(8,128)S(1)} async-done(((f32[8,24,512]{2,1,0:T(8,128)}), f32[8,24,512]{2,1,0:T(8,128)S(1)}, u32[]{:S(2)}, u32[]{:S(2)}) %all-to-all-start) | async-done | bytes 393248 | tf_op jit(solution)/shard_map/all_to_all | solution.py:420
  18.9 0.0 copy-done.2
  18.9 0.0 copy-done.4
  18.9 1.4 %shard_map.106 = (f32[32,8,128]{2,1,0:T(8,128)}, f32[4,16,512]{2,1,0:T(8,128)S(1)}, f32[4,16,512]{2,1,0:T(8,128)S(1)}) custom-call(s32[40,128]{1,0:T(8,128)S(1)} %copy-done.4, f32[8,24,512]{2,1,0:T(8,128)S(1)} %all-to-all-done.held, f32[16,4096]{1,0:T(8,128)S(1)} %copy-done.2), custom_call_target="tpu_custom_call" | custom-call | flops 5242880 | bytes 1310720 | tf_op jit(solution)/shard_map/pallas_call | solution.py:425
  20.3 10.4 %all-to-all-start.1 = ((f32[32,8,128]{2,1,0:T(8,128)}), f32[32,8,128]{2,1,0:T(8,128)S(1)}, u32[]{:S(2)}, u32[]{:S(2)}) async-start(f32[32,8,128]{2,1,0:T(8,128)} %get-tuple-element.19), calls=%async_computation.1 | async-start | bytes 262144 | tf_op jit(solution)/shard_map/all_to_all | solution.py:434
  30.7 1.2 %collective-permute-start = (f32[4,16,512]{2,1,0:T(8,128)S(1)}, f32[4,16,512]{2,1,0:T(8,128)S(1)}, u32[]{:S(2)}, u32[]{:S(2)}) collective-permute-start(f32[4,16,512]{2,1,0:T(8,128)S(1)} %get-tuple-element.23), channel_id=1, source_target_pairs={{0,32},{32,0},{1,33},{33,1},{2,34},{34,2},{3,35},{35,3},{4,36},{36... | collective-permute-start | bytes 393224 | tf_op jit(solution)/shard_map/ppermute | solution.py:435
  32.0 1.0 %collective-permute-done = f32[4,16,512]{2,1,0:T(8,128)S(1)} collective-permute-done((f32[4,16,512]{2,1,0:T(8,128)S(1)}, f32[4,16,512]{2,1,0:T(8,128)S(1)}, u32[]{:S(2)}, u32[]{:S(2)}) %collective-permute-start) | collective-permute-done | bytes 131104 | tf_op jit(solution)/shard_map/ppermute | solution.py:435
  33.0 0.0 copy-start.1
  33.0 0.4 collective-permute-start.1
  33.4 1.8 %collective-permute-start.2 = (f32[2,16,512]{2,1,0:T(8,128)S(1)}, f32[2,16,512]{2,1,0:T(8,128)S(1)}, u32[]{:S(2)}, u32[]{:S(2)}) collective-permute-start(f32[2,16,512]{2,1,0:T(8,128)S(1)} %pad_maximum_fusion.2), channel_id=1, source_target_pairs={{0,128},{64,192},{128,0},{192,64},{1,129},{65,193},{129,1},{193,65... | collective-permute-start | bytes 196616 | tf_op jit(solution)/shard_map/ppermute | solution.py:438
  35.2 1.8 %collective-permute-start.3 = (f32[2,16,512]{2,1,0:T(8,128)S(1)}, f32[2,16,512]{2,1,0:T(8,128)S(1)}, u32[]{:S(2)}, u32[]{:S(2)}) collective-permute-start(f32[2,16,512]{2,1,0:T(8,128)S(1)} %pad_maximum_fusion.3), channel_id=1, source_target_pairs={{0,192},{64,128},{128,64},{192,0},{1,193},{65,129},{129,65},{193,1... | collective-permute-start | bytes 196616 | tf_op jit(solution)/shard_map/ppermute | solution.py:438
  37.0 0.0 copy-start.5
  37.0 0.0 copy-start.6
  37.0 0.0 copy-start.3
  37.0 0.0 collective-permute-done.1.refs_1_
  37.0 1.6 %collective-permute-done.2.refs_2_ = f32[2,16,512]{2,1,0:T(8,128)S(1)} collective-permute-done((f32[2,16,512]{2,1,0:T(8,128)S(1)}, f32[2,16,512]{2,1,0:T(8,128)S(1)}, u32[]{:S(2)}, u32[]{:S(2)}) %collective-permute-start.2) | collective-permute-done | bytes 65568 | tf_op jit(solution)/shard_map/ppermute | solution.py:438
  38.6 1.5 %collective-permute-done.3.refs_3_ = f32[2,16,512]{2,1,0:T(8,128)S(1)} collective-permute-done((f32[2,16,512]{2,1,0:T(8,128)S(1)}, f32[2,16,512]{2,1,0:T(8,128)S(1)}, u32[]{:S(2)}, u32[]{:S(2)}) %collective-permute-start.3) | collective-permute-done | bytes 65568 | tf_op jit(solution)/shard_map/ppermute | solution.py:438
  40.1 0.0 copy-done.1
  40.1 0.0 copy-done.5
  40.1 0.0 copy-done.6
  40.1 0.6 shard_map.108
  40.7 0.0 all-to-all-done.1.sums
  40.7 0.1 shard_map.107
  40.8 0.1 shard_map.109
  40.9 25.8 %all_to_all.21 = f32[256,1,128]{2,1,0:T(1,128)S(1)} all-to-all(f32[256,1,128]{2,1,0:T(1,128)S(1)} %bitcast.19), channel_id=1, replica_groups=mesh['band_0'=4,'band_1'=2,'pos_0'=4,'pos_1'=8] {'band_0','band_1','pos_..., dimensions={0} | all-to-all | bytes 262144 | tf_op jit(solution)/shard_map/all_to_all | solution.py:457
  66.7 0.0 copy-done.3
  66.7 1.1 %shard_map.110 = (f32[16,4096]{1,0:T(8,128)}, f32[16,4096]{1,0:T(8,128)}) custom-call(f32[256,128]{1,0:T(8,128)S(1)} %bitcast.18, f32[8,16,512]{2,1,0:T(8,128)S(1)} %get-tuple-element.26.refs_0_, f32[8,16,512]{2,1,0:T(8,128)S(1)} %get-tuple-element.27.refs_1_, f32[16,4096]{1,0:T(8,128)S(1)} %bitcast.16, f32[4,16,4096]{2,1,0:T(8,128)S(1)} %bitcast.17, ...), custom_call_target="tpu_custom_call" | custom-call | flops 2097152 | bytes 3670016 | tf_op jit(solution)/shard_map/pallas_call | solution.py:458
  (6 shorter events, 0.0 us)
Async XLA Ops:
  0.6 10.2 %copy-start = (f32[4,1,16,4096]{3,2,1,0:T(8,128)S(1)}, f32[4,1,16,4096]{3,2,1,0:T(8,128)}, u32[]{:S(2)}) copy-start(f32[4,1,16,4096]{3,2,1,0:T(8,128)} %param.11) | copy-start | bytes 3145732
  4.2 14.7 %all-to-all-start = ((f32[8,24,512]{2,1,0:T(8,128)}), f32[8,24,512]{2,1,0:T(8,128)S(1)}, u32[]{:S(2)}, u32[]{:S(2)}) async-start(f32[8,24,512]{2,1,0:T(8,128)} %get-tuple-element.17), calls=%async_computation | async-start | bytes 786432 | tf_op jit(solution)/shard_map/all_to_all | solution.py:420
  10.8 8.1 %copy-start.2 = (f32[16,4096]{1,0:T(8,128)S(1)}, f32[16,4096]{1,0:T(8,128)}, u32[]{:S(2)}) copy-start(f32[16,4096]{1,0:T(8,128)} %refs_4_.3) | copy-start | bytes 786436
  10.8 8.1 %copy-start.4 = (s32[40,128]{1,0:T(8,128)S(1)}, s32[40,128]{1,0:T(8,128)}, u32[]{:S(2)}) copy-start(s32[40,128]{1,0:T(8,128)} %get-tuple-element.16.notes) | copy-start | bytes 61444
  20.3 20.3 %all-to-all-start.1 = ((f32[32,8,128]{2,1,0:T(8,128)}), f32[32,8,128]{2,1,0:T(8,128)S(1)}, u32[]{:S(2)}, u32[]{:S(2)}) async-start(f32[32,8,128]{2,1,0:T(8,128)} %get-tuple-element.19), calls=%async_computation.1 | async-start | bytes 262144 | tf_op jit(solution)/shard_map/all_to_all | solution.py:434
  30.7 2.2 %collective-permute-start = (f32[4,16,512]{2,1,0:T(8,128)S(1)}, f32[4,16,512]{2,1,0:T(8,128)S(1)}, u32[]{:S(2)}, u32[]{:S(2)}) collective-permute-start(f32[4,16,512]{2,1,0:T(8,128)S(1)} %get-tuple-element.23), channel_id=1, source_target_pairs={{0,32},{32,0},{1,33},{33,1},{2,34},{34,2},{3,35},{35,3},{4,36},{36... | collective-permute-start | bytes 393224 | tf_op jit(solution)/shard_map/ppermute | solution.py:435
  33.0 7.1 %copy-start.1 = (f32[1,16,4096]{2,1,0:T(8,128)S(1)}, f32[1,16,4096]{2,1,0:T(8,128)}, u32[]{:S(2)}) copy-start(f32[1,16,4096]{2,1,0:T(8,128)} %param.9) | copy-start | bytes 786436
  33.0 4.0 %collective-permute-start.1 = (f32[2,16,512]{2,1,0:T(8,128)S(1)}, f32[2,16,512]{2,1,0:T(8,128)S(1)}, u32[]{:S(2)}, u32[]{:S(2)}) collective-permute-start(f32[2,16,512]{2,1,0:T(8,128)S(1)} %pad_maximum_fusion.1), channel_id=1, source_target_pairs={{0,64},{64,0},{128,192},{192,128},{1,65},{65,1},{129,193},{193,129... | collective-permute-start | bytes 196616 | tf_op jit(solution)/shard_map/ppermute | solution.py:438
  33.4 5.2 %collective-permute-start.2 = (f32[2,16,512]{2,1,0:T(8,128)S(1)}, f32[2,16,512]{2,1,0:T(8,128)S(1)}, u32[]{:S(2)}, u32[]{:S(2)}) collective-permute-start(f32[2,16,512]{2,1,0:T(8,128)S(1)} %pad_maximum_fusion.2), channel_id=1, source_target_pairs={{0,128},{64,192},{128,0},{192,64},{1,129},{65,193},{129,1},{193,65... | collective-permute-start | bytes 196616 | tf_op jit(solution)/shard_map/ppermute | solution.py:438
  35.2 4.9 %collective-permute-start.3 = (f32[2,16,512]{2,1,0:T(8,128)S(1)}, f32[2,16,512]{2,1,0:T(8,128)S(1)}, u32[]{:S(2)}, u32[]{:S(2)}) collective-permute-start(f32[2,16,512]{2,1,0:T(8,128)S(1)} %pad_maximum_fusion.3), channel_id=1, source_target_pairs={{0,192},{64,128},{128,64},{192,0},{1,193},{65,129},{129,65},{193,1... | collective-permute-start | bytes 196616 | tf_op jit(solution)/shard_map/ppermute | solution.py:438
  37.0 3.1 %copy-start.5 = (f32[1,4096]{1,0:T(1,128)S(1)}, f32[1,4096]{1,0:T(1,128)}, u32[]{:S(2)}) copy-start(f32[1,4096]{1,0:T(1,128)} %refs_5_.3) | copy-start | bytes 49156
  37.0 3.1 %copy-start.6 = (f32[1,4096]{1,0:T(1,128)S(1)}, f32[1,4096]{1,0:T(1,128)}, u32[]{:S(2)}) copy-start(f32[1,4096]{1,0:T(1,128)} %refs_6_.3) | copy-start | bytes 49156
  37.0 29.8 %copy-start.3 = (f32[4,1,16,4096]{3,2,1,0:T(8,128)S(1)}, f32[4,1,16,4096]{3,2,1,0:T(8,128)}, u32[]{:S(2)}) copy-start(f32[4,1,16,4096]{3,2,1,0:T(8,128)} %param.10) | copy-start | bytes 3145732

commit v4 on v3

--- a/solution.py
+++ b/solution.py
@@ -77,12 +77,6 @@
     return a, b, ends
 
 
-def coefficients(velocity, out_rate, kb, h):
-    v = velocity[h * ROWS : (h + 1) * ROWS, tile(kb)]
-    r = jnp.broadcast_to(out_rate[:, tile(kb)], (ROWS, LANES))
-    return v, r, 1.0 / (v + r)
-
-
 def flag(notes, index):
     return jnp.broadcast_to(notes[pl.ds(index, 1), :], (ROWS, LANES)) == 1
 
@@ -109,57 +103,60 @@
     return parts[0]
 
 
+def columns_of(kb):
+    return pl.ds(pl.multiple_of(kb * LANES, LANES), LANES)
+
+
 def open_kernel(*refs):
-    sources, message, notes, held, ready, arrived, gone = refs[:8], refs[8], refs[9], refs[10:18], *refs[18:]
-    copies = [pltpu.make_async_copy(a, b, arrived.at[n]) for n, (a, b) in enumerate(zip(sources, held))]
+    sources, own, other, notes, held, arrived = refs[:8], refs[8], refs[9], refs[10], refs[11:19], refs[19]
+    offsets, padded, directions, coupling, velocity, out_rate, inflow, past_residuals = held
+    moments = offsets.shape[1]
+    tiles = moments // LANES
+    chips, _, share = own.shape
+    per = share // LANES
+    places = [padded.at[:, pl.ds(LANES, moments)] if ref is padded else ref for ref in held]
+    copies = [pltpu.make_async_copy(a, b, arrived.at[n]) for n, (a, b) in enumerate(zip(sources, places))]
     for copy in copies:
         copy.start()
-    offsets, wigner, directions, coupling, velocity, out_rate, inflow, past_residuals = held
-    tiles = wigner.shape[1] // LANES
-    per = message.shape[2] // LANES
+    band = lax.axis_index(BAND)
     row, lane = iota(0), iota(1)
-    zero = jnp.zeros((ROWS, LANES), jnp.float32)
+    for kb in (0, tiles + 1):
+        padded[:, tile(kb)] = jnp.zeros((2 * ROWS, LANES), jnp.float32)
+    spots = [
+        (target, d, t, (band ^ (2 * d + core)) * per + t)
+        for core, target in ((1, other), (0, own))
+        for d in range(chips)
+        for t in range(per)
+    ]
     copies[0].wait()
     copies[1].wait()
-    for kb in range(tiles):
-        off = jnp.broadcast_to(offsets[:, tile(kb)], (ROWS, LANES))
-        up, below_at = lane + off, lane - off
-        up_in, down_in = up & (LANES - 1), below_at & (LANES - 1)
+    for target, d, t, kb in spots:
+        off = jnp.broadcast_to(offsets[:, columns_of(kb)], (ROWS, LANES))
+        up, low = lane + off, lane - off
+        up_in, low_in = up & (LANES - 1), low & (LANES - 1)
         for h in range(2):
-            here = wigner[half(h), tile(kb)]
-            nxt = pick(wigner[half(h), tile(kb + 1)], up_in, 1) if kb + 1 < tiles else zero
-            prv = pick(wigner[half(h), tile(kb - 1)], down_in, 1) if kb else zero
-            above = jnp.where(up < LANES, pick(here, up_in, 1), nxt)
-            below = jnp.where(below_at >= 0, pick(here, down_in, 1), prv)
-            ready[kb // per, half(h), tile(kb % per)] = 0.5 * (above + below)
+            prv, here, nxt = [padded[half(h), columns_of(kb + n)] for n in range(3)]
+            above = jnp.where(up < LANES, pick(here, up_in, 1), pick(nxt, up_in, 1))
+            below = jnp.where(low >= 0, pick(here, low_in, 1), pick(prv, low_in, 1))
+            target[d, half(h), tile(t)] = 0.5 * (above + below)
     for copy in copies[2:]:
         copy.wait()
-    out = [pltpu.make_async_copy(ready.at[b], message.at[b], gone.at[b]) for b in range(message.shape[0])]
-    for kb in range(tiles):
+    for target, d, t, kb in spots:
         back = jnp.full((ROWS, LANES), directions[kb], jnp.int32) == 1
-        slope = []
-        for h in range(2):
-            v, _, inv = coefficients(velocity, out_rate, kb, h)
-            slope.append(v * inv)
-        reach, _, _ = scan_tile(back, slope, None)
-        parts = [sum(past_residuals[j, half(h), tile(kb)] * reach[h] for h in range(2)) for j in range(HIST)]
+        rate = jnp.broadcast_to(out_rate[:, columns_of(kb)], (ROWS, LANES))
+        enters = jnp.broadcast_to(inflow[:, columns_of(kb)], (ROWS, LANES))
+        speeds = [velocity[half(h), columns_of(kb)] for h in range(2)]
+        reach, _, _ = scan_tile(back, [v * (1.0 / (v + rate)) for v in speeds], None)
+        parts = [sum(past_residuals[j, half(h), columns_of(kb)] * reach[h] for h in range(2)) for j in range(HIST)]
         parts.append(sum(reach[h] * reach[h] for h in range(2)))
-        parts.append(sum(reach[h] * wigner[half(h), tile(kb)] for h in range(2)))
-        rate = jnp.broadcast_to(out_rate[:, tile(kb)], (ROWS, LANES))
-        enters = jnp.broadcast_to(inflow[:, tile(kb)], (ROWS, LANES))
-        ready[kb // per, 2 * ROWS :, tile(kb % per)] = jnp.where(
-            row == 6, rate, jnp.where(row == 7, enters, added_rows(parts))
-        )
-        if kb % per == per - 1:
-            out[kb // per].start()
+        parts.append(sum(reach[h] * padded[half(h), columns_of(kb + 1)] for h in range(2)))
+        target[d, 2 * ROWS :, tile(t)] = jnp.where(row == 6, rate, jnp.where(row == 7, enters, added_rows(parts)))
     known = [directions[n] for n in range(tiles)] + [coupling[n] for n in range(coupling.shape[0])]
     for q in range(len(known) // ROWS):
         rows = jnp.zeros((ROWS, LANES), jnp.int32)
         for n in range(ROWS):
             rows = jnp.where(row == n, known[q * ROWS + n], rows)
         notes[half(q), :] = rows
-    for copy in out:
-        copy.wait()
 
 
 def history_kernel(past_residuals, gram):
@@ -184,15 +181,19 @@
     return [jnp.where(first, slope[0] * wide, 0.0), jnp.where(final, slope[1] * wide, 0.0)]
 
 
-def fold_kernel(notes, held, velocity, message, *refs):
-    bands = held.shape[0]
-    own, other, both, ready, gone = refs
+def fold_kernel(notes, velocity, *refs):
+    chips = (len(refs) - 4) // 2
+    held, message, own, other, across = refs[:chips], *refs[chips : chips + 3], refs[chips + 3 : -2]
+    ready, gone = refs[-2:]
+    bands = 2 * chips
     blocks = message.shape[0]
-    per = held.shape[2] // LANES
+    per = own.shape[1] // LANES
     row, lane = iota(0), iota(1)
     band = lax.axis_index(BAND)
-    first = blocks
-    chosen = [jnp.broadcast_to(notes[first + s : first + s + 1, :], (ROWS, LANES)) for s in range(bands)]
+    chosen = [
+        jnp.broadcast_to(notes[pl.ds(blocks + (band ^ u), 1), :], (ROWS, LANES)) ^ jnp.full((ROWS, LANES), band, jnp.int32)
+        for u in range(bands)
+    ]
     out = [
         pltpu.make_async_copy(
             ready.at[pl.ds(kt * bands, bands)], message.at[pl.ds(kt * bands, bands)], gone.at[kt]
@@ -202,20 +203,22 @@
     for kt in range(per):
         kb = band * per + kt
         back = flag(notes, kb)
-        columns = pl.ds(pl.multiple_of(kb * LANES, LANES), LANES)
-        speeds = [velocity[half(h), columns] for h in range(2)]
-        spread = [[held[s, half(h), tile(kt)] for h in range(2)] for s in range(bands)]
+        speeds = [velocity[half(h), columns_of(kb)] for h in range(2)]
+        spread = [[held[u // 2][u % 2, half(h), tile(kt)] for h in range(2)] for u in range(bands)]
         parts = []
-        for s in range(bands):
-            tail = held[s, 2 * ROWS :, tile(kt)]
+        for u in range(bands):
+            tail = held[u // 2][u % 2, 2 * ROWS :, tile(kt)]
             rate = jnp.broadcast_to(tail[6:7], (ROWS, LANES))
             slope, offset = [], []
             for h in range(2):
                 partner = spread[0][h]
                 for t in range(1, bands):
-                    partner = jnp.where(chosen[s] == t, spread[t][h], partner)
-                pair = spread[s][h] + partner
-                both[s, half(h), tile(kt)] = pair
+                    partner = jnp.where(chosen[u] == t, spread[t][h], partner)
+                pair = spread[u][h] + partner
+                if u < 2:
+                    (other if u else own)[half(h), tile(kt)] = pair
+                else:
+                    across[u // 2 - 1][u % 2, half(h), tile(kt)] = pair
                 inv = 1.0 / (speeds[h] + rate)
                 slope.append(speeds[h] * inv)
                 offset.append(rate * 0.5 * pair * inv)
@@ -230,31 +233,30 @@
             step = 1 << bit
             high = ((lane >> (4 + bit)) & 1) == 1
             swapped = list(parts)
-            for s in range(bands):
-                if not s & step:
-                    swapped[s] = jnp.where(high, pltpu.roll(parts[s + step], GROUP * step, 1), parts[s])
-                    swapped[s + step] = jnp.where(high, parts[s + step], pltpu.roll(parts[s], LANES - GROUP * step, 1))
+            for u in range(bands):
+                if not u & step:
+                    swapped[u] = jnp.where(high, pltpu.roll(parts[u + step], GROUP * step, 1), parts[u])
+                    swapped[u + step] = jnp.where(high, parts[u + step], pltpu.roll(parts[u], LANES - GROUP * step, 1))
             parts = swapped
         for g in range(bands):
             ready[kt * bands + g] = parts[g]
         out[kt].start()
-    for d in range(bands // 2):
-        own[d] = both[band ^ (2 * d)]
-        other[d] = both[band ^ (2 * d + 1)]
     for copy in out:
         copy.wait()
 
 
-def settle_kernel(notes, *refs):
+def settle_kernel(flip, notes, *refs):
     shares = refs[:-9]
     velocity, out_rate, inflow, wigner, past_residuals, early, reach_out, rest, gram = refs[-9:]
+    shares = shares if len(shares) > 1 else [shares[0].at[d] for d in range(shares[0].shape[0])]
+    shares = [share if len(share.shape) == 2 else share.at[0] for share in shares]
     per = rest.shape[2] // LANES
     blocks = velocity.shape[1] // LANES
     band = lax.axis_index(BAND)
     acc = [jnp.zeros((ROWS, LANES), jnp.float32) for _ in range(HIST + 1)]
-    for d in range(2 * len(shares)):
+    for d in range(len(shares)):
         for kt in range(per):
-            kb = (band ^ d) * per + kt
+            kb = (band ^ (2 * d + flip)) * per + kt
             back = flag(notes, kb)
             columns = pl.ds(pl.multiple_of(kb * LANES, LANES), LANES)
             rate = jnp.broadcast_to(out_rate[:, columns], (ROWS, LANES))
@@ -263,7 +265,7 @@
                 v = velocity[half(h), columns]
                 inv = 1.0 / (v + rate)
                 slope.append(v * inv)
-                offset.append(rate * 0.5 * shares[d // 2][d % 2, half(h), tile(kt)] * inv)
+                offset.append(rate * 0.5 * shares[d][half(h), tile(kt)] * inv)
             edge = at_contact(blocks, back, slope, inflow[:, columns])
             offset = [offset[h] + edge[h] for h in range(2)]
             reach, run, _ = scan_tile(back, slope, offset)
@@ -305,10 +307,12 @@
         total = jnp.broadcast_to(jnp.sum(whole[h], axis=1, keepdims=True), (ROWS, LANES))
         line = line + jnp.where(lane == GROUP + h * ROWS + row, total, 0.0)
     line = jnp.broadcast_to(down(line), (ROWS, LANES))
+    band = lax.axis_index(BAND)
     for q in range(blocks // ROWS):
-        for s in range(LANES // GROUP):
-            turned = pltpu.roll(carries[half(q), :], LANES - GROUP * s, 1) if s else carries[half(q), :]
-            message[s * blocks + q * ROWS : s * blocks + (q + 1) * ROWS, :] = jnp.where(lane < GROUP, turned, line)
+        for u in range(LANES // GROUP):
+            turned = pltpu.roll(carries[half(q), :], LANES - GROUP * u, 1) if u else carries[half(q), :]
+            start = pl.multiple_of((band ^ u) * blocks + q * ROWS, ROWS)
+            message[pl.ds(start, ROWS), :] = jnp.where(lane < GROUP, turned, line)
 
 
 def mixing_weights(entry):
@@ -340,9 +344,10 @@
 
 
 def finish_kernel(message, *refs):
-    reach, rest, wigner, past_iterates, past_residuals, residual, mixed, found, mixes, gone = refs
+    reach, rest = (refs[0], refs[2]), (refs[1], refs[3])
+    wigner, past_iterates, past_residuals, residual, mixed, found, mixes, gone = refs[4:]
     cells, moments = wigner.shape
-    bands, _, share = rest.shape
+    chips, _, share = rest[0].shape
     per = share // LANES
     band = lax.axis_index(BAND)
     tiles = moments // LANES
@@ -366,15 +371,15 @@
             return term(4) + term(5) if i == HIST else term(i)
         return term(6 + PAIRS.index((i, j)))
 
-    for d in range(bands):
+    for d in range(2 * chips):
         for kt in range(per):
             kb = (band ^ d) * per + kt
             rows = message[pl.ds(pl.multiple_of(kb * ROWS, ROWS), ROWS), :]
             spots = pick(rows, lane & (GROUP - 1), 1)
             carry = jnp.broadcast_to(down(jnp.where((lane >> 4) == row, spots, 0.0)), (ROWS, LANES))
             for h in range(2):
-                at = (d, half(h), tile(kt))
-                found[half(h), pl.ds(pl.multiple_of(kb * LANES, LANES), LANES)] = rest[at] + reach[at] * carry
+                at = (d // 2, half(h), tile(kt))
+                found[half(h), pl.ds(pl.multiple_of(kb * LANES, LANES), LANES)] = rest[d % 2][at] + reach[d % 2][at] * carry
     for copy in out[:pieces]:
         copy.start()
     weights = mixing_weights(entry)
@@ -404,47 +409,61 @@
     field = f32(cells, moments)
     dma = pltpu.SemaphoreType.DMA
 
+    chips = lax.axis_size(BAND[0])
+
+    def to_core(x):
+        return lax.ppermute(x, BAND[1], [(0, 1), (1, 0)])
+
+    def to_chip(x, d):
+        return lax.ppermute(x, BAND[0], [(i, i ^ d) for i in range(chips)])
+
     sources = (offsets, wigner, directions, coupling, velocity, out_rate, inflow, past_residuals)
-    opened = f32(bands, cells + ROWS, share)
-    message, notes = call(
+    opened = f32(chips, cells + ROWS, share)
+    own, other, notes = call(
         open_kernel,
-        (opened, jax.ShapeDtypeStruct((blocks + bands, LANES), jnp.int32)),
+        (opened, opened, jax.ShapeDtypeStruct((blocks + bands, LANES), jnp.int32)),
         [HBM] * 8,
         20 * size,
         8 * size,
-        [(pltpu.SMEM if x.ndim == 1 else pltpu.VMEM)(x.shape, x.dtype) for x in sources]
-        + [pltpu.VMEM(opened.shape, jnp.float32), dma((8,)), dma((bands,))],
-        60,
-        (HBM, VMEM),
-    )(*sources)
-    held = lax.all_to_all(message, BAND, 0, 0, tiled=True)
+        [
+            pltpu.SMEM(x.shape, x.dtype)
+            if x.ndim == 1
+            else pltpu.VMEM((cells, moments + 2 * LANES) if x is wigner else x.shape, x.dtype)
+            for x in sources
+        ]
+        + [dma((8,))],
+    )(*[pltpu.with_memory_space_constraint(x, pltpu.HBM) for x in sources])
+    other = to_core(other)
+    held = [jnp.stack([own[d], other[d]]) for d in range(chips)]
+    held = held[:1] + [to_chip(held[d], d) for d in range(1, chips)]
     early = call(history_kernel, f32(16, LANES), [VMEM], 8 * size, 4 * size)(past_residuals)
-    held, early = lax.optimization_barrier((held, early))
-    chips = lax.axis_size(BAND[0])
-    part = f32(chips, cells, share)
-    sums, own, other = call(
+    *held, early = lax.optimization_barrier((*held, early))
+    pair = f32(2, cells, share)
+    sums, own, other, *across = call(
         fold_kernel,
-        (f32(blocks, ROWS, LANES), part, part),
-        [VMEM] * 3,
+        (f32(blocks, ROWS, LANES), f32(cells, share), f32(cells, share)) + (pair,) * (chips - 1),
+        [VMEM] * (chips + 2),
         20 * size,
         5 * size,
-        [pltpu.VMEM((bands, cells, share), jnp.float32), pltpu.VMEM((blocks, ROWS, LANES), jnp.float32), dma((4,))],
-        out_specs=(HBM, VMEM, VMEM),
-    )(notes, held, velocity)
+        [pltpu.VMEM((blocks, ROWS, LANES), jnp.float32), dma((4,))],
+        out_specs=(HBM,) + (VMEM,) * (chips + 1),
+    )(notes, velocity, *held)
     sums = lax.all_to_all(sums, POS, 0, 0, tiled=True)
-    other = lax.ppermute(other, BAND[1], [(0, 1), (1, 0)])
-    across = [jnp.stack([own[d], other[d]]) for d in range(chips)]
-    across = across[:1] + [
-        lax.ppermute(across[d], BAND[0], [(i, i ^ d) for i in range(chips)]) for d in range(1, chips)
-    ]
+    across = [to_chip(across[d - 1], d) for d in range(1, chips)]
+    other = to_core(jnp.stack([other] + [x[1] for x in across]))
     local = (velocity, out_rate, inflow, wigner, past_residuals)
-    reach, rest, gram = call(
-        settle_kernel,
-        (f32(bands, cells, share), f32(bands, cells, share), f32(16, LANES)),
-        [VMEM] * (chips + 7),
-        size,
-        size,
-    )(notes, *across, *local, early)
+    part = f32(chips, cells, share)
+    settled = []
+    gram = early
+    for flip, shares in enumerate(((own, *across), (other,))):
+        reach, rest, gram = call(
+            functools.partial(settle_kernel, flip),
+            (part, part, f32(16, LANES)),
+            [VMEM] * (len(shares) + 7),
+            size // 64,
+            size // 64,
+        )(notes, *shares, *local, gram)
+        settled += [reach, rest]
     carries, terms = call(
         carry_kernel,
         (f32(blocks, LANES), f32(ROWS, LANES)),
@@ -458,12 +477,12 @@
     residual, mixed = call(
         finish_kernel,
         (field, field),
-        [VMEM] * 6,
+        [VMEM] * 8,
         8 * size,
         14 * size,
         [pltpu.VMEM((cells, moments), jnp.float32)] * 2 + [dma((8,))],
         out_specs=(HBM, HBM),
-    )(message, reach, rest, wigner, past_iterates, past_residuals)
+    )(message, *settled, wigner, past_iterates, past_residuals)
     return mixed[None], residual[None]
 
 

time: 68.1 us -> 64.9 us (0.953)
  blocking collectives: 25.8 us -> 20.8 us
  starting transfers between devices: 22.2 us -> 24.3 us
  Pallas kernels: 7.08 us -> 5.77 us
  waiting for transfers between devices: 11.9 us -> 12.8 us
    ppermute x4 -> x8, starting transfers between devices: 5.18 us -> 13.1 us  [the longest x6 8.03 us: to_chip(): return lax.ppermute(x, BAND[0], [(i, i ^ d) for i in range(chips)])]
    all_to_all x1 -> x0, waiting for transfers between devices: 7.84 us -> none  [body(): held = lax.all_to_all(message, BAND, 0, 0, tiled=True)]
    all_to_all x1 -> x0, starting transfers between devices: 6.61 us -> none  [body(): held = lax.all_to_all(message, BAND, 0, 0, tiled=True)]
    all_to_all x1, waiting for transfers between devices: 0.01 us -> 6.05 us  [body(): sums = lax.all_to_all(sums, POS, 0, 0, tiled=True)]
    all_to_all x1, blocking collectives: 25.8 us -> 20.8 us  [body(): message = lax.all_to_all(message, ALL, 0, 0, tiled=True)]
    ppermute x4 -> x8, waiting for transfers between devices: 4.08 us -> 6.79 us  [the longest x6 5.29 us: to_chip(): return lax.ppermute(x, BAND[0], [(i, i ^ d) for i in range(chips)])]
    pallas_call x4 -> x5, Pallas kernels: 6.64 us -> 5.35 us  [the longest x1 2.3 us: body(): call(open_kernel, (opened, opened, jax.ShapeDtypeStruct((blocks + bands,...]
    all_to_all x1, starting transfers between devices: 10.4 us -> 11.2 us  [body(): sums = lax.all_to_all(sums, POS, 0, 0, tiled=True)]
  transfers between devices with their start and end apart: 6 -> 9, of which waited for: 4 -> 5; matrix products, arithmetic and copies ran while one was open for 0% -> 0% of each run, Pallas kernels for 1% -> 1%
where the time goes in v4:
time: 64.9 us; the launch traced here: 64.7 us
  starting transfers between devices  24.3 us (37%)
  blocking collectives  20.8 us (32%)
  waiting for transfers between devices  12.8 us (20%)
  Pallas kernels  5.77 us (9%)
  between operations  0.82 us (1%)
    all_to_all x1, blocking collectives, body(): message = lax.all_to_all(message, ALL, 0, 0, tiled=True)  20.8 us
    all_to_all x1, starting transfers between devices, body(): sums = lax.all_to_all(sums, POS, 0, 0, tiled=True)  11.2 us
    ppermute x6, starting transfers between devices, to_chip(): return lax.ppermute(x, BAND[0], [(i, i ^ d) for i in range(chips)])  8.03 us
    all_to_all x1, waiting for transfers between devices, body(): sums = lax.all_to_all(sums, POS, 0, 0, tiled=True)  6.05 us
    ppermute x6, waiting for transfers between devices, to_chip(): return lax.ppermute(x, BAND[0], [(i, i ^ d) for i in range(chips)])  5.29 us
    ppermute x2, starting transfers between devices, to_core(): return lax.ppermute(x, BAND[1], [(0, 1), (1, 0)])  5.05 us
    pallas_call x1, Pallas kernels, body(): call(open_kernel, (opened, opened, jax.ShapeDtypeStruct((blocks + bands,...  2.3 us
    ppermute x2, waiting for transfers between devices, to_core(): return lax.ppermute(x, BAND[1], [(0, 1), (1, 0)])  1.5 us
  transfers between devices with their start and end apart: 9, of which 5 were waited for; matrix products, arithmetic and copies ran while one was open for 0% of the time, Pallas kernels for 1%

profile of v4, /device:TPU:1, one launch (start us, length us, event | category | flops | bytes accessed | tf_op | source)
XLA Modules:
  0.0 64.7 jit_solution(11264884823854933485)
XLA Ops:
  0.6 0.0 copy-start
  0.6 2.3 %shard_map.104 = (f32[4,24,512]{2,1,0:T(8,128)S(1)}, f32[4,24,512]{2,1,0:T(8,128)S(1)}, s32[40,128]{1,0:T(8,128)S(1)}) custom-call(s32[1,4096]{1,0:T(1,128)} %bitcast.24, f32[16,4096]{1,0:T(8,128)} %bitcast.16, s32[32]{0:T(128)} %refs_2_.2, s32[8]{0:T(128)} %refs_3_.2, f32[16,4096]{1,0:T(8,128)} %refs_1_.1, f32[1,4096]{1,0:T(1,128)} %refs_2_.3, ...), custom_call_target="tpu_custom_call" | custom-call | flops 5242880 | bytes 2097152 | tf_op jit(solution)/shard_map/pallas_call | solution.py:422
  2.9 3.3 %collective-permute-start = (f32[4,24,512]{2,1,0:T(8,128)S(1)}, f32[4,24,512]{2,1,0:T(8,128)S(1)}, u32[]{:S(2)}, u32[]{:S(2)}) collective-permute-start(f32[4,24,512]{2,1,0:T(8,128)S(1)} %get-tuple-element.28), channel_id=1, source_target_pairs={{0,32},{32,0},{1,33},{33,1},{2,34},{34,2},{3,35},{35,3},{4,36},{36... | collective-permute-start | bytes 589832 | tf_op jit(solution)/shard_map/ppermute | solution.py:415
  6.3 0.0 copy-done
  6.3 0.2 shard_map.105.refs_9_
  6.5 0.8 %collective-permute-done = f32[4,24,512]{2,1,0:T(8,128)S(1)} collective-permute-done((f32[4,24,512]{2,1,0:T(8,128)S(1)}, f32[4,24,512]{2,1,0:T(8,128)S(1)}, u32[]{:S(2)}, u32[]{:S(2)}) %collective-permute-start) | collective-permute-done | bytes 196640 | tf_op jit(solution)/shard_map/ppermute | solution.py:415
  7.4 0.1 collective-permute-start.1
  7.5 0.0 copy-start.2
  7.5 2.0 %collective-permute-start.2 = (f32[2,24,512]{2,1,0:T(8,128)S(1)}, f32[2,24,512]{2,1,0:T(8,128)S(1)}, u32[]{:S(2)}, u32[]{:S(2)}) collective-permute-start(f32[2,24,512]{2,1,0:T(8,128)S(1)} %pad_maximum_fusion.3), channel_id=1, source_target_pairs={{0,128},{64,192},{128,0},{192,64},{1,129},{65,193},{129,1},{193,65... | collective-permute-start | bytes 294920 | tf_op jit(solution)/shard_map/ppermute | solution.py:418
  9.5 2.0 %collective-permute-start.3 = (f32[2,24,512]{2,1,0:T(8,128)S(1)}, f32[2,24,512]{2,1,0:T(8,128)S(1)}, u32[]{:S(2)}, u32[]{:S(2)}) collective-permute-start(f32[2,24,512]{2,1,0:T(8,128)S(1)} %pad_maximum_fusion.4), channel_id=1, source_target_pairs={{0,192},{64,128},{128,64},{192,0},{1,193},{65,129},{129,65},{193,1... | collective-permute-start | bytes 294920 | tf_op jit(solution)/shard_map/ppermute | solution.py:418
  11.5 0.0 collective-permute-done.1.refs_1_
  11.5 2.5 %collective-permute-done.2.refs_2_ = f32[2,24,512]{2,1,0:T(8,128)S(1)} collective-permute-done((f32[2,24,512]{2,1,0:T(8,128)S(1)}, f32[2,24,512]{2,1,0:T(8,128)S(1)}, u32[]{:S(2)}, u32[]{:S(2)}) %collective-permute-start.2) | collective-permute-done | bytes 98336 | tf_op jit(solution)/shard_map/ppermute | solution.py:418
  14.0 2.8 %collective-permute-done.3.refs_3_ = f32[2,24,512]{2,1,0:T(8,128)S(1)} collective-permute-done((f32[2,24,512]{2,1,0:T(8,128)S(1)}, f32[2,24,512]{2,1,0:T(8,128)S(1)}, u32[]{:S(2)}, u32[]{:S(2)}) %collective-permute-start.3) | collective-permute-done | bytes 98336 | tf_op jit(solution)/shard_map/ppermute | solution.py:418
  16.8 0.0 copy-done.2
  16.8 1.4 %shard_map.106 = (f32[32,8,128]{2,1,0:T(8,128)}, f32[16,512]{1,0:T(8,128)S(1)}, f32[16,512]{1,0:T(8,128)S(1)}, f32[2,16,512]{2,1,0:T(8,128)S(1)}, f32[2,16,512]{2,1,0:T(8,128)S(1)}, /*index=5*/f32[2,16,512]{2,1,0:T(8,128)S(1)}) custom-call(s32[40,128]{1,0:T(8,128)S(1)} %get-tuple-element.26.notes, f32[16,4096]{1,0:T(8,128)S(1)} %copy-done.2, ...), custom_call_target="tpu_custom_call" | custom-call | flops 5242880 | bytes 1310720 | tf_op jit(solution)/shard_map/pallas_call | solution.py:442
  18.2 0.1 collective-permute-start.4
  18.3 3.1 %collective-permute-start.5 = (f32[2,16,512]{2,1,0:T(8,128)S(1)}, f32[2,16,512]{2,1,0:T(8,128)S(1)}, u32[]{:S(2)}, u32[]{:S(2)}) collective-permute-start(f32[2,16,512]{2,1,0:T(8,128)S(1)} %get-tuple-element.38), channel_id=1, source_target_pairs={{0,128},{64,192},{128,0},{192,64},{1,129},{65,193},{129,1},{193,65... | collective-permute-start | bytes 196616 | tf_op jit(solution)/shard_map/ppermute | solution.py:418
  21.4 0.7 %collective-permute-start.6 = (f32[2,16,512]{2,1,0:T(8,128)S(1)}, f32[2,16,512]{2,1,0:T(8,128)S(1)}, u32[]{:S(2)}, u32[]{:S(2)}) collective-permute-start(f32[2,16,512]{2,1,0:T(8,128)S(1)} %get-tuple-element.39), channel_id=1, source_target_pairs={{0,192},{64,128},{128,64},{192,0},{1,193},{65,129},{129,65},{193,1... | collective-permute-start | bytes 196616 | tf_op jit(solution)/shard_map/ppermute | solution.py:418
  22.2 11.2 %all-to-all-start = ((f32[32,8,128]{2,1,0:T(8,128)}), f32[32,8,128]{2,1,0:T(8,128)S(1)}, u32[]{:S(2)}, u32[]{:S(2)}) async-start(f32[32,8,128]{2,1,0:T(8,128)} %get-tuple-element.33), calls=%async_computation | async-start | bytes 262144 | tf_op jit(solution)/shard_map/all_to_all | solution.py:451
  33.4 0.0 copy-start.1
  33.4 0.0 collective-permute-done.4.refs_1_
  33.4 0.0 collective-permute-done.5.refs_2_
  33.4 0.0 collective-permute-done.6.refs_3_
  33.5 0.0 copy-start.4
  33.5 0.0 copy-start.5
  33.5 1.7 %collective-permute-start.7 = (f32[4,16,512]{2,1,0:T(8,128)S(1)}, f32[4,16,512]{2,1,0:T(8,128)S(1)}, u32[]{:S(2)}, u32[]{:S(2)}) collective-permute-start(f32[4,16,512]{2,1,0:T(8,128)S(1)} %pad_maximum_fusion), channel_id=1, source_target_pairs={{0,32},{32,0},{1,33},{33,1},{2,34},{34,2},{3,35},{35,3},{4,36},{36... | collective-permute-start | bytes 393224 | tf_op jit(solution)/shard_map/ppermute | solution.py:415
  35.2 0.0 copy-done.1
  35.2 0.0 copy-done.4
  35.2 0.0 copy-done.5
  35.2 0.3 shard_map.108
  35.5 0.7 %collective-permute-done.7.refs_0_ = f32[4,16,512]{2,1,0:T(8,128)S(1)} collective-permute-done((f32[4,16,512]{2,1,0:T(8,128)S(1)}, f32[4,16,512]{2,1,0:T(8,128)S(1)}, u32[]{:S(2)}, u32[]{:S(2)}) %collective-permute-start.7) | collective-permute-done | bytes 131104 | tf_op jit(solution)/shard_map/ppermute | solution.py:415
  36.2 0.0 copy-start.3
  36.2 0.3 shard_map.109
  36.5 6.1 %all-to-all-done.sums = f32[32,8,128]{2,1,0:T(8,128)S(1)} async-done(((f32[32,8,128]{2,1,0:T(8,128)}), f32[32,8,128]{2,1,0:T(8,128)S(1)}, u32[]{:S(2)}, u32[]{:S(2)}) %all-to-all-start) | async-done | bytes 131104 | tf_op jit(solution)/shard_map/all_to_all | solution.py:451
  42.6 0.1 shard_map.107
  42.6 0.1 shard_map.110
  42.7 20.8 %all_to_all.16 = f32[256,1,128]{2,1,0:T(1,128)S(1)} all-to-all(f32[256,1,128]{2,1,0:T(1,128)S(1)} %bitcast.22), channel_id=1, replica_groups=mesh['band_0'=4,'band_1'=2,'pos_0'=4,'pos_1'=8] {'band_0','band_1','pos_..., dimensions={0} | all-to-all | bytes 262144 | tf_op jit(solution)/shard_map/all_to_all | solution.py:476
  63.6 0.0 copy-done.3
  63.6 1.1 %shard_map.111 = (f32[16,4096]{1,0:T(8,128)}, f32[16,4096]{1,0:T(8,128)}) custom-call(f32[256,128]{1,0:T(8,128)S(1)} %bitcast.21, f32[4,16,512]{2,1,0:T(8,128)S(1)} %get-tuple-element.44.refs_0_, f32[4,16,512]{2,1,0:T(8,128)S(1)} %get-tuple-element.45.refs_1_, f32[4,16,512]{2,1,0:T(8,128)S(1)} %get-tuple-element.46.refs_2_, ...), custom_call_target="tpu_custom_call" | custom-call | flops 2097152 | bytes 3670016 | tf_op jit(solution)/shard_map/pallas_call | solution.py:477
  (10 shorter events, 0.1 us)
Async XLA Ops:
  0.6 5.6 %copy-start = (f32[4,1,16,4096]{3,2,1,0:T(8,128)S(1)}, f32[4,1,16,4096]{3,2,1,0:T(8,128)}, u32[]{:S(2)}) copy-start(f32[4,1,16,4096]{3,2,1,0:T(8,128)} %param.11) | copy-start | bytes 3145732
  2.9 4.4 %collective-permute-start = (f32[4,24,512]{2,1,0:T(8,128)S(1)}, f32[4,24,512]{2,1,0:T(8,128)S(1)}, u32[]{:S(2)}, u32[]{:S(2)}) collective-permute-start(f32[4,24,512]{2,1,0:T(8,128)S(1)} %get-tuple-element.28), channel_id=1, source_target_pairs={{0,32},{32,0},{1,33},{33,1},{2,34},{34,2},{3,35},{35,3},{4,36},{36... | collective-permute-start | bytes 589832 | tf_op jit(solution)/shard_map/ppermute | solution.py:415
  7.4 4.1 %collective-permute-start.1 = (f32[2,24,512]{2,1,0:T(8,128)S(1)}, f32[2,24,512]{2,1,0:T(8,128)S(1)}, u32[]{:S(2)}, u32[]{:S(2)}) collective-permute-start(f32[2,24,512]{2,1,0:T(8,128)S(1)} %pad_maximum_fusion.2), channel_id=1, source_target_pairs={{0,64},{64,0},{128,192},{192,128},{1,65},{65,1},{129,193},{193,129... | collective-permute-start | bytes 294920 | tf_op jit(solution)/shard_map/ppermute | solution.py:418
  7.5 9.3 %copy-start.2 = (f32[16,4096]{1,0:T(8,128)S(1)}, f32[16,4096]{1,0:T(8,128)}, u32[]{:S(2)}) copy-start(f32[16,4096]{1,0:T(8,128)} %refs_1_.1) | copy-start | bytes 786436
  7.5 6.5 %collective-permute-start.2 = (f32[2,24,512]{2,1,0:T(8,128)S(1)}, f32[2,24,512]{2,1,0:T(8,128)S(1)}, u32[]{:S(2)}, u32[]{:S(2)}) collective-permute-start(f32[2,24,512]{2,1,0:T(8,128)S(1)} %pad_maximum_fusion.3), channel_id=1, source_target_pairs={{0,128},{64,192},{128,0},{192,64},{1,129},{65,193},{129,1},{193,65... | collective-permute-start | bytes 294920 | tf_op jit(solution)/shard_map/ppermute | solution.py:418
  9.5 7.3 %collective-permute-start.3 = (f32[2,24,512]{2,1,0:T(8,128)S(1)}, f32[2,24,512]{2,1,0:T(8,128)S(1)}, u32[]{:S(2)}, u32[]{:S(2)}) collective-permute-start(f32[2,24,512]{2,1,0:T(8,128)S(1)} %pad_maximum_fusion.4), channel_id=1, source_target_pairs={{0,192},{64,128},{128,64},{192,0},{1,193},{65,129},{129,65},{193,1... | collective-permute-start | bytes 294920 | tf_op jit(solution)/shard_map/ppermute | solution.py:418
  18.2 15.2 %collective-permute-start.4 = (f32[2,16,512]{2,1,0:T(8,128)S(1)}, f32[2,16,512]{2,1,0:T(8,128)S(1)}, u32[]{:S(2)}, u32[]{:S(2)}) collective-permute-start(f32[2,16,512]{2,1,0:T(8,128)S(1)} %get-tuple-element.37), channel_id=1, source_target_pairs={{0,64},{64,0},{128,192},{192,128},{1,65},{65,1},{129,193},{193,129... | collective-permute-start | bytes 196616 | tf_op jit(solution)/shard_map/ppermute | solution.py:418
  18.3 15.1 %collective-permute-start.5 = (f32[2,16,512]{2,1,0:T(8,128)S(1)}, f32[2,16,512]{2,1,0:T(8,128)S(1)}, u32[]{:S(2)}, u32[]{:S(2)}) collective-permute-start(f32[2,16,512]{2,1,0:T(8,128)S(1)} %get-tuple-element.38), channel_id=1, source_target_pairs={{0,128},{64,192},{128,0},{192,64},{1,129},{65,193},{129,1},{193,65... | collective-permute-start | bytes 196616 | tf_op jit(solution)/shard_map/ppermute | solution.py:418
  21.4 12.0 %collective-permute-start.6 = (f32[2,16,512]{2,1,0:T(8,128)S(1)}, f32[2,16,512]{2,1,0:T(8,128)S(1)}, u32[]{:S(2)}, u32[]{:S(2)}) collective-permute-start(f32[2,16,512]{2,1,0:T(8,128)S(1)} %get-tuple-element.39), channel_id=1, source_target_pairs={{0,192},{64,128},{128,64},{192,0},{1,193},{65,129},{129,65},{193,1... | collective-permute-start | bytes 196616 | tf_op jit(solution)/shard_map/ppermute | solution.py:418
  22.2 20.4 %all-to-all-start = ((f32[32,8,128]{2,1,0:T(8,128)}), f32[32,8,128]{2,1,0:T(8,128)S(1)}, u32[]{:S(2)}, u32[]{:S(2)}) async-start(f32[32,8,128]{2,1,0:T(8,128)} %get-tuple-element.33), calls=%async_computation | async-start | bytes 262144 | tf_op jit(solution)/shard_map/all_to_all | solution.py:451
  33.4 1.8 %copy-start.1 = (f32[1,16,4096]{2,1,0:T(8,128)S(1)}, f32[1,16,4096]{2,1,0:T(8,128)}, u32[]{:S(2)}) copy-start(f32[1,16,4096]{2,1,0:T(8,128)} %param.9) | copy-start | bytes 786436
  33.5 1.8 %copy-start.4 = (f32[1,4096]{1,0:T(1,128)S(1)}, f32[1,4096]{1,0:T(1,128)}, u32[]{:S(2)}) copy-start(f32[1,4096]{1,0:T(1,128)} %refs_2_.3) | copy-start | bytes 49156
  33.5 1.8 %copy-start.5 = (f32[1,4096]{1,0:T(1,128)S(1)}, f32[1,4096]{1,0:T(1,128)}, u32[]{:S(2)}) copy-start(f32[1,4096]{1,0:T(1,128)} %refs_3_.3) | copy-start | bytes 49156
  33.5 2.7 %collective-permute-start.7 = (f32[4,16,512]{2,1,0:T(8,128)S(1)}, f32[4,16,512]{2,1,0:T(8,128)S(1)}, u32[]{:S(2)}, u32[]{:S(2)}) collective-permute-start(f32[4,16,512]{2,1,0:T(8,128)S(1)} %pad_maximum_fusion), channel_id=1, source_target_pairs={{0,32},{32,0},{1,33},{33,1},{2,34},{34,2},{3,35},{35,3},{4,36},{36... | collective-permute-start | bytes 393224 | tf_op jit(solution)/shard_map/ppermute | solution.py:415
  36.2 27.3 %copy-start.3 = (f32[4,1,16,4096]{3,2,1,0:T(8,128)S(1)}, f32[4,1,16,4096]{3,2,1,0:T(8,128)}, u32[]{:S(2)}) copy-start(f32[4,1,16,4096]{3,2,1,0:T(8,128)} %param.10) | copy-start | bytes 3145732

commit v5 on v4

--- a/solution.py
+++ b/solution.py
@@ -450,12 +450,12 @@
     )(notes, velocity, *held)
     sums = lax.all_to_all(sums, POS, 0, 0, tiled=True)
     across = [to_chip(across[d - 1], d) for d in range(1, chips)]
-    other = to_core(jnp.stack([other] + [x[1] for x in across]))
+    others = [to_core(other)] + [to_core(x[1]) for x in across]
     local = (velocity, out_rate, inflow, wigner, past_residuals)
     part = f32(chips, cells, share)
     settled = []
     gram = early
-    for flip, shares in enumerate(((own, *across), (other,))):
+    for flip, shares in enumerate(((own, *across), others)):
         reach, rest, gram = call(
             functools.partial(settle_kernel, flip),
             (part, part, f32(16, LANES)),

time: 64.9 us -> 66.1 us (1.018)
  waiting for transfers between devices: 12.8 us -> 7.32 us
  blocking collectives: 20.8 us -> 25.2 us
  starting transfers between devices: 24.3 us -> 26.6 us
    all_to_all x1, waiting for transfers between devices: 6.05 us -> 0.01 us  [body(): sums = lax.all_to_all(sums, POS, 0, 0, tiled=True)]
    all_to_all x1, blocking collectives: 20.8 us -> 25.2 us  [body(): message = lax.all_to_all(message, ALL, 0, 0, tiled=True)]
    ppermute x2 -> x5, starting transfers between devices: 5.05 us -> 7.03 us  [to_core(): return lax.ppermute(x, BAND[1], [(0, 1), (1, 0)])]
    ppermute x6, waiting for transfers between devices: 5.29 us -> 5.96 us  [to_chip(): return lax.ppermute(x, BAND[0], [(i, i ^ d) for i in range(chips)])]
    ppermute x2 -> x5, waiting for transfers between devices: 1.5 us -> 1.35 us  [to_core(): return lax.ppermute(x, BAND[1], [(0, 1), (1, 0)])]
  transfers between devices with their start and end apart: 9 -> 12, of which waited for: 5 -> 6; matrix products, arithmetic and copies ran while one was open for 0% -> 0% of each run, Pallas kernels for 1% -> 1%
where the time goes in v5:
time: 66.1 us; the launch traced here: 65.8 us
  starting transfers between devices  26.6 us (40%)
  blocking collectives  25.2 us (38%)
  waiting for transfers between devices  7.32 us (11%)
  Pallas kernels  5.79 us (9%)
  between operations  0.79 us (1%)
    all_to_all x1, blocking collectives, body(): message = lax.all_to_all(message, ALL, 0, 0, tiled=True)  25.2 us
    all_to_all x1, starting transfers between devices, body(): sums = lax.all_to_all(sums, POS, 0, 0, tiled=True)  11.2 us
    ppermute x6, starting transfers between devices, to_chip(): return lax.ppermute(x, BAND[0], [(i, i ^ d) for i in range(chips)])  8.32 us
    ppermute x5, starting transfers between devices, to_core(): return lax.ppermute(x, BAND[1], [(0, 1), (1, 0)])  7.03 us
    ppermute x6, waiting for transfers between devices, to_chip(): return lax.ppermute(x, BAND[0], [(i, i ^ d) for i in range(chips)])  5.96 us
    pallas_call x1, Pallas kernels, body(): call(open_kernel, (opened, opened, jax.ShapeDtypeStruct((blocks + bands,...  2.3 us
    pallas_call x1, Pallas kernels, body(): call(fold_kernel, (f32(blocks, ROWS, LANES), f32(cells, share), f32(cells...  1.4 us
    ppermute x5, waiting for transfers between devices, to_core(): return lax.ppermute(x, BAND[1], [(0, 1), (1, 0)])  1.35 us
  transfers between devices with their start and end apart: 12, of which 6 were waited for; matrix products, arithmetic and copies ran while one was open for 0% of the time, Pallas kernels for 1%

profile of v5, /device:TPU:1, one launch (start us, length us, event | category | flops | bytes accessed | tf_op | source)
XLA Modules:
  0.0 65.8 jit_solution(13513492816610726200)
XLA Ops:
  0.6 0.0 copy-start
  0.6 2.3 %shard_map.104 = (f32[4,24,512]{2,1,0:T(8,128)S(1)}, f32[4,24,512]{2,1,0:T(8,128)S(1)}, s32[40,128]{1,0:T(8,128)S(1)}) custom-call(s32[1,4096]{1,0:T(1,128)} %bitcast.28, f32[16,4096]{1,0:T(8,128)} %bitcast.21, s32[32]{0:T(128)} %refs_2_.1, s32[8]{0:T(128)} %refs_3_.1, f32[16,4096]{1,0:T(8,128)} %refs_4_.5, f32[1,4096]{1,0:T(1,128)} %refs_5_.5, ...), custom_call_target="tpu_custom_call" | custom-call | flops 5242880 | bytes 2097152 | tf_op jit(solution)/shard_map/pallas_call | solution.py:422
  2.9 3.3 %collective-permute-start = (f32[4,24,512]{2,1,0:T(8,128)S(1)}, f32[4,24,512]{2,1,0:T(8,128)S(1)}, u32[]{:S(2)}, u32[]{:S(2)}) collective-permute-start(f32[4,24,512]{2,1,0:T(8,128)S(1)} %get-tuple-element.28), channel_id=1, source_target_pairs={{0,32},{32,0},{1,33},{33,1},{2,34},{34,2},{3,35},{35,3},{4,36},{36... | collective-permute-start | bytes 589832 | tf_op jit(solution)/shard_map/ppermute | solution.py:415
  6.3 0.0 copy-done
  6.3 0.2 shard_map.105.refs_9_
  6.5 0.8 %collective-permute-done = f32[4,24,512]{2,1,0:T(8,128)S(1)} collective-permute-done((f32[4,24,512]{2,1,0:T(8,128)S(1)}, f32[4,24,512]{2,1,0:T(8,128)S(1)}, u32[]{:S(2)}, u32[]{:S(2)}) %collective-permute-start) | collective-permute-done | bytes 196640 | tf_op jit(solution)/shard_map/ppermute | solution.py:415
  7.4 0.1 collective-permute-start.1
  7.5 0.0 copy-start.2
  7.5 2.0 %collective-permute-start.2 = (f32[2,24,512]{2,1,0:T(8,128)S(1)}, f32[2,24,512]{2,1,0:T(8,128)S(1)}, u32[]{:S(2)}, u32[]{:S(2)}) collective-permute-start(f32[2,24,512]{2,1,0:T(8,128)S(1)} %pad_maximum_fusion.2), channel_id=1, source_target_pairs={{0,128},{64,192},{128,0},{192,64},{1,129},{65,193},{129,1},{193,65... | collective-permute-start | bytes 294920 | tf_op jit(solution)/shard_map/ppermute | solution.py:418
  9.5 2.0 %collective-permute-start.3 = (f32[2,24,512]{2,1,0:T(8,128)S(1)}, f32[2,24,512]{2,1,0:T(8,128)S(1)}, u32[]{:S(2)}, u32[]{:S(2)}) collective-permute-start(f32[2,24,512]{2,1,0:T(8,128)S(1)} %pad_maximum_fusion.3), channel_id=1, source_target_pairs={{0,192},{64,128},{128,64},{192,0},{1,193},{65,129},{129,65},{193,1... | collective-permute-start | bytes 294920 | tf_op jit(solution)/shard_map/ppermute | solution.py:418
  11.5 0.0 collective-permute-done.1.refs_1_
  11.5 2.5 %collective-permute-done.2.refs_2_ = f32[2,24,512]{2,1,0:T(8,128)S(1)} collective-permute-done((f32[2,24,512]{2,1,0:T(8,128)S(1)}, f32[2,24,512]{2,1,0:T(8,128)S(1)}, u32[]{:S(2)}, u32[]{:S(2)}) %collective-permute-start.2) | collective-permute-done | bytes 98336 | tf_op jit(solution)/shard_map/ppermute | solution.py:418
  14.0 2.8 %collective-permute-done.3.refs_3_ = f32[2,24,512]{2,1,0:T(8,128)S(1)} collective-permute-done((f32[2,24,512]{2,1,0:T(8,128)S(1)}, f32[2,24,512]{2,1,0:T(8,128)S(1)}, u32[]{:S(2)}, u32[]{:S(2)}) %collective-permute-start.3) | collective-permute-done | bytes 98336 | tf_op jit(solution)/shard_map/ppermute | solution.py:418
  16.8 0.0 copy-done.2
  16.8 1.4 %shard_map.106 = (f32[32,8,128]{2,1,0:T(8,128)}, f32[16,512]{1,0:T(8,128)S(1)}, f32[16,512]{1,0:T(8,128)S(1)}, f32[2,16,512]{2,1,0:T(8,128)S(1)}, f32[2,16,512]{2,1,0:T(8,128)S(1)}, /*index=5*/f32[2,16,512]{2,1,0:T(8,128)S(1)}) custom-call(s32[40,128]{1,0:T(8,128)S(1)} %get-tuple-element.26.notes, f32[16,4096]{1,0:T(8,128)S(1)} %copy-done.2, ...), custom_call_target="tpu_custom_call" | custom-call | flops 5242880 | bytes 1310720 | tf_op jit(solution)/shard_map/pallas_call | solution.py:442
  18.2 0.0 copy-start.1
  18.2 0.1 collective-permute-start.5
  18.3 11.2 %all-to-all-start = ((f32[32,8,128]{2,1,0:T(8,128)}), f32[32,8,128]{2,1,0:T(8,128)S(1)}, u32[]{:S(2)}, u32[]{:S(2)}) async-start(f32[32,8,128]{2,1,0:T(8,128)} %get-tuple-element.33), calls=%async_computation | async-start | bytes 262144 | tf_op jit(solution)/shard_map/all_to_all | solution.py:451
  29.6 0.9 %collective-permute-start.4 = (f32[16,512]{1,0:T(8,128)S(1)}, f32[16,512]{1,0:T(8,128)S(1)}, u32[]{:S(2)}, u32[]{:S(2)}) collective-permute-start(f32[16,512]{1,0:T(8,128)S(1)} %get-tuple-element.36), channel_id=1, source_target_pairs={{0,32},{32,0},{1,33},{33,1},{2,34},{34,2},{3,35},{35,3},{4,36},{36... | collective-permute-start | bytes 98312 | tf_op jit(solution)/shard_map/ppermute | solution.py:415
  30.4 1.8 %collective-permute-start.7 = (f32[2,16,512]{2,1,0:T(8,128)S(1)}, f32[2,16,512]{2,1,0:T(8,128)S(1)}, u32[]{:S(2)}, u32[]{:S(2)}) collective-permute-start(f32[2,16,512]{2,1,0:T(8,128)S(1)} %get-tuple-element.38), channel_id=1, source_target_pairs={{0,128},{64,192},{128,0},{192,64},{1,129},{65,193},{129,1},{193,65... | collective-permute-start | bytes 196616 | tf_op jit(solution)/shard_map/ppermute | solution.py:418
  32.3 2.3 %collective-permute-start.9 = (f32[2,16,512]{2,1,0:T(8,128)S(1)}, f32[2,16,512]{2,1,0:T(8,128)S(1)}, u32[]{:S(2)}, u32[]{:S(2)}) collective-permute-start(f32[2,16,512]{2,1,0:T(8,128)S(1)} %get-tuple-element.39), channel_id=1, source_target_pairs={{0,192},{64,128},{128,64},{192,0},{1,193},{65,129},{129,65},{193,1... | collective-permute-start | bytes 196616 | tf_op jit(solution)/shard_map/ppermute | solution.py:418
  34.6 0.0 collective-permute-done.5.refs_1_
  34.6 0.6 collective-permute-start.6
  35.2 0.4 collective-permute-done.7.refs_2_
  35.6 0.0 copy-start.4
  35.6 0.0 copy-start.5
  35.6 1.0 %collective-permute-start.8 = (f32[16,512]{1,0:T(8,128)S(1)}, f32[16,512]{1,0:T(8,128)S(1)}, u32[]{:S(2)}, u32[]{:S(2)}) collective-permute-start(f32[16,512]{1,0:T(8,128)S(1)} %slice_bitcast_fusion.1), channel_id=1, source_target_pairs={{0,32},{32,0},{1,33},{33,1},{2,34},{34,2},{3,35},{35,3},{4,36},{36... | collective-permute-start | bytes 98312 | tf_op jit(solution)/shard_map/ppermute | solution.py:415
  36.6 0.3 collective-permute-done.9.refs_3_
  36.9 1.2 %collective-permute-start.10 = (f32[16,512]{1,0:T(8,128)S(1)}, f32[16,512]{1,0:T(8,128)S(1)}, u32[]{:S(2)}, u32[]{:S(2)}) collective-permute-start(f32[16,512]{1,0:T(8,128)S(1)} %slice_bitcast_fusion), channel_id=1, source_target_pairs={{0,32},{32,0},{1,33},{33,1},{2,34},{34,2},{3,35},{35,3},{4,36},{36... | collective-permute-start | bytes 98312 | tf_op jit(solution)/shard_map/ppermute | solution.py:415
  38.1 0.0 copy-done.1
  38.1 0.0 copy-done.4
  38.1 0.0 copy-done.5
  38.1 0.3 shard_map.108
  38.4 0.0 collective-permute-done.4.refs_0_
  38.4 0.0 collective-permute-done.6.refs_1_
  38.4 0.0 collective-permute-done.8.refs_2_
  38.4 0.5 collective-permute-done.10.refs_3_
  39.0 0.0 copy-start.3
  39.0 0.3 shard_map.109
  39.2 0.0 all-to-all-done.sums
  39.2 0.1 shard_map.107
  39.3 0.1 shard_map.110
  39.5 25.2 %all_to_all.16 = f32[256,1,128]{2,1,0:T(1,128)S(1)} all-to-all(f32[256,1,128]{2,1,0:T(1,128)S(1)} %bitcast.27), channel_id=1, replica_groups=mesh['band_0'=4,'band_1'=2,'pos_0'=4,'pos_1'=8] {'band_0','band_1','pos_..., dimensions={0} | all-to-all | bytes 262144 | tf_op jit(solution)/shard_map/all_to_all | solution.py:476
  64.7 0.0 copy-done.3
  64.7 1.1 %shard_map.111 = (f32[16,4096]{1,0:T(8,128)}, f32[16,4096]{1,0:T(8,128)}) custom-call(f32[256,128]{1,0:T(8,128)S(1)} %bitcast.26, f32[4,16,512]{2,1,0:T(8,128)S(1)} %get-tuple-element.44.refs_0_, f32[4,16,512]{2,1,0:T(8,128)S(1)} %get-tuple-element.45.refs_1_, f32[4,16,512]{2,1,0:T(8,128)S(1)} %get-tuple-element.46.refs_2_, ...), custom_call_target="tpu_custom_call" | custom-call | flops 2097152 | bytes 3670016 | tf_op jit(solution)/shard_map/pallas_call | solution.py:477
  (9 shorter events, 0.1 us)
Async XLA Ops:
  0.6 5.6 %copy-start = (f32[4,1,16,4096]{3,2,1,0:T(8,128)S(1)}, f32[4,1,16,4096]{3,2,1,0:T(8,128)}, u32[]{:S(2)}) copy-start(f32[4,1,16,4096]{3,2,1,0:T(8,128)} %param.11) | copy-start | bytes 3145732
  2.9 4.4 %collective-permute-start = (f32[4,24,512]{2,1,0:T(8,128)S(1)}, f32[4,24,512]{2,1,0:T(8,128)S(1)}, u32[]{:S(2)}, u32[]{:S(2)}) collective-permute-start(f32[4,24,512]{2,1,0:T(8,128)S(1)} %get-tuple-element.28), channel_id=1, source_target_pairs={{0,32},{32,0},{1,33},{33,1},{2,34},{34,2},{3,35},{35,3},{4,36},{36... | collective-permute-start | bytes 589832 | tf_op jit(solution)/shard_map/ppermute | solution.py:415
  7.4 4.1 %collective-permute-start.1 = (f32[2,24,512]{2,1,0:T(8,128)S(1)}, f32[2,24,512]{2,1,0:T(8,128)S(1)}, u32[]{:S(2)}, u32[]{:S(2)}) collective-permute-start(f32[2,24,512]{2,1,0:T(8,128)S(1)} %pad_maximum_fusion.1), channel_id=1, source_target_pairs={{0,64},{64,0},{128,192},{192,128},{1,65},{65,1},{129,193},{193,129... | collective-permute-start | bytes 294920 | tf_op jit(solution)/shard_map/ppermute | solution.py:418
  7.5 9.3 %copy-start.2 = (f32[16,4096]{1,0:T(8,128)S(1)}, f32[16,4096]{1,0:T(8,128)}, u32[]{:S(2)}) copy-start(f32[16,4096]{1,0:T(8,128)} %refs_4_.5) | copy-start | bytes 786436
  7.5 6.5 %collective-permute-start.2 = (f32[2,24,512]{2,1,0:T(8,128)S(1)}, f32[2,24,512]{2,1,0:T(8,128)S(1)}, u32[]{:S(2)}, u32[]{:S(2)}) collective-permute-start(f32[2,24,512]{2,1,0:T(8,128)S(1)} %pad_maximum_fusion.2), channel_id=1, source_target_pairs={{0,128},{64,192},{128,0},{192,64},{1,129},{65,193},{129,1},{193,65... | collective-permute-start | bytes 294920 | tf_op jit(solution)/shard_map/ppermute | solution.py:418
  9.5 7.3 %collective-permute-start.3 = (f32[2,24,512]{2,1,0:T(8,128)S(1)}, f32[2,24,512]{2,1,0:T(8,128)S(1)}, u32[]{:S(2)}, u32[]{:S(2)}) collective-permute-start(f32[2,24,512]{2,1,0:T(8,128)S(1)} %pad_maximum_fusion.3), channel_id=1, source_target_pairs={{0,192},{64,128},{128,64},{192,0},{1,193},{65,129},{129,65},{193,1... | collective-permute-start | bytes 294920 | tf_op jit(solution)/shard_map/ppermute | solution.py:418
  18.2 19.9 %copy-start.1 = (f32[1,16,4096]{2,1,0:T(8,128)S(1)}, f32[1,16,4096]{2,1,0:T(8,128)}, u32[]{:S(2)}) copy-start(f32[1,16,4096]{2,1,0:T(8,128)} %param.9) | copy-start | bytes 786436
  18.2 16.3 %collective-permute-start.5 = (f32[2,16,512]{2,1,0:T(8,128)S(1)}, f32[2,16,512]{2,1,0:T(8,128)S(1)}, u32[]{:S(2)}, u32[]{:S(2)}) collective-permute-start(f32[2,16,512]{2,1,0:T(8,128)S(1)} %get-tuple-element.37), channel_id=1, source_target_pairs={{0,64},{64,0},{128,192},{192,128},{1,65},{65,1},{129,193},{193,129... | collective-permute-start | bytes 196616 | tf_op jit(solution)/shard_map/ppermute | solution.py:418
  18.3 20.9 %all-to-all-start = ((f32[32,8,128]{2,1,0:T(8,128)}), f32[32,8,128]{2,1,0:T(8,128)S(1)}, u32[]{:S(2)}, u32[]{:S(2)}) async-start(f32[32,8,128]{2,1,0:T(8,128)} %get-tuple-element.33), calls=%async_computation | async-start | bytes 262144 | tf_op jit(solution)/shard_map/all_to_all | solution.py:451
  29.6 8.8 %collective-permute-start.4 = (f32[16,512]{1,0:T(8,128)S(1)}, f32[16,512]{1,0:T(8,128)S(1)}, u32[]{:S(2)}, u32[]{:S(2)}) collective-permute-start(f32[16,512]{1,0:T(8,128)S(1)} %get-tuple-element.36), channel_id=1, source_target_pairs={{0,32},{32,0},{1,33},{33,1},{2,34},{34,2},{3,35},{35,3},{4,36},{36... | collective-permute-start | bytes 98312 | tf_op jit(solution)/shard_map/ppermute | solution.py:415
  30.4 5.2 %collective-permute-start.7 = (f32[2,16,512]{2,1,0:T(8,128)S(1)}, f32[2,16,512]{2,1,0:T(8,128)S(1)}, u32[]{:S(2)}, u32[]{:S(2)}) collective-permute-start(f32[2,16,512]{2,1,0:T(8,128)S(1)} %get-tuple-element.38), channel_id=1, source_target_pairs={{0,128},{64,192},{128,0},{192,64},{1,129},{65,193},{129,1},{193,65... | collective-permute-start | bytes 196616 | tf_op jit(solution)/shard_map/ppermute | solution.py:418
  32.3 4.6 %collective-permute-start.9 = (f32[2,16,512]{2,1,0:T(8,128)S(1)}, f32[2,16,512]{2,1,0:T(8,128)S(1)}, u32[]{:S(2)}, u32[]{:S(2)}) collective-permute-start(f32[2,16,512]{2,1,0:T(8,128)S(1)} %get-tuple-element.39), channel_id=1, source_target_pairs={{0,192},{64,128},{128,64},{192,0},{1,193},{65,129},{129,65},{193,1... | collective-permute-start | bytes 196616 | tf_op jit(solution)/shard_map/ppermute | solution.py:418
  34.6 3.8 %collective-permute-start.6 = (f32[16,512]{1,0:T(8,128)S(1)}, f32[16,512]{1,0:T(8,128)S(1)}, u32[]{:S(2)}, u32[]{:S(2)}) collective-permute-start(f32[16,512]{1,0:T(8,128)S(1)} %slice_bitcast_fusion.2), channel_id=1, source_target_pairs={{0,32},{32,0},{1,33},{33,1},{2,34},{34,2},{3,35},{35,3},{4,36},{36... | collective-permute-start | bytes 98312 | tf_op jit(solution)/shard_map/ppermute | solution.py:415
  35.6 2.5 %copy-start.4 = (f32[1,4096]{1,0:T(1,128)S(1)}, f32[1,4096]{1,0:T(1,128)}, u32[]{:S(2)}) copy-start(f32[1,4096]{1,0:T(1,128)} %refs_5_.5) | copy-start | bytes 49156
  35.6 2.5 %copy-start.5 = (f32[1,4096]{1,0:T(1,128)S(1)}, f32[1,4096]{1,0:T(1,128)}, u32[]{:S(2)}) copy-start(f32[1,4096]{1,0:T(1,128)} %refs_6_.5) | copy-start | bytes 49156
  35.6 2.8 %collective-permute-start.8 = (f32[16,512]{1,0:T(8,128)S(1)}, f32[16,512]{1,0:T(8,128)S(1)}, u32[]{:S(2)}, u32[]{:S(2)}) collective-permute-start(f32[16,512]{1,0:T(8,128)S(1)} %slice_bitcast_fusion.1), channel_id=1, source_target_pairs={{0,32},{32,0},{1,33},{33,1},{2,34},{34,2},{3,35},{35,3},{4,36},{36... | collective-permute-start | bytes 98312 | tf_op jit(solution)/shard_map/ppermute | solution.py:415
  36.9 2.1 %collective-permute-start.10 = (f32[16,512]{1,0:T(8,128)S(1)}, f32[16,512]{1,0:T(8,128)S(1)}, u32[]{:S(2)}, u32[]{:S(2)}) collective-permute-start(f32[16,512]{1,0:T(8,128)S(1)} %slice_bitcast_fusion), channel_id=1, source_target_pairs={{0,32},{32,0},{1,33},{33,1},{2,34},{34,2},{3,35},{35,3},{4,36},{36... | collective-permute-start | bytes 98312 | tf_op jit(solution)/shard_map/ppermute | solution.py:415
  39.0 25.8 %copy-start.3 = (f32[4,1,16,4096]{3,2,1,0:T(8,128)S(1)}, f32[4,1,16,4096]{3,2,1,0:T(8,128)}, u32[]{:S(2)}) copy-start(f32[4,1,16,4096]{3,2,1,0:T(8,128)} %param.10) | copy-start | bytes 3145732

commit v6 on v5

--- a/solution.py
+++ b/solution.py
@@ -245,18 +245,18 @@
         copy.wait()
 
 
-def settle_kernel(flip, notes, *refs):
+def settle_kernel(plan, notes, *refs):
     shares = refs[:-9]
     velocity, out_rate, inflow, wigner, past_residuals, early, reach_out, rest, gram = refs[-9:]
-    shares = shares if len(shares) > 1 else [shares[0].at[d] for d in range(shares[0].shape[0])]
-    shares = [share if len(share.shape) == 2 else share.at[0] for share in shares]
     per = rest.shape[2] // LANES
     blocks = velocity.shape[1] // LANES
     band = lax.axis_index(BAND)
     acc = [jnp.zeros((ROWS, LANES), jnp.float32) for _ in range(HIST + 1)]
-    for d in range(len(shares)):
+    for which, place, u in plan:
+        d = u // 2
+        source = shares[which] if len(shares[which].shape) == 2 else shares[which].at[place]
         for kt in range(per):
-            kb = (band ^ (2 * d + flip)) * per + kt
+            kb = (band ^ u) * per + kt
             back = flag(notes, kb)
             columns = pl.ds(pl.multiple_of(kb * LANES, LANES), LANES)
             rate = jnp.broadcast_to(out_rate[:, columns], (ROWS, LANES))
@@ -265,7 +265,7 @@
                 v = velocity[half(h), columns]
                 inv = 1.0 / (v + rate)
                 slope.append(v * inv)
-                offset.append(rate * 0.5 * shares[d][half(h), tile(kt)] * inv)
+                offset.append(rate * 0.5 * source[half(h), tile(kt)] * inv)
             edge = at_contact(blocks, back, slope, inflow[:, columns])
             offset = [offset[h] + edge[h] for h in range(2)]
             reach, run, _ = scan_tile(back, slope, offset)
@@ -450,14 +450,17 @@
     )(notes, velocity, *held)
     sums = lax.all_to_all(sums, POS, 0, 0, tiled=True)
     across = [to_chip(across[d - 1], d) for d in range(1, chips)]
-    others = [to_core(other)] + [to_core(x[1]) for x in across]
+    other = [other] + [x[1] for x in across]
+    groups = [[0, 2, 3], [1]]
+    others = [to_core(jnp.stack([other[d] for d in group])) for group in groups]
     local = (velocity, out_rate, inflow, wigner, past_residuals)
     part = f32(chips, cells, share)
     settled = []
     gram = early
-    for flip, shares in enumerate(((own, *across), others)):
+    plans = [(n, 0, 2 * n) for n in range(chips)], [(n, m, 2 * d + 1) for n, g in enumerate(groups) for m, d in enumerate(g)]
+    for plan, shares in zip(plans, ((own, *across), others)):
         reach, rest, gram = call(
-            functools.partial(settle_kernel, flip),
+            functools.partial(settle_kernel, plan),
             (part, part, f32(16, LANES)),
             [VMEM] * (len(shares) + 7),
             size // 64,

time: 66.1 us -> 63.6 us (0.962)
  blocking collectives: 25.2 us -> 22.4 us
  waiting for transfers between devices: 7.32 us -> 8.28 us
    all_to_all x1, blocking collectives: 25.2 us -> 22.4 us  [body(): message = lax.all_to_all(message, ALL, 0, 0, tiled=True)]
    all_to_all x1, waiting for transfers between devices: 0.01 us -> 1.61 us  [body(): sums = lax.all_to_all(sums, POS, 0, 0, tiled=True)]
    all_to_all x1, starting transfers between devices: 11.2 us -> 10.2 us  [body(): sums = lax.all_to_all(sums, POS, 0, 0, tiled=True)]
    ppermute x5 -> x3, starting transfers between devices: 7.03 us -> 7.96 us  [to_core(): return lax.ppermute(x, BAND[1], [(0, 1), (1, 0)])]
    ppermute x6, waiting for transfers between devices: 5.96 us -> 5.29 us  [to_chip(): return lax.ppermute(x, BAND[0], [(i, i ^ d) for i in range(chips)])]
    ppermute x5 -> x3, waiting for transfers between devices: 1.35 us -> 1.38 us  [to_core(): return lax.ppermute(x, BAND[1], [(0, 1), (1, 0)])]
  transfers between devices with their start and end apart: 12 -> 10, of which waited for: 6 -> 5; matrix products, arithmetic and copies ran while one was open for 0% -> 0% of each run, Pallas kernels for 1% -> 1%
where the time goes in v6:
time: 63.6 us; the launch traced here: 63.4 us
  starting transfers between devices  26.1 us (41%)
  blocking collectives  22.4 us (35%)
  waiting for transfers between devices  8.28 us (13%)
  Pallas kernels  5.77 us (9%)
  between operations  0.78 us (1%)
    all_to_all x1, blocking collectives, body(): message = lax.all_to_all(message, ALL, 0, 0, tiled=True)  22.4 us
    all_to_all x1, starting transfers between devices, body(): sums = lax.all_to_all(sums, POS, 0, 0, tiled=True)  10.2 us
    ppermute x3, starting transfers between devices, to_core(): return lax.ppermute(x, BAND[1], [(0, 1), (1, 0)])  7.96 us
    ppermute x6, starting transfers between devices, to_chip(): return lax.ppermute(x, BAND[0], [(i, i ^ d) for i in range(chips)])  7.87 us
    ppermute x6, waiting for transfers between devices, to_chip(): return lax.ppermute(x, BAND[0], [(i, i ^ d) for i in range(chips)])  5.29 us
    pallas_call x1, Pallas kernels, body(): call(open_kernel, (opened, opened, jax.ShapeDtypeStruct((blocks + bands,...  2.3 us
    all_to_all x1, waiting for transfers between devices, body(): sums = lax.all_to_all(sums, POS, 0, 0, tiled=True)  1.61 us
    pallas_call x1, Pallas kernels, body(): call(fold_kernel, (f32(blocks, ROWS, LANES), f32(cells, share), f32(cells...  1.4 us
  transfers between devices with their start and end apart: 10, of which 5 were waited for; matrix products, arithmetic and copies ran while one was open for 0% of the time, Pallas kernels for 1%

profile of v6, /device:TPU:1, one launch (start us, length us, event | category | flops | bytes accessed | tf_op | source)
XLA Modules:
  0.0 63.4 jit_solution(4657147599022324450)
XLA Ops:
  0.6 0.0 copy-start
  0.6 2.3 %shard_map.104 = (f32[4,24,512]{2,1,0:T(8,128)S(1)}, f32[4,24,512]{2,1,0:T(8,128)S(1)}, s32[40,128]{1,0:T(8,128)S(1)}) custom-call(s32[1,4096]{1,0:T(1,128)} %bitcast.24, f32[16,4096]{1,0:T(8,128)} %bitcast.16, s32[32]{0:T(128)} %refs_2_.2, s32[8]{0:T(128)} %refs_3_.2, f32[16,4096]{1,0:T(8,128)} %refs_2_.3, f32[1,4096]{1,0:T(1,128)} %refs_3_.3, ...), custom_call_target="tpu_custom_call" | custom-call | flops 5242880 | bytes 2097152 | tf_op jit(solution)/shard_map/pallas_call | solution.py:422
  2.9 3.3 %collective-permute-start = (f32[4,24,512]{2,1,0:T(8,128)S(1)}, f32[4,24,512]{2,1,0:T(8,128)S(1)}, u32[]{:S(2)}, u32[]{:S(2)}) collective-permute-start(f32[4,24,512]{2,1,0:T(8,128)S(1)} %get-tuple-element.28), channel_id=1, source_target_pairs={{0,32},{32,0},{1,33},{33,1},{2,34},{34,2},{3,35},{35,3},{4,36},{36... | collective-permute-start | bytes 589832 | tf_op jit(solution)/shard_map/ppermute | solution.py:415
  6.3 0.0 copy-done
  6.3 0.2 shard_map.105.refs_9_
  6.5 0.8 %collective-permute-done = f32[4,24,512]{2,1,0:T(8,128)S(1)} collective-permute-done((f32[4,24,512]{2,1,0:T(8,128)S(1)}, f32[4,24,512]{2,1,0:T(8,128)S(1)}, u32[]{:S(2)}, u32[]{:S(2)}) %collective-permute-start) | collective-permute-done | bytes 196640 | tf_op jit(solution)/shard_map/ppermute | solution.py:415
  7.4 0.1 collective-permute-start.1
  7.5 0.0 copy-start.2
  7.5 2.0 %collective-permute-start.2 = (f32[2,24,512]{2,1,0:T(8,128)S(1)}, f32[2,24,512]{2,1,0:T(8,128)S(1)}, u32[]{:S(2)}, u32[]{:S(2)}) collective-permute-start(f32[2,24,512]{2,1,0:T(8,128)S(1)} %pad_maximum_fusion.2), channel_id=1, source_target_pairs={{0,128},{64,192},{128,0},{192,64},{1,129},{65,193},{129,1},{193,65... | collective-permute-start | bytes 294920 | tf_op jit(solution)/shard_map/ppermute | solution.py:418
  9.5 2.0 %collective-permute-start.3 = (f32[2,24,512]{2,1,0:T(8,128)S(1)}, f32[2,24,512]{2,1,0:T(8,128)S(1)}, u32[]{:S(2)}, u32[]{:S(2)}) collective-permute-start(f32[2,24,512]{2,1,0:T(8,128)S(1)} %pad_maximum_fusion.3), channel_id=1, source_target_pairs={{0,192},{64,128},{128,64},{192,0},{1,193},{65,129},{129,65},{193,1... | collective-permute-start | bytes 294920 | tf_op jit(solution)/shard_map/ppermute | solution.py:418
  11.5 0.0 collective-permute-done.1.refs_1_
  11.5 2.5 %collective-permute-done.2.refs_2_ = f32[2,24,512]{2,1,0:T(8,128)S(1)} collective-permute-done((f32[2,24,512]{2,1,0:T(8,128)S(1)}, f32[2,24,512]{2,1,0:T(8,128)S(1)}, u32[]{:S(2)}, u32[]{:S(2)}) %collective-permute-start.2) | collective-permute-done | bytes 98336 | tf_op jit(solution)/shard_map/ppermute | solution.py:418
  14.0 2.8 %collective-permute-done.3.refs_3_ = f32[2,24,512]{2,1,0:T(8,128)S(1)} collective-permute-done((f32[2,24,512]{2,1,0:T(8,128)S(1)}, f32[2,24,512]{2,1,0:T(8,128)S(1)}, u32[]{:S(2)}, u32[]{:S(2)}) %collective-permute-start.3) | collective-permute-done | bytes 98336 | tf_op jit(solution)/shard_map/ppermute | solution.py:418
  16.8 0.0 copy-done.2
  16.8 1.4 %shard_map.106 = (f32[32,8,128]{2,1,0:T(8,128)}, f32[16,512]{1,0:T(8,128)S(1)}, f32[16,512]{1,0:T(8,128)S(1)}, f32[2,16,512]{2,1,0:T(8,128)S(1)}, f32[2,16,512]{2,1,0:T(8,128)S(1)}, /*index=5*/f32[2,16,512]{2,1,0:T(8,128)S(1)}) custom-call(s32[40,128]{1,0:T(8,128)S(1)} %get-tuple-element.26.notes, f32[16,4096]{1,0:T(8,128)S(1)} %copy-done.2, ...), custom_call_target="tpu_custom_call" | custom-call | flops 5242880 | bytes 1310720 | tf_op jit(solution)/shard_map/pallas_call | solution.py:442
  18.2 0.3 collective-permute-start.4
  18.5 1.8 %collective-permute-start.5 = (f32[2,16,512]{2,1,0:T(8,128)S(1)}, f32[2,16,512]{2,1,0:T(8,128)S(1)}, u32[]{:S(2)}, u32[]{:S(2)}) collective-permute-start(f32[2,16,512]{2,1,0:T(8,128)S(1)} %get-tuple-element.38), channel_id=1, source_target_pairs={{0,192},{64,128},{128,64},{192,0},{1,193},{65,129},{129,65},{193,1... | collective-permute-start | bytes 196616 | tf_op jit(solution)/shard_map/ppermute | solution.py:418
  20.3 10.2 %all-to-all-start = ((f32[32,8,128]{2,1,0:T(8,128)}), f32[32,8,128]{2,1,0:T(8,128)S(1)}, u32[]{:S(2)}, u32[]{:S(2)}) async-start(f32[32,8,128]{2,1,0:T(8,128)} %get-tuple-element.33), calls=%async_computation | async-start | bytes 262144 | tf_op jit(solution)/shard_map/all_to_all | solution.py:451
  30.6 0.0 copy-start.1
  30.6 1.7 %collective-permute-start.7 = (f32[2,16,512]{2,1,0:T(8,128)S(1)}, f32[2,16,512]{2,1,0:T(8,128)S(1)}, u32[]{:S(2)}, u32[]{:S(2)}) collective-permute-start(f32[2,16,512]{2,1,0:T(8,128)S(1)} %get-tuple-element.39), channel_id=1, source_target_pairs={{0,64},{64,0},{128,192},{192,128},{1,65},{65,1},{129,193},{193,129... | collective-permute-start | bytes 196616 | tf_op jit(solution)/shard_map/ppermute | solution.py:418
  32.3 0.0 collective-permute-done.4.refs_2_
  32.3 0.0 collective-permute-done.5.refs_3_
  32.3 0.0 copy-start.4
  32.3 0.0 copy-start.5
  32.3 1.7 %collective-permute-start.6 = (f32[3,16,512]{2,1,0:T(8,128)S(1)}, f32[3,16,512]{2,1,0:T(8,128)S(1)}, u32[]{:S(2)}, u32[]{:S(2)}) collective-permute-start(f32[3,16,512]{2,1,0:T(8,128)S(1)} %pad_maximum_fusion.4), channel_id=1, source_target_pairs={{0,32},{32,0},{1,33},{33,1},{2,34},{34,2},{3,35},{35,3},{4,36},{36... | collective-permute-start | bytes 294920 | tf_op jit(solution)/shard_map/ppermute | solution.py:415
  34.1 0.0 collective-permute-done.7.refs_1_
  34.1 2.9 %collective-permute-start.8 = (f32[1,16,512]{2,1,0:T(8,128)S(1)}, f32[1,16,512]{2,1,0:T(8,128)S(1)}, u32[]{:S(2)}, u32[]{:S(2)}) collective-permute-start(f32[1,16,512]{2,1,0:T(8,128)S(1)} %slice.50), channel_id=1, source_target_pairs={{0,32},{32,0},{1,33},{33,1},{2,34},{34,2},{3,35},{35,3},{4,36},{36... | collective-permute-start | bytes 98312 | tf_op jit(solution)/shard_map/ppermute | solution.py:415
  37.0 0.0 copy-done.1
  37.0 0.0 copy-done.4
  37.0 0.0 copy-done.5
  37.0 0.3 shard_map.108
  37.3 0.6 collective-permute-done.8.refs_1_
  37.8 0.0 collective-permute-done.6.refs_0_
  37.8 0.0 copy-start.3
  37.8 0.3 shard_map.109
  38.1 1.6 %all-to-all-done.sums = f32[32,8,128]{2,1,0:T(8,128)S(1)} async-done(((f32[32,8,128]{2,1,0:T(8,128)}), f32[32,8,128]{2,1,0:T(8,128)S(1)}, u32[]{:S(2)}, u32[]{:S(2)}) %all-to-all-start) | async-done | bytes 131104 | tf_op jit(solution)/shard_map/all_to_all | solution.py:451
  39.8 0.1 shard_map.107
  39.8 0.1 shard_map.110
  39.9 22.4 %all_to_all.16 = f32[256,1,128]{2,1,0:T(1,128)S(1)} all-to-all(f32[256,1,128]{2,1,0:T(1,128)S(1)} %bitcast.22), channel_id=1, replica_groups=mesh['band_0'=4,'band_1'=2,'pos_0'=4,'pos_1'=8] {'band_0','band_1','pos_..., dimensions={0} | all-to-all | bytes 262144 | tf_op jit(solution)/shard_map/all_to_all | solution.py:479
  62.3 0.0 copy-done.3
  62.3 1.1 %shard_map.111 = (f32[16,4096]{1,0:T(8,128)}, f32[16,4096]{1,0:T(8,128)}) custom-call(f32[256,128]{1,0:T(8,128)S(1)} %bitcast.21, f32[4,16,512]{2,1,0:T(8,128)S(1)} %get-tuple-element.44.refs_0_, f32[4,16,512]{2,1,0:T(8,128)S(1)} %get-tuple-element.45.refs_1_, f32[4,16,512]{2,1,0:T(8,128)S(1)} %get-tuple-element.46.refs_2_, ...), custom_call_target="tpu_custom_call" | custom-call | flops 2097152 | bytes 3670016 | tf_op jit(solution)/shard_map/pallas_call | solution.py:480
  (10 shorter events, 0.1 us)
Async XLA Ops:
  0.6 5.6 %copy-start = (f32[4,1,16,4096]{3,2,1,0:T(8,128)S(1)}, f32[4,1,16,4096]{3,2,1,0:T(8,128)}, u32[]{:S(2)}) copy-start(f32[4,1,16,4096]{3,2,1,0:T(8,128)} %param.11) | copy-start | bytes 3145732
  2.9 4.4 %collective-permute-start = (f32[4,24,512]{2,1,0:T(8,128)S(1)}, f32[4,24,512]{2,1,0:T(8,128)S(1)}, u32[]{:S(2)}, u32[]{:S(2)}) collective-permute-start(f32[4,24,512]{2,1,0:T(8,128)S(1)} %get-tuple-element.28), channel_id=1, source_target_pairs={{0,32},{32,0},{1,33},{33,1},{2,34},{34,2},{3,35},{35,3},{4,36},{36... | collective-permute-start | bytes 589832 | tf_op jit(solution)/shard_map/ppermute | solution.py:415
  7.4 4.1 %collective-permute-start.1 = (f32[2,24,512]{2,1,0:T(8,128)S(1)}, f32[2,24,512]{2,1,0:T(8,128)S(1)}, u32[]{:S(2)}, u32[]{:S(2)}) collective-permute-start(f32[2,24,512]{2,1,0:T(8,128)S(1)} %pad_maximum_fusion.1), channel_id=1, source_target_pairs={{0,64},{64,0},{128,192},{192,128},{1,65},{65,1},{129,193},{193,129... | collective-permute-start | bytes 294920 | tf_op jit(solution)/shard_map/ppermute | solution.py:418
  7.5 9.3 %copy-start.2 = (f32[16,4096]{1,0:T(8,128)S(1)}, f32[16,4096]{1,0:T(8,128)}, u32[]{:S(2)}) copy-start(f32[16,4096]{1,0:T(8,128)} %refs_2_.3) | copy-start | bytes 786436
  7.5 6.5 %collective-permute-start.2 = (f32[2,24,512]{2,1,0:T(8,128)S(1)}, f32[2,24,512]{2,1,0:T(8,128)S(1)}, u32[]{:S(2)}, u32[]{:S(2)}) collective-permute-start(f32[2,24,512]{2,1,0:T(8,128)S(1)} %pad_maximum_fusion.2), channel_id=1, source_target_pairs={{0,128},{64,192},{128,0},{192,64},{1,129},{65,193},{129,1},{193,65... | collective-permute-start | bytes 294920 | tf_op jit(solution)/shard_map/ppermute | solution.py:418
  9.5 7.3 %collective-permute-start.3 = (f32[2,24,512]{2,1,0:T(8,128)S(1)}, f32[2,24,512]{2,1,0:T(8,128)S(1)}, u32[]{:S(2)}, u32[]{:S(2)}) collective-permute-start(f32[2,24,512]{2,1,0:T(8,128)S(1)} %pad_maximum_fusion.3), channel_id=1, source_target_pairs={{0,192},{64,128},{128,64},{192,0},{1,193},{65,129},{129,65},{193,1... | collective-permute-start | bytes 294920 | tf_op jit(solution)/shard_map/ppermute | solution.py:418
  18.2 14.1 %collective-permute-start.4 = (f32[2,16,512]{2,1,0:T(8,128)S(1)}, f32[2,16,512]{2,1,0:T(8,128)S(1)}, u32[]{:S(2)}, u32[]{:S(2)}) collective-permute-start(f32[2,16,512]{2,1,0:T(8,128)S(1)} %get-tuple-element.37), channel_id=1, source_target_pairs={{0,128},{64,192},{128,0},{192,64},{1,129},{65,193},{129,1},{193,65... | collective-permute-start | bytes 196616 | tf_op jit(solution)/shard_map/ppermute | solution.py:418
  18.5 13.7 %collective-permute-start.5 = (f32[2,16,512]{2,1,0:T(8,128)S(1)}, f32[2,16,512]{2,1,0:T(8,128)S(1)}, u32[]{:S(2)}, u32[]{:S(2)}) collective-permute-start(f32[2,16,512]{2,1,0:T(8,128)S(1)} %get-tuple-element.38), channel_id=1, source_target_pairs={{0,192},{64,128},{128,64},{192,0},{1,193},{65,129},{129,65},{193,1... | collective-permute-start | bytes 196616 | tf_op jit(solution)/shard_map/ppermute | solution.py:418
  20.3 19.4 %all-to-all-start = ((f32[32,8,128]{2,1,0:T(8,128)}), f32[32,8,128]{2,1,0:T(8,128)S(1)}, u32[]{:S(2)}, u32[]{:S(2)}) async-start(f32[32,8,128]{2,1,0:T(8,128)} %get-tuple-element.33), calls=%async_computation | async-start | bytes 262144 | tf_op jit(solution)/shard_map/all_to_all | solution.py:451
  30.6 6.4 %copy-start.1 = (f32[1,16,4096]{2,1,0:T(8,128)S(1)}, f32[1,16,4096]{2,1,0:T(8,128)}, u32[]{:S(2)}) copy-start(f32[1,16,4096]{2,1,0:T(8,128)} %param.9) | copy-start | bytes 786436
  30.6 3.5 %collective-permute-start.7 = (f32[2,16,512]{2,1,0:T(8,128)S(1)}, f32[2,16,512]{2,1,0:T(8,128)S(1)}, u32[]{:S(2)}, u32[]{:S(2)}) collective-permute-start(f32[2,16,512]{2,1,0:T(8,128)S(1)} %get-tuple-element.39), channel_id=1, source_target_pairs={{0,64},{64,0},{128,192},{192,128},{1,65},{65,1},{129,193},{193,129... | collective-permute-start | bytes 196616 | tf_op jit(solution)/shard_map/ppermute | solution.py:418
  32.3 4.7 %copy-start.4 = (f32[1,4096]{1,0:T(1,128)S(1)}, f32[1,4096]{1,0:T(1,128)}, u32[]{:S(2)}) copy-start(f32[1,4096]{1,0:T(1,128)} %refs_3_.3) | copy-start | bytes 49156
  32.3 4.7 %copy-start.5 = (f32[1,4096]{1,0:T(1,128)S(1)}, f32[1,4096]{1,0:T(1,128)}, u32[]{:S(2)}) copy-start(f32[1,4096]{1,0:T(1,128)} %refs_4_.5) | copy-start | bytes 49156
  32.3 5.5 %collective-permute-start.6 = (f32[3,16,512]{2,1,0:T(8,128)S(1)}, f32[3,16,512]{2,1,0:T(8,128)S(1)}, u32[]{:S(2)}, u32[]{:S(2)}) collective-permute-start(f32[3,16,512]{2,1,0:T(8,128)S(1)} %pad_maximum_fusion.4), channel_id=1, source_target_pairs={{0,32},{32,0},{1,33},{33,1},{2,34},{34,2},{3,35},{35,3},{4,36},{36... | collective-permute-start | bytes 294920 | tf_op jit(solution)/shard_map/ppermute | solution.py:415
  34.1 3.8 %collective-permute-start.8 = (f32[1,16,512]{2,1,0:T(8,128)S(1)}, f32[1,16,512]{2,1,0:T(8,128)S(1)}, u32[]{:S(2)}, u32[]{:S(2)}) collective-permute-start(f32[1,16,512]{2,1,0:T(8,128)S(1)} %slice.50), channel_id=1, source_target_pairs={{0,32},{32,0},{1,33},{33,1},{2,34},{34,2},{3,35},{35,3},{4,36},{36... | collective-permute-start | bytes 98312 | tf_op jit(solution)/shard_map/ppermute | solution.py:415
  37.8 24.5 %copy-start.3 = (f32[4,1,16,4096]{3,2,1,0:T(8,128)S(1)}, f32[4,1,16,4096]{3,2,1,0:T(8,128)}, u32[]{:S(2)}) copy-start(f32[4,1,16,4096]{3,2,1,0:T(8,128)} %param.10) | copy-start | bytes 3145732

commit v7 on v6

--- a/solution.py
+++ b/solution.py
@@ -15,6 +15,7 @@
 MIX_STEP = 0.5
 RIDGE_SCALE = 0.0001
 LANES = 128
+FARTHEST_FIRST = (2, 1, 3)
 GROUP = 16
 ROWS = 8
 HIST = 4
@@ -184,6 +185,7 @@
 def fold_kernel(notes, velocity, *refs):
     chips = (len(refs) - 4) // 2
     held, message, own, other, across = refs[:chips], *refs[chips : chips + 3], refs[chips + 3 : -2]
+    held = [held[0]] + [held[1 + FARTHEST_FIRST.index(d)] for d in range(1, chips)]
     ready, gone = refs[-2:]
     bands = 2 * chips
     blocks = message.shape[0]
@@ -435,7 +437,7 @@
     )(*[pltpu.with_memory_space_constraint(x, pltpu.HBM) for x in sources])
     other = to_core(other)
     held = [jnp.stack([own[d], other[d]]) for d in range(chips)]
-    held = held[:1] + [to_chip(held[d], d) for d in range(1, chips)]
+    held = [held[0]] + [to_chip(held[d], d) for d in FARTHEST_FIRST]
     early = call(history_kernel, f32(16, LANES), [VMEM], 8 * size, 4 * size)(past_residuals)
     *held, early = lax.optimization_barrier((*held, early))
     pair = f32(2, cells, share)

time: 63.6 us -> 63.5 us (level)
    ppermute x6, starting transfers between devices: 7.87 us -> 5.49 us  [to_chip(): return lax.ppermute(x, BAND[0], [(i, i ^ d) for i in range(chips)])]
    all_to_all x1, starting transfers between devices: 10.2 us -> 11.3 us  [body(): sums = lax.all_to_all(sums, POS, 0, 0, tiled=True)]
    ppermute x3, starting transfers between devices: 7.96 us -> 8.99 us  [to_core(): return lax.ppermute(x, BAND[1], [(0, 1), (1, 0)])]
    all_to_all x1, blocking collectives: 22.4 us -> 23 us  [body(): message = lax.all_to_all(message, ALL, 0, 0, tiled=True)]
  transfers between devices with their start and end apart: 10 -> 10, of which waited for: 5 -> 7; matrix products, arithmetic and copies ran while one was open for 0% -> 0% of each run, Pallas kernels for 1% -> 1%
where the time goes in v7:
time: 63.5 us; the launch traced here: 63.3 us
  starting transfers between devices  25.8 us (41%)
  blocking collectives  23 us (36%)
  waiting for transfers between devices  7.78 us (12%)
  Pallas kernels  5.77 us (9%)
  between operations  0.79 us (1%)
    all_to_all x1, blocking collectives, body(): message = lax.all_to_all(message, ALL, 0, 0, tiled=True)  23 us
    all_to_all x1, starting transfers between devices, body(): sums = lax.all_to_all(sums, POS, 0, 0, tiled=True)  11.3 us
    ppermute x3, starting transfers between devices, to_core(): return lax.ppermute(x, BAND[1], [(0, 1), (1, 0)])  8.99 us
    ppermute x6, starting transfers between devices, to_chip(): return lax.ppermute(x, BAND[0], [(i, i ^ d) for i in range(chips)])  5.49 us
    ppermute x6, waiting for transfers between devices, to_chip(): return lax.ppermute(x, BAND[0], [(i, i ^ d) for i in range(chips)])  4.85 us
    pallas_call x1, Pallas kernels, body(): call(open_kernel, (opened, opened, jax.ShapeDtypeStruct((blocks + bands,...  2.3 us
    all_to_all x1, waiting for transfers between devices, body(): sums = lax.all_to_all(sums, POS, 0, 0, tiled=True)  1.56 us
    pallas_call x1, Pallas kernels, body(): call(fold_kernel, (f32(blocks, ROWS, LANES), f32(cells, share), f32(cells...  1.4 us
  transfers between devices with their start and end apart: 10, of which 7 were waited for; matrix products, arithmetic and copies ran while one was open for 0% of the time, Pallas kernels for 1%

profile of v7, /device:TPU:1, one launch (start us, length us, event | category | flops | bytes accessed | tf_op | source)
XLA Modules:
  0.0 63.3 jit_solution(11004904251617492547)
XLA Ops:
  0.6 0.0 copy-start
  0.6 2.3 %shard_map.104 = (f32[4,24,512]{2,1,0:T(8,128)S(1)}, f32[4,24,512]{2,1,0:T(8,128)S(1)}, s32[40,128]{1,0:T(8,128)S(1)}) custom-call(s32[1,4096]{1,0:T(1,128)} %bitcast.24, f32[16,4096]{1,0:T(8,128)} %bitcast.16, s32[32]{0:T(128)} %refs_2_.2, s32[8]{0:T(128)} %refs_3_.2, f32[16,4096]{1,0:T(8,128)} %refs_2_.3, f32[1,4096]{1,0:T(1,128)} %refs_3_.3, ...), custom_call_target="tpu_custom_call" | custom-call | flops 5242880 | bytes 2097152 | tf_op jit(solution)/shard_map/pallas_call | solution.py:424
  2.9 3.3 %collective-permute-start = (f32[4,24,512]{2,1,0:T(8,128)S(1)}, f32[4,24,512]{2,1,0:T(8,128)S(1)}, u32[]{:S(2)}, u32[]{:S(2)}) collective-permute-start(f32[4,24,512]{2,1,0:T(8,128)S(1)} %get-tuple-element.28), channel_id=1, source_target_pairs={{0,32},{32,0},{1,33},{33,1},{2,34},{34,2},{3,35},{35,3},{4,36},{36... | collective-permute-start | bytes 589832 | tf_op jit(solution)/shard_map/ppermute | solution.py:417
  6.3 0.0 copy-done
  6.3 0.2 shard_map.105.refs_9_
  6.5 0.8 %collective-permute-done = f32[4,24,512]{2,1,0:T(8,128)S(1)} collective-permute-done((f32[4,24,512]{2,1,0:T(8,128)S(1)}, f32[4,24,512]{2,1,0:T(8,128)S(1)}, u32[]{:S(2)}, u32[]{:S(2)}) %collective-permute-start) | collective-permute-done | bytes 196640 | tf_op jit(solution)/shard_map/ppermute | solution.py:417
  7.4 1.1 %collective-permute-start.1 = (f32[2,24,512]{2,1,0:T(8,128)S(1)}, f32[2,24,512]{2,1,0:T(8,128)S(1)}, u32[]{:S(2)}, u32[]{:S(2)}) collective-permute-start(f32[2,24,512]{2,1,0:T(8,128)S(1)} %pad_maximum_fusion.1), channel_id=1, source_target_pairs={{0,128},{64,192},{128,0},{192,64},{1,129},{65,193},{129,1},{193,65... | collective-permute-start | bytes 294920 | tf_op jit(solution)/shard_map/ppermute | solution.py:420
  8.5 0.0 copy-start.2
  8.5 0.4 collective-permute-start.2
  8.9 2.0 %collective-permute-start.3 = (f32[2,24,512]{2,1,0:T(8,128)S(1)}, f32[2,24,512]{2,1,0:T(8,128)S(1)}, u32[]{:S(2)}, u32[]{:S(2)}) collective-permute-start(f32[2,24,512]{2,1,0:T(8,128)S(1)} %pad_maximum_fusion.3), channel_id=1, source_target_pairs={{0,192},{64,128},{128,64},{192,0},{1,193},{65,129},{129,65},{193,1... | collective-permute-start | bytes 294920 | tf_op jit(solution)/shard_map/ppermute | solution.py:420
  10.9 2.1 %collective-permute-done.1.refs_1_ = f32[2,24,512]{2,1,0:T(8,128)S(1)} collective-permute-done((f32[2,24,512]{2,1,0:T(8,128)S(1)}, f32[2,24,512]{2,1,0:T(8,128)S(1)}, u32[]{:S(2)}, u32[]{:S(2)}) %collective-permute-start.1) | collective-permute-done | bytes 98336 | tf_op jit(solution)/shard_map/ppermute | solution.py:420
  13.0 0.5 collective-permute-done.2.refs_2_
  13.4 1.7 %collective-permute-done.3.refs_3_ = f32[2,24,512]{2,1,0:T(8,128)S(1)} collective-permute-done((f32[2,24,512]{2,1,0:T(8,128)S(1)}, f32[2,24,512]{2,1,0:T(8,128)S(1)}, u32[]{:S(2)}, u32[]{:S(2)}) %collective-permute-start.3) | collective-permute-done | bytes 98336 | tf_op jit(solution)/shard_map/ppermute | solution.py:420
  15.2 0.0 copy-done.2
  15.2 1.4 %shard_map.106 = (f32[32,8,128]{2,1,0:T(8,128)}, f32[16,512]{1,0:T(8,128)S(1)}, f32[16,512]{1,0:T(8,128)S(1)}, f32[2,16,512]{2,1,0:T(8,128)S(1)}, f32[2,16,512]{2,1,0:T(8,128)S(1)}, /*index=5*/f32[2,16,512]{2,1,0:T(8,128)S(1)}) custom-call(s32[40,128]{1,0:T(8,128)S(1)} %get-tuple-element.26.notes, f32[16,4096]{1,0:T(8,128)S(1)} %copy-done.2, ...), custom_call_target="tpu_custom_call" | custom-call | flops 5242880 | bytes 1310720 | tf_op jit(solution)/shard_map/pallas_call | solution.py:444
  16.6 1.3 %collective-permute-start.4 = (f32[2,16,512]{2,1,0:T(8,128)S(1)}, f32[2,16,512]{2,1,0:T(8,128)S(1)}, u32[]{:S(2)}, u32[]{:S(2)}) collective-permute-start(f32[2,16,512]{2,1,0:T(8,128)S(1)} %get-tuple-element.37), channel_id=1, source_target_pairs={{0,128},{64,192},{128,0},{192,64},{1,129},{65,193},{129,1},{193,65... | collective-permute-start | bytes 196616 | tf_op jit(solution)/shard_map/ppermute | solution.py:420
  17.9 0.6 collective-permute-start.5
  18.5 11.3 %all-to-all-start = ((f32[32,8,128]{2,1,0:T(8,128)}), f32[32,8,128]{2,1,0:T(8,128)S(1)}, u32[]{:S(2)}, u32[]{:S(2)}) async-start(f32[32,8,128]{2,1,0:T(8,128)} %get-tuple-element.33), calls=%async_computation | async-start | bytes 262144 | tf_op jit(solution)/shard_map/all_to_all | solution.py:453
  29.8 0.0 copy-start.1
  29.8 0.1 collective-permute-start.7
  29.9 0.0 collective-permute-done.4.refs_2_
  30.0 0.0 collective-permute-done.5.refs_3_
  30.0 0.0 copy-start.4
  30.0 0.0 copy-start.5
  30.0 2.4 %collective-permute-start.6 = (f32[3,16,512]{2,1,0:T(8,128)S(1)}, f32[3,16,512]{2,1,0:T(8,128)S(1)}, u32[]{:S(2)}, u32[]{:S(2)}) collective-permute-start(f32[3,16,512]{2,1,0:T(8,128)S(1)} %pad_maximum_fusion.4), channel_id=1, source_target_pairs={{0,32},{32,0},{1,33},{33,1},{2,34},{34,2},{3,35},{35,3},{4,36},{36... | collective-permute-start | bytes 294920 | tf_op jit(solution)/shard_map/ppermute | solution.py:417
  32.5 0.6 collective-permute-done.7.refs_1_
  33.1 3.2 %collective-permute-start.8 = (f32[1,16,512]{2,1,0:T(8,128)S(1)}, f32[1,16,512]{2,1,0:T(8,128)S(1)}, u32[]{:S(2)}, u32[]{:S(2)}) collective-permute-start(f32[1,16,512]{2,1,0:T(8,128)S(1)} %slice.50), channel_id=1, source_target_pairs={{0,32},{32,0},{1,33},{33,1},{2,34},{34,2},{3,35},{35,3},{4,36},{36... | collective-permute-start | bytes 98312 | tf_op jit(solution)/shard_map/ppermute | solution.py:417
  36.3 0.0 copy-done.1
  36.3 0.0 copy-done.4
  36.3 0.0 copy-done.5
  36.3 0.3 shard_map.108
  36.6 0.6 collective-permute-done.8.refs_1_
  37.1 0.0 collective-permute-done.6.refs_0_
  37.1 0.0 copy-start.3
  37.1 0.3 shard_map.109
  37.4 1.6 %all-to-all-done.sums = f32[32,8,128]{2,1,0:T(8,128)S(1)} async-done(((f32[32,8,128]{2,1,0:T(8,128)}), f32[32,8,128]{2,1,0:T(8,128)S(1)}, u32[]{:S(2)}, u32[]{:S(2)}) %all-to-all-start) | async-done | bytes 131104 | tf_op jit(solution)/shard_map/all_to_all | solution.py:453
  39.0 0.1 shard_map.107
  39.1 0.1 shard_map.110
  39.2 23.0 %all_to_all.16 = f32[256,1,128]{2,1,0:T(1,128)S(1)} all-to-all(f32[256,1,128]{2,1,0:T(1,128)S(1)} %bitcast.22), channel_id=1, replica_groups=mesh['band_0'=4,'band_1'=2,'pos_0'=4,'pos_1'=8] {'band_0','band_1','pos_..., dimensions={0} | all-to-all | bytes 262144 | tf_op jit(solution)/shard_map/all_to_all | solution.py:481
  62.2 0.0 copy-done.3
  62.2 1.1 %shard_map.111 = (f32[16,4096]{1,0:T(8,128)}, f32[16,4096]{1,0:T(8,128)}) custom-call(f32[256,128]{1,0:T(8,128)S(1)} %bitcast.21, f32[4,16,512]{2,1,0:T(8,128)S(1)} %get-tuple-element.44.refs_0_, f32[4,16,512]{2,1,0:T(8,128)S(1)} %get-tuple-element.45.refs_1_, f32[4,16,512]{2,1,0:T(8,128)S(1)} %get-tuple-element.46.refs_2_, ...), custom_call_target="tpu_custom_call" | custom-call | flops 2097152 | bytes 3670016 | tf_op jit(solution)/shard_map/pallas_call | solution.py:482
  (10 shorter events, 0.1 us)
Async XLA Ops:
  0.6 5.6 %copy-start = (f32[4,1,16,4096]{3,2,1,0:T(8,128)S(1)}, f32[4,1,16,4096]{3,2,1,0:T(8,128)}, u32[]{:S(2)}) copy-start(f32[4,1,16,4096]{3,2,1,0:T(8,128)} %param.11) | copy-start | bytes 3145732
  2.9 4.4 %collective-permute-start = (f32[4,24,512]{2,1,0:T(8,128)S(1)}, f32[4,24,512]{2,1,0:T(8,128)S(1)}, u32[]{:S(2)}, u32[]{:S(2)}) collective-permute-start(f32[4,24,512]{2,1,0:T(8,128)S(1)} %get-tuple-element.28), channel_id=1, source_target_pairs={{0,32},{32,0},{1,33},{33,1},{2,34},{34,2},{3,35},{35,3},{4,36},{36... | collective-permute-start | bytes 589832 | tf_op jit(solution)/shard_map/ppermute | solution.py:417
  7.4 5.6 %collective-permute-start.1 = (f32[2,24,512]{2,1,0:T(8,128)S(1)}, f32[2,24,512]{2,1,0:T(8,128)S(1)}, u32[]{:S(2)}, u32[]{:S(2)}) collective-permute-start(f32[2,24,512]{2,1,0:T(8,128)S(1)} %pad_maximum_fusion.1), channel_id=1, source_target_pairs={{0,128},{64,192},{128,0},{192,64},{1,129},{65,193},{129,1},{193,65... | collective-permute-start | bytes 294920 | tf_op jit(solution)/shard_map/ppermute | solution.py:420
  8.5 6.7 %copy-start.2 = (f32[16,4096]{1,0:T(8,128)S(1)}, f32[16,4096]{1,0:T(8,128)}, u32[]{:S(2)}) copy-start(f32[16,4096]{1,0:T(8,128)} %refs_2_.3) | copy-start | bytes 786436
  8.5 5.0 %collective-permute-start.2 = (f32[2,24,512]{2,1,0:T(8,128)S(1)}, f32[2,24,512]{2,1,0:T(8,128)S(1)}, u32[]{:S(2)}, u32[]{:S(2)}) collective-permute-start(f32[2,24,512]{2,1,0:T(8,128)S(1)} %pad_maximum_fusion.2), channel_id=1, source_target_pairs={{0,64},{64,0},{128,192},{192,128},{1,65},{65,1},{129,193},{193,129... | collective-permute-start | bytes 294920 | tf_op jit(solution)/shard_map/ppermute | solution.py:420
  8.9 6.3 %collective-permute-start.3 = (f32[2,24,512]{2,1,0:T(8,128)S(1)}, f32[2,24,512]{2,1,0:T(8,128)S(1)}, u32[]{:S(2)}, u32[]{:S(2)}) collective-permute-start(f32[2,24,512]{2,1,0:T(8,128)S(1)} %pad_maximum_fusion.3), channel_id=1, source_target_pairs={{0,192},{64,128},{128,64},{192,0},{1,193},{65,129},{129,65},{193,1... | collective-permute-start | bytes 294920 | tf_op jit(solution)/shard_map/ppermute | solution.py:420
  16.6 13.4 %collective-permute-start.4 = (f32[2,16,512]{2,1,0:T(8,128)S(1)}, f32[2,16,512]{2,1,0:T(8,128)S(1)}, u32[]{:S(2)}, u32[]{:S(2)}) collective-permute-start(f32[2,16,512]{2,1,0:T(8,128)S(1)} %get-tuple-element.37), channel_id=1, source_target_pairs={{0,128},{64,192},{128,0},{192,64},{1,129},{65,193},{129,1},{193,65... | collective-permute-start | bytes 196616 | tf_op jit(solution)/shard_map/ppermute | solution.py:420
  17.9 12.0 %collective-permute-start.5 = (f32[2,16,512]{2,1,0:T(8,128)S(1)}, f32[2,16,512]{2,1,0:T(8,128)S(1)}, u32[]{:S(2)}, u32[]{:S(2)}) collective-permute-start(f32[2,16,512]{2,1,0:T(8,128)S(1)} %get-tuple-element.38), channel_id=1, source_target_pairs={{0,192},{64,128},{128,64},{192,0},{1,193},{65,129},{129,65},{193,1... | collective-permute-start | bytes 196616 | tf_op jit(solution)/shard_map/ppermute | solution.py:420
  18.5 20.5 %all-to-all-start = ((f32[32,8,128]{2,1,0:T(8,128)}), f32[32,8,128]{2,1,0:T(8,128)S(1)}, u32[]{:S(2)}, u32[]{:S(2)}) async-start(f32[32,8,128]{2,1,0:T(8,128)} %get-tuple-element.33), calls=%async_computation | async-start | bytes 262144 | tf_op jit(solution)/shard_map/all_to_all | solution.py:453
  29.8 6.4 %copy-start.1 = (f32[1,16,4096]{2,1,0:T(8,128)S(1)}, f32[1,16,4096]{2,1,0:T(8,128)}, u32[]{:S(2)}) copy-start(f32[1,16,4096]{2,1,0:T(8,128)} %param.9) | copy-start | bytes 786436
  29.8 3.2 %collective-permute-start.7 = (f32[2,16,512]{2,1,0:T(8,128)S(1)}, f32[2,16,512]{2,1,0:T(8,128)S(1)}, u32[]{:S(2)}, u32[]{:S(2)}) collective-permute-start(f32[2,16,512]{2,1,0:T(8,128)S(1)} %get-tuple-element.39), channel_id=1, source_target_pairs={{0,64},{64,0},{128,192},{192,128},{1,65},{65,1},{129,193},{193,129... | collective-permute-start | bytes 196616 | tf_op jit(solution)/shard_map/ppermute | solution.py:420
  30.0 6.3 %copy-start.4 = (f32[1,4096]{1,0:T(1,128)S(1)}, f32[1,4096]{1,0:T(1,128)}, u32[]{:S(2)}) copy-start(f32[1,4096]{1,0:T(1,128)} %refs_3_.3) | copy-start | bytes 49156
  30.0 6.3 %copy-start.5 = (f32[1,4096]{1,0:T(1,128)S(1)}, f32[1,4096]{1,0:T(1,128)}, u32[]{:S(2)}) copy-start(f32[1,4096]{1,0:T(1,128)} %refs_4_.5) | copy-start | bytes 49156
  30.0 7.1 %collective-permute-start.6 = (f32[3,16,512]{2,1,0:T(8,128)S(1)}, f32[3,16,512]{2,1,0:T(8,128)S(1)}, u32[]{:S(2)}, u32[]{:S(2)}) collective-permute-start(f32[3,16,512]{2,1,0:T(8,128)S(1)} %pad_maximum_fusion.4), channel_id=1, source_target_pairs={{0,32},{32,0},{1,33},{33,1},{2,34},{34,2},{3,35},{35,3},{4,36},{36... | collective-permute-start | bytes 294920 | tf_op jit(solution)/shard_map/ppermute | solution.py:417
  33.1 4.1 %collective-permute-start.8 = (f32[1,16,512]{2,1,0:T(8,128)S(1)}, f32[1,16,512]{2,1,0:T(8,128)S(1)}, u32[]{:S(2)}, u32[]{:S(2)}) collective-permute-start(f32[1,16,512]{2,1,0:T(8,128)S(1)} %slice.50), channel_id=1, source_target_pairs={{0,32},{32,0},{1,33},{33,1},{2,34},{34,2},{3,35},{35,3},{4,36},{36... | collective-permute-start | bytes 98312 | tf_op jit(solution)/shard_map/ppermute | solution.py:417
  37.1 25.1 %copy-start.3 = (f32[4,1,16,4096]{3,2,1,0:T(8,128)S(1)}, f32[4,1,16,4096]{3,2,1,0:T(8,128)}, u32[]{:S(2)}) copy-start(f32[4,1,16,4096]{3,2,1,0:T(8,128)} %param.10) | copy-start | bytes 3145732

commit v8 on v6

--- a/solution.py
+++ b/solution.py
@@ -451,7 +451,7 @@
     sums = lax.all_to_all(sums, POS, 0, 0, tiled=True)
     across = [to_chip(across[d - 1], d) for d in range(1, chips)]
     other = [other] + [x[1] for x in across]
-    groups = [[0, 2, 3], [1]]
+    groups = [[0, 1, 2], [3]]
     others = [to_core(jnp.stack([other[d] for d in group])) for group in groups]
     local = (velocity, out_rate, inflow, wigner, past_residuals)
     part = f32(chips, cells, share)

time: 63.6 us -> 65.9 us (1.036)
  blocking collectives: 22.4 us -> 24.2 us
  starting transfers between devices: 26.1 us -> 26.9 us
    ppermute x6, starting transfers between devices: 7.87 us -> 9.69 us  [to_chip(): return lax.ppermute(x, BAND[0], [(i, i ^ d) for i in range(chips)])]
    all_to_all x1, blocking collectives: 22.4 us -> 24.2 us  [body(): message = lax.all_to_all(message, ALL, 0, 0, tiled=True)]
  transfers between devices with their start and end apart: 10 -> 10, of which waited for: 5 -> 6; matrix products, arithmetic and copies ran while one was open for 0% -> 0% of each run, Pallas kernels for 1% -> 1%
where the time goes in v8:
time: 65.9 us; the launch traced here: 65.7 us
  starting transfers between devices  26.9 us (41%)
  blocking collectives  24.2 us (37%)
  waiting for transfers between devices  7.99 us (12%)
  Pallas kernels  5.77 us (9%)
  between operations  0.79 us (1%)
    all_to_all x1, blocking collectives, body(): message = lax.all_to_all(message, ALL, 0, 0, tiled=True)  24.2 us
    ppermute x6, starting transfers between devices, to_chip(): return lax.ppermute(x, BAND[0], [(i, i ^ d) for i in range(chips)])  9.69 us
    all_to_all x1, starting transfers between devices, body(): sums = lax.all_to_all(sums, POS, 0, 0, tiled=True)  9.64 us
    ppermute x3, starting transfers between devices, to_core(): return lax.ppermute(x, BAND[1], [(0, 1), (1, 0)])  7.54 us
    ppermute x6, waiting for transfers between devices, to_chip(): return lax.ppermute(x, BAND[0], [(i, i ^ d) for i in range(chips)])  5.51 us
    pallas_call x1, Pallas kernels, body(): call(open_kernel, (opened, opened, jax.ShapeDtypeStruct((blocks + bands,...  2.3 us
    pallas_call x1, Pallas kernels, body(): call(fold_kernel, (f32(blocks, ROWS, LANES), f32(cells, share), f32(cells...  1.4 us
    ppermute x3, waiting for transfers between devices, to_core(): return lax.ppermute(x, BAND[1], [(0, 1), (1, 0)])  1.38 us
  transfers between devices with their start and end apart: 10, of which 6 were waited for; matrix products, arithmetic and copies ran while one was open for 0% of the time, Pallas kernels for 1%

profile of v8, /device:TPU:1, one launch (start us, length us, event | category | flops | bytes accessed | tf_op | source)
XLA Modules:
  0.0 65.7 jit_solution(3428961289230495776)
XLA Ops:
  0.6 0.0 copy-start
  0.6 2.3 %shard_map.104 = (f32[4,24,512]{2,1,0:T(8,128)S(1)}, f32[4,24,512]{2,1,0:T(8,128)S(1)}, s32[40,128]{1,0:T(8,128)S(1)}) custom-call(s32[1,4096]{1,0:T(1,128)} %bitcast.24, f32[16,4096]{1,0:T(8,128)} %bitcast.16, s32[32]{0:T(128)} %refs_2_.2, s32[8]{0:T(128)} %refs_3_.2, f32[16,4096]{1,0:T(8,128)} %refs_2_.3, f32[1,4096]{1,0:T(1,128)} %refs_3_.3, ...), custom_call_target="tpu_custom_call" | custom-call | flops 5242880 | bytes 2097152 | tf_op jit(solution)/shard_map/pallas_call | solution.py:422
  2.9 3.3 %collective-permute-start = (f32[4,24,512]{2,1,0:T(8,128)S(1)}, f32[4,24,512]{2,1,0:T(8,128)S(1)}, u32[]{:S(2)}, u32[]{:S(2)}) collective-permute-start(f32[4,24,512]{2,1,0:T(8,128)S(1)} %get-tuple-element.28), channel_id=1, source_target_pairs={{0,32},{32,0},{1,33},{33,1},{2,34},{34,2},{3,35},{35,3},{4,36},{36... | collective-permute-start | bytes 589832 | tf_op jit(solution)/shard_map/ppermute | solution.py:415
  6.3 0.0 copy-done
  6.3 0.2 shard_map.105.refs_9_
  6.5 0.8 %collective-permute-done = f32[4,24,512]{2,1,0:T(8,128)S(1)} collective-permute-done((f32[4,24,512]{2,1,0:T(8,128)S(1)}, f32[4,24,512]{2,1,0:T(8,128)S(1)}, u32[]{:S(2)}, u32[]{:S(2)}) %collective-permute-start) | collective-permute-done | bytes 196640 | tf_op jit(solution)/shard_map/ppermute | solution.py:415
  7.4 0.1 collective-permute-start.1
  7.5 0.0 copy-start.2
  7.5 2.0 %collective-permute-start.2 = (f32[2,24,512]{2,1,0:T(8,128)S(1)}, f32[2,24,512]{2,1,0:T(8,128)S(1)}, u32[]{:S(2)}, u32[]{:S(2)}) collective-permute-start(f32[2,24,512]{2,1,0:T(8,128)S(1)} %pad_maximum_fusion.2), channel_id=1, source_target_pairs={{0,128},{64,192},{128,0},{192,64},{1,129},{65,193},{129,1},{193,65... | collective-permute-start | bytes 294920 | tf_op jit(solution)/shard_map/ppermute | solution.py:418
  9.5 2.0 %collective-permute-start.3 = (f32[2,24,512]{2,1,0:T(8,128)S(1)}, f32[2,24,512]{2,1,0:T(8,128)S(1)}, u32[]{:S(2)}, u32[]{:S(2)}) collective-permute-start(f32[2,24,512]{2,1,0:T(8,128)S(1)} %pad_maximum_fusion.3), channel_id=1, source_target_pairs={{0,192},{64,128},{128,64},{192,0},{1,193},{65,129},{129,65},{193,1... | collective-permute-start | bytes 294920 | tf_op jit(solution)/shard_map/ppermute | solution.py:418
  11.5 0.0 collective-permute-done.1.refs_1_
  11.5 2.5 %collective-permute-done.2.refs_2_ = f32[2,24,512]{2,1,0:T(8,128)S(1)} collective-permute-done((f32[2,24,512]{2,1,0:T(8,128)S(1)}, f32[2,24,512]{2,1,0:T(8,128)S(1)}, u32[]{:S(2)}, u32[]{:S(2)}) %collective-permute-start.2) | collective-permute-done | bytes 98336 | tf_op jit(solution)/shard_map/ppermute | solution.py:418
  14.0 2.8 %collective-permute-done.3.refs_3_ = f32[2,24,512]{2,1,0:T(8,128)S(1)} collective-permute-done((f32[2,24,512]{2,1,0:T(8,128)S(1)}, f32[2,24,512]{2,1,0:T(8,128)S(1)}, u32[]{:S(2)}, u32[]{:S(2)}) %collective-permute-start.3) | collective-permute-done | bytes 98336 | tf_op jit(solution)/shard_map/ppermute | solution.py:418
  16.8 0.0 copy-done.2
  16.8 1.4 %shard_map.106 = (f32[32,8,128]{2,1,0:T(8,128)}, f32[16,512]{1,0:T(8,128)S(1)}, f32[16,512]{1,0:T(8,128)S(1)}, f32[2,16,512]{2,1,0:T(8,128)S(1)}, f32[2,16,512]{2,1,0:T(8,128)S(1)}, /*index=5*/f32[2,16,512]{2,1,0:T(8,128)S(1)}) custom-call(s32[40,128]{1,0:T(8,128)S(1)} %get-tuple-element.26.notes, f32[16,4096]{1,0:T(8,128)S(1)} %copy-done.2, ...), custom_call_target="tpu_custom_call" | custom-call | flops 5242880 | bytes 1310720 | tf_op jit(solution)/shard_map/pallas_call | solution.py:442
  18.2 0.1 collective-permute-start.4
  18.3 3.1 %collective-permute-start.5 = (f32[2,16,512]{2,1,0:T(8,128)S(1)}, f32[2,16,512]{2,1,0:T(8,128)S(1)}, u32[]{:S(2)}, u32[]{:S(2)}) collective-permute-start(f32[2,16,512]{2,1,0:T(8,128)S(1)} %get-tuple-element.38), channel_id=1, source_target_pairs={{0,128},{64,192},{128,0},{192,64},{1,129},{65,193},{129,1},{193,65... | collective-permute-start | bytes 196616 | tf_op jit(solution)/shard_map/ppermute | solution.py:418
  21.4 9.6 %all-to-all-start = ((f32[32,8,128]{2,1,0:T(8,128)}), f32[32,8,128]{2,1,0:T(8,128)S(1)}, u32[]{:S(2)}, u32[]{:S(2)}) async-start(f32[32,8,128]{2,1,0:T(8,128)} %get-tuple-element.33), calls=%async_computation | async-start | bytes 262144 | tf_op jit(solution)/shard_map/all_to_all | solution.py:451
  31.1 0.0 copy-start.1
  31.1 2.4 %collective-permute-start.7 = (f32[2,16,512]{2,1,0:T(8,128)S(1)}, f32[2,16,512]{2,1,0:T(8,128)S(1)}, u32[]{:S(2)}, u32[]{:S(2)}) collective-permute-start(f32[2,16,512]{2,1,0:T(8,128)S(1)} %get-tuple-element.39), channel_id=1, source_target_pairs={{0,192},{64,128},{128,64},{192,0},{1,193},{65,129},{129,65},{193,1... | collective-permute-start | bytes 196616 | tf_op jit(solution)/shard_map/ppermute | solution.py:418
  33.5 0.0 collective-permute-done.4.refs_1_
  33.5 0.0 collective-permute-done.5.refs_2_
  33.5 0.0 copy-start.4
  33.5 0.0 copy-start.5
  33.6 1.7 %collective-permute-start.6 = (f32[3,16,512]{2,1,0:T(8,128)S(1)}, f32[3,16,512]{2,1,0:T(8,128)S(1)}, u32[]{:S(2)}, u32[]{:S(2)}) collective-permute-start(f32[3,16,512]{2,1,0:T(8,128)S(1)} %pad_maximum_fusion.4), channel_id=1, source_target_pairs={{0,32},{32,0},{1,33},{33,1},{2,34},{34,2},{3,35},{35,3},{4,36},{36... | collective-permute-start | bytes 294920 | tf_op jit(solution)/shard_map/ppermute | solution.py:415
  35.3 0.2 collective-permute-done.7.refs_3_
  35.5 2.5 %collective-permute-start.8 = (f32[1,16,512]{2,1,0:T(8,128)S(1)}, f32[1,16,512]{2,1,0:T(8,128)S(1)}, u32[]{:S(2)}, u32[]{:S(2)}) collective-permute-start(f32[1,16,512]{2,1,0:T(8,128)S(1)} %slice.50), channel_id=1, source_target_pairs={{0,32},{32,0},{1,33},{33,1},{2,34},{34,2},{3,35},{35,3},{4,36},{36... | collective-permute-start | bytes 98312 | tf_op jit(solution)/shard_map/ppermute | solution.py:415
  38.0 0.0 copy-done.1
  38.0 0.0 copy-done.4
  38.0 0.0 copy-done.5
  38.0 0.3 shard_map.108
  38.3 0.6 collective-permute-done.8.refs_1_
  38.9 0.0 collective-permute-done.6.refs_0_
  38.9 0.0 copy-start.3
  38.9 0.3 shard_map.109
  39.1 1.1 %all-to-all-done.sums = f32[32,8,128]{2,1,0:T(8,128)S(1)} async-done(((f32[32,8,128]{2,1,0:T(8,128)}), f32[32,8,128]{2,1,0:T(8,128)S(1)}, u32[]{:S(2)}, u32[]{:S(2)}) %all-to-all-start) | async-done | bytes 131104 | tf_op jit(solution)/shard_map/all_to_all | solution.py:451
  40.3 0.1 shard_map.107
  40.3 0.1 shard_map.110
  40.4 24.2 %all_to_all.16 = f32[256,1,128]{2,1,0:T(1,128)S(1)} all-to-all(f32[256,1,128]{2,1,0:T(1,128)S(1)} %bitcast.22), channel_id=1, replica_groups=mesh['band_0'=4,'band_1'=2,'pos_0'=4,'pos_1'=8] {'band_0','band_1','pos_..., dimensions={0} | all-to-all | bytes 262144 | tf_op jit(solution)/shard_map/all_to_all | solution.py:479
  64.6 0.0 copy-done.3
  64.6 1.1 %shard_map.111 = (f32[16,4096]{1,0:T(8,128)}, f32[16,4096]{1,0:T(8,128)}) custom-call(f32[256,128]{1,0:T(8,128)S(1)} %bitcast.21, f32[4,16,512]{2,1,0:T(8,128)S(1)} %get-tuple-element.44.refs_0_, f32[4,16,512]{2,1,0:T(8,128)S(1)} %get-tuple-element.45.refs_1_, f32[4,16,512]{2,1,0:T(8,128)S(1)} %get-tuple-element.46.refs_2_, ...), custom_call_target="tpu_custom_call" | custom-call | flops 2097152 | bytes 3670016 | tf_op jit(solution)/shard_map/pallas_call | solution.py:480
  (10 shorter events, 0.1 us)
Async XLA Ops:
  0.6 5.6 %copy-start = (f32[4,1,16,4096]{3,2,1,0:T(8,128)S(1)}, f32[4,1,16,4096]{3,2,1,0:T(8,128)}, u32[]{:S(2)}) copy-start(f32[4,1,16,4096]{3,2,1,0:T(8,128)} %param.11) | copy-start | bytes 3145732
  2.9 4.4 %collective-permute-start = (f32[4,24,512]{2,1,0:T(8,128)S(1)}, f32[4,24,512]{2,1,0:T(8,128)S(1)}, u32[]{:S(2)}, u32[]{:S(2)}) collective-permute-start(f32[4,24,512]{2,1,0:T(8,128)S(1)} %get-tuple-element.28), channel_id=1, source_target_pairs={{0,32},{32,0},{1,33},{33,1},{2,34},{34,2},{3,35},{35,3},{4,36},{36... | collective-permute-start | bytes 589832 | tf_op jit(solution)/shard_map/ppermute | solution.py:415
  7.4 4.1 %collective-permute-start.1 = (f32[2,24,512]{2,1,0:T(8,128)S(1)}, f32[2,24,512]{2,1,0:T(8,128)S(1)}, u32[]{:S(2)}, u32[]{:S(2)}) collective-permute-start(f32[2,24,512]{2,1,0:T(8,128)S(1)} %pad_maximum_fusion.1), channel_id=1, source_target_pairs={{0,64},{64,0},{128,192},{192,128},{1,65},{65,1},{129,193},{193,129... | collective-permute-start | bytes 294920 | tf_op jit(solution)/shard_map/ppermute | solution.py:418
  7.5 9.3 %copy-start.2 = (f32[16,4096]{1,0:T(8,128)S(1)}, f32[16,4096]{1,0:T(8,128)}, u32[]{:S(2)}) copy-start(f32[16,4096]{1,0:T(8,128)} %refs_2_.3) | copy-start | bytes 786436
  7.5 6.5 %collective-permute-start.2 = (f32[2,24,512]{2,1,0:T(8,128)S(1)}, f32[2,24,512]{2,1,0:T(8,128)S(1)}, u32[]{:S(2)}, u32[]{:S(2)}) collective-permute-start(f32[2,24,512]{2,1,0:T(8,128)S(1)} %pad_maximum_fusion.2), channel_id=1, source_target_pairs={{0,128},{64,192},{128,0},{192,64},{1,129},{65,193},{129,1},{193,65... | collective-permute-start | bytes 294920 | tf_op jit(solution)/shard_map/ppermute | solution.py:418
  9.5 7.3 %collective-permute-start.3 = (f32[2,24,512]{2,1,0:T(8,128)S(1)}, f32[2,24,512]{2,1,0:T(8,128)S(1)}, u32[]{:S(2)}, u32[]{:S(2)}) collective-permute-start(f32[2,24,512]{2,1,0:T(8,128)S(1)} %pad_maximum_fusion.3), channel_id=1, source_target_pairs={{0,192},{64,128},{128,64},{192,0},{1,193},{65,129},{129,65},{193,1... | collective-permute-start | bytes 294920 | tf_op jit(solution)/shard_map/ppermute | solution.py:418
  18.2 15.3 %collective-permute-start.4 = (f32[2,16,512]{2,1,0:T(8,128)S(1)}, f32[2,16,512]{2,1,0:T(8,128)S(1)}, u32[]{:S(2)}, u32[]{:S(2)}) collective-permute-start(f32[2,16,512]{2,1,0:T(8,128)S(1)} %get-tuple-element.37), channel_id=1, source_target_pairs={{0,64},{64,0},{128,192},{192,128},{1,65},{65,1},{129,193},{193,129... | collective-permute-start | bytes 196616 | tf_op jit(solution)/shard_map/ppermute | solution.py:418
  18.3 15.2 %collective-permute-start.5 = (f32[2,16,512]{2,1,0:T(8,128)S(1)}, f32[2,16,512]{2,1,0:T(8,128)S(1)}, u32[]{:S(2)}, u32[]{:S(2)}) collective-permute-start(f32[2,16,512]{2,1,0:T(8,128)S(1)} %get-tuple-element.38), channel_id=1, source_target_pairs={{0,128},{64,192},{128,0},{192,64},{1,129},{65,193},{129,1},{193,65... | collective-permute-start | bytes 196616 | tf_op jit(solution)/shard_map/ppermute | solution.py:418
  21.4 18.8 %all-to-all-start = ((f32[32,8,128]{2,1,0:T(8,128)}), f32[32,8,128]{2,1,0:T(8,128)S(1)}, u32[]{:S(2)}, u32[]{:S(2)}) async-start(f32[32,8,128]{2,1,0:T(8,128)} %get-tuple-element.33), calls=%async_computation | async-start | bytes 262144 | tf_op jit(solution)/shard_map/all_to_all | solution.py:451
  31.1 6.9 %copy-start.1 = (f32[1,16,4096]{2,1,0:T(8,128)S(1)}, f32[1,16,4096]{2,1,0:T(8,128)}, u32[]{:S(2)}) copy-start(f32[1,16,4096]{2,1,0:T(8,128)} %param.9) | copy-start | bytes 786436
  31.1 4.4 %collective-permute-start.7 = (f32[2,16,512]{2,1,0:T(8,128)S(1)}, f32[2,16,512]{2,1,0:T(8,128)S(1)}, u32[]{:S(2)}, u32[]{:S(2)}) collective-permute-start(f32[2,16,512]{2,1,0:T(8,128)S(1)} %get-tuple-element.39), channel_id=1, source_target_pairs={{0,192},{64,128},{128,64},{192,0},{1,193},{65,129},{129,65},{193,1... | collective-permute-start | bytes 196616 | tf_op jit(solution)/shard_map/ppermute | solution.py:418
  33.5 4.5 %copy-start.4 = (f32[1,4096]{1,0:T(1,128)S(1)}, f32[1,4096]{1,0:T(1,128)}, u32[]{:S(2)}) copy-start(f32[1,4096]{1,0:T(1,128)} %refs_3_.3) | copy-start | bytes 49156
  33.5 4.5 %copy-start.5 = (f32[1,4096]{1,0:T(1,128)S(1)}, f32[1,4096]{1,0:T(1,128)}, u32[]{:S(2)}) copy-start(f32[1,4096]{1,0:T(1,128)} %refs_4_.5) | copy-start | bytes 49156
  33.6 5.3 %collective-permute-start.6 = (f32[3,16,512]{2,1,0:T(8,128)S(1)}, f32[3,16,512]{2,1,0:T(8,128)S(1)}, u32[]{:S(2)}, u32[]{:S(2)}) collective-permute-start(f32[3,16,512]{2,1,0:T(8,128)S(1)} %pad_maximum_fusion.4), channel_id=1, source_target_pairs={{0,32},{32,0},{1,33},{33,1},{2,34},{34,2},{3,35},{35,3},{4,36},{36... | collective-permute-start | bytes 294920 | tf_op jit(solution)/shard_map/ppermute | solution.py:415
  35.5 3.4 %collective-permute-start.8 = (f32[1,16,512]{2,1,0:T(8,128)S(1)}, f32[1,16,512]{2,1,0:T(8,128)S(1)}, u32[]{:S(2)}, u32[]{:S(2)}) collective-permute-start(f32[1,16,512]{2,1,0:T(8,128)S(1)} %slice.50), channel_id=1, source_target_pairs={{0,32},{32,0},{1,33},{33,1},{2,34},{34,2},{3,35},{35,3},{4,36},{36... | collective-permute-start | bytes 98312 | tf_op jit(solution)/shard_map/ppermute | solution.py:415
  38.9 25.8 %copy-start.3 = (f32[4,1,16,4096]{3,2,1,0:T(8,128)S(1)}, f32[4,1,16,4096]{3,2,1,0:T(8,128)}, u32[]{:S(2)}) copy-start(f32[4,1,16,4096]{3,2,1,0:T(8,128)} %param.10) | copy-start | bytes 3145732

commit v9 on v8

--- a/solution.py
+++ b/solution.py
@@ -451,7 +451,7 @@
     sums = lax.all_to_all(sums, POS, 0, 0, tiled=True)
     across = [to_chip(across[d - 1], d) for d in range(1, chips)]
     other = [other] + [x[1] for x in across]
-    groups = [[0, 1, 2], [3]]
+    groups = [[0, 3, 2], [1]]
     others = [to_core(jnp.stack([other[d] for d in group])) for group in groups]
     local = (velocity, out_rate, inflow, wigner, past_residuals)
     part = f32(chips, cells, share)

time: 65.9 us -> 64.2 us (0.974)
  starting transfers between devices: 26.9 us -> 25.9 us
  blocking collectives: 24.2 us -> 23.5 us
    ppermute x6, starting transfers between devices: 9.69 us -> 8.99 us  [to_chip(): return lax.ppermute(x, BAND[0], [(i, i ^ d) for i in range(chips)])]
  transfers between devices with their start and end apart: 10 -> 10, of which waited for: 6 -> 5; matrix products, arithmetic and copies ran while one was open for 0% -> 0% of each run, Pallas kernels for 1% -> 1%
where the time goes in v9:
time: 64.2 us; the launch traced here: 64 us
  starting transfers between devices  25.9 us (40%)
  blocking collectives  23.5 us (37%)
  waiting for transfers between devices  7.89 us (12%)
  Pallas kernels  5.77 us (9%)
  between operations  0.78 us (1%)
    all_to_all x1, blocking collectives, body(): message = lax.all_to_all(message, ALL, 0, 0, tiled=True)  23.5 us
    all_to_all x1, starting transfers between devices, body(): sums = lax.all_to_all(sums, POS, 0, 0, tiled=True)  9.74 us
    ppermute x6, starting transfers between devices, to_chip(): return lax.ppermute(x, BAND[0], [(i, i ^ d) for i in range(chips)])  8.99 us
    ppermute x3, starting transfers between devices, to_core(): return lax.ppermute(x, BAND[1], [(0, 1), (1, 0)])  7.14 us
    ppermute x6, waiting for transfers between devices, to_chip(): return lax.ppermute(x, BAND[0], [(i, i ^ d) for i in range(chips)])  5.29 us
    pallas_call x1, Pallas kernels, body(): call(open_kernel, (opened, opened, jax.ShapeDtypeStruct((blocks + bands,...  2.3 us
    pallas_call x1, Pallas kernels, body(): call(fold_kernel, (f32(blocks, ROWS, LANES), f32(cells, share), f32(cells...  1.4 us
    ppermute x3, waiting for transfers between devices, to_core(): return lax.ppermute(x, BAND[1], [(0, 1), (1, 0)])  1.38 us
  transfers between devices with their start and end apart: 10, of which 5 were waited for; matrix products, arithmetic and copies ran while one was open for 0% of the time, Pallas kernels for 1%

profile of v9, /device:TPU:1, one launch (start us, length us, event | category | flops | bytes accessed | tf_op | source)
XLA Modules:
  0.0 64.0 jit_solution(591265784613341589)
XLA Ops:
  0.6 0.0 copy-start
  0.6 2.3 %shard_map.104 = (f32[4,24,512]{2,1,0:T(8,128)S(1)}, f32[4,24,512]{2,1,0:T(8,128)S(1)}, s32[40,128]{1,0:T(8,128)S(1)}) custom-call(s32[1,4096]{1,0:T(1,128)} %bitcast.24, f32[16,4096]{1,0:T(8,128)} %bitcast.16, s32[32]{0:T(128)} %refs_2_.2, s32[8]{0:T(128)} %refs_3_.2, f32[16,4096]{1,0:T(8,128)} %refs_2_.3, f32[1,4096]{1,0:T(1,128)} %refs_3_.3, ...), custom_call_target="tpu_custom_call" | custom-call | flops 5242880 | bytes 2097152 | tf_op jit(solution)/shard_map/pallas_call | solution.py:422
  2.9 3.3 %collective-permute-start = (f32[4,24,512]{2,1,0:T(8,128)S(1)}, f32[4,24,512]{2,1,0:T(8,128)S(1)}, u32[]{:S(2)}, u32[]{:S(2)}) collective-permute-start(f32[4,24,512]{2,1,0:T(8,128)S(1)} %get-tuple-element.28), channel_id=1, source_target_pairs={{0,32},{32,0},{1,33},{33,1},{2,34},{34,2},{3,35},{35,3},{4,36},{36... | collective-permute-start | bytes 589832 | tf_op jit(solution)/shard_map/ppermute | solution.py:415
  6.3 0.0 copy-done
  6.3 0.2 shard_map.105.refs_9_
  6.5 0.8 %collective-permute-done = f32[4,24,512]{2,1,0:T(8,128)S(1)} collective-permute-done((f32[4,24,512]{2,1,0:T(8,128)S(1)}, f32[4,24,512]{2,1,0:T(8,128)S(1)}, u32[]{:S(2)}, u32[]{:S(2)}) %collective-permute-start) | collective-permute-done | bytes 196640 | tf_op jit(solution)/shard_map/ppermute | solution.py:415
  7.4 0.1 collective-permute-start.1
  7.5 0.0 copy-start.2
  7.5 2.0 %collective-permute-start.2 = (f32[2,24,512]{2,1,0:T(8,128)S(1)}, f32[2,24,512]{2,1,0:T(8,128)S(1)}, u32[]{:S(2)}, u32[]{:S(2)}) collective-permute-start(f32[2,24,512]{2,1,0:T(8,128)S(1)} %pad_maximum_fusion.2), channel_id=1, source_target_pairs={{0,128},{64,192},{128,0},{192,64},{1,129},{65,193},{129,1},{193,65... | collective-permute-start | bytes 294920 | tf_op jit(solution)/shard_map/ppermute | solution.py:418
  9.5 2.0 %collective-permute-start.3 = (f32[2,24,512]{2,1,0:T(8,128)S(1)}, f32[2,24,512]{2,1,0:T(8,128)S(1)}, u32[]{:S(2)}, u32[]{:S(2)}) collective-permute-start(f32[2,24,512]{2,1,0:T(8,128)S(1)} %pad_maximum_fusion.3), channel_id=1, source_target_pairs={{0,192},{64,128},{128,64},{192,0},{1,193},{65,129},{129,65},{193,1... | collective-permute-start | bytes 294920 | tf_op jit(solution)/shard_map/ppermute | solution.py:418
  11.5 0.0 collective-permute-done.1.refs_1_
  11.5 2.5 %collective-permute-done.2.refs_2_ = f32[2,24,512]{2,1,0:T(8,128)S(1)} collective-permute-done((f32[2,24,512]{2,1,0:T(8,128)S(1)}, f32[2,24,512]{2,1,0:T(8,128)S(1)}, u32[]{:S(2)}, u32[]{:S(2)}) %collective-permute-start.2) | collective-permute-done | bytes 98336 | tf_op jit(solution)/shard_map/ppermute | solution.py:418
  14.0 2.8 %collective-permute-done.3.refs_3_ = f32[2,24,512]{2,1,0:T(8,128)S(1)} collective-permute-done((f32[2,24,512]{2,1,0:T(8,128)S(1)}, f32[2,24,512]{2,1,0:T(8,128)S(1)}, u32[]{:S(2)}, u32[]{:S(2)}) %collective-permute-start.3) | collective-permute-done | bytes 98336 | tf_op jit(solution)/shard_map/ppermute | solution.py:418
  16.8 0.0 copy-done.2
  16.8 1.4 %shard_map.106 = (f32[32,8,128]{2,1,0:T(8,128)}, f32[16,512]{1,0:T(8,128)S(1)}, f32[16,512]{1,0:T(8,128)S(1)}, f32[2,16,512]{2,1,0:T(8,128)S(1)}, f32[2,16,512]{2,1,0:T(8,128)S(1)}, /*index=5*/f32[2,16,512]{2,1,0:T(8,128)S(1)}) custom-call(s32[40,128]{1,0:T(8,128)S(1)} %get-tuple-element.26.notes, f32[16,4096]{1,0:T(8,128)S(1)} %copy-done.2, ...), custom_call_target="tpu_custom_call" | custom-call | flops 5242880 | bytes 1310720 | tf_op jit(solution)/shard_map/pallas_call | solution.py:442
  18.2 2.0 %collective-permute-start.4 = (f32[2,16,512]{2,1,0:T(8,128)S(1)}, f32[2,16,512]{2,1,0:T(8,128)S(1)}, u32[]{:S(2)}, u32[]{:S(2)}) collective-permute-start(f32[2,16,512]{2,1,0:T(8,128)S(1)} %get-tuple-element.37), channel_id=1, source_target_pairs={{0,192},{64,128},{128,64},{192,0},{1,193},{65,129},{129,65},{193,1... | collective-permute-start | bytes 196616 | tf_op jit(solution)/shard_map/ppermute | solution.py:418
  20.2 0.0 collective-permute-start.5
  20.2 9.7 %all-to-all-start = ((f32[32,8,128]{2,1,0:T(8,128)}), f32[32,8,128]{2,1,0:T(8,128)S(1)}, u32[]{:S(2)}, u32[]{:S(2)}) async-start(f32[32,8,128]{2,1,0:T(8,128)} %get-tuple-element.33), calls=%async_computation | async-start | bytes 262144 | tf_op jit(solution)/shard_map/all_to_all | solution.py:451
  30.0 0.0 copy-start.1
  30.0 2.9 %collective-permute-start.7 = (f32[2,16,512]{2,1,0:T(8,128)S(1)}, f32[2,16,512]{2,1,0:T(8,128)S(1)}, u32[]{:S(2)}, u32[]{:S(2)}) collective-permute-start(f32[2,16,512]{2,1,0:T(8,128)S(1)} %get-tuple-element.39), channel_id=1, source_target_pairs={{0,64},{64,0},{128,192},{192,128},{1,65},{65,1},{129,193},{193,129... | collective-permute-start | bytes 196616 | tf_op jit(solution)/shard_map/ppermute | solution.py:418
  32.9 0.0 collective-permute-done.4.refs_3_
  32.9 0.0 collective-permute-done.5.refs_2_
  32.9 0.0 copy-start.4
  32.9 0.0 copy-start.5
  32.9 1.7 %collective-permute-start.6 = (f32[3,16,512]{2,1,0:T(8,128)S(1)}, f32[3,16,512]{2,1,0:T(8,128)S(1)}, u32[]{:S(2)}, u32[]{:S(2)}) collective-permute-start(f32[3,16,512]{2,1,0:T(8,128)S(1)} %pad_maximum_fusion.4), channel_id=1, source_target_pairs={{0,32},{32,0},{1,33},{33,1},{2,34},{34,2},{3,35},{35,3},{4,36},{36... | collective-permute-start | bytes 294920 | tf_op jit(solution)/shard_map/ppermute | solution.py:415
  34.7 0.0 collective-permute-done.7.refs_1_
  34.7 2.1 %collective-permute-start.8 = (f32[1,16,512]{2,1,0:T(8,128)S(1)}, f32[1,16,512]{2,1,0:T(8,128)S(1)}, u32[]{:S(2)}, u32[]{:S(2)}) collective-permute-start(f32[1,16,512]{2,1,0:T(8,128)S(1)} %slice.50), channel_id=1, source_target_pairs={{0,32},{32,0},{1,33},{33,1},{2,34},{34,2},{3,35},{35,3},{4,36},{36... | collective-permute-start | bytes 98312 | tf_op jit(solution)/shard_map/ppermute | solution.py:415
  36.8 0.0 copy-done.1
  36.8 0.0 copy-done.4
  36.8 0.0 copy-done.5
  36.8 0.3 shard_map.108
  37.1 0.6 collective-permute-done.8.refs_1_
  37.6 0.0 collective-permute-done.6.refs_0_
  37.6 0.0 copy-start.3
  37.6 0.3 shard_map.109
  37.9 1.2 %all-to-all-done.sums = f32[32,8,128]{2,1,0:T(8,128)S(1)} async-done(((f32[32,8,128]{2,1,0:T(8,128)}), f32[32,8,128]{2,1,0:T(8,128)S(1)}, u32[]{:S(2)}, u32[]{:S(2)}) %all-to-all-start) | async-done | bytes 131104 | tf_op jit(solution)/shard_map/all_to_all | solution.py:451
  39.1 0.1 shard_map.107
  39.2 0.1 shard_map.110
  39.3 23.5 %all_to_all.16 = f32[256,1,128]{2,1,0:T(1,128)S(1)} all-to-all(f32[256,1,128]{2,1,0:T(1,128)S(1)} %bitcast.22), channel_id=1, replica_groups=mesh['band_0'=4,'band_1'=2,'pos_0'=4,'pos_1'=8] {'band_0','band_1','pos_..., dimensions={0} | all-to-all | bytes 262144 | tf_op jit(solution)/shard_map/all_to_all | solution.py:479
  62.9 0.0 copy-done.3
  62.9 1.1 %shard_map.111 = (f32[16,4096]{1,0:T(8,128)}, f32[16,4096]{1,0:T(8,128)}) custom-call(f32[256,128]{1,0:T(8,128)S(1)} %bitcast.21, f32[4,16,512]{2,1,0:T(8,128)S(1)} %get-tuple-element.44.refs_0_, f32[4,16,512]{2,1,0:T(8,128)S(1)} %get-tuple-element.45.refs_1_, f32[4,16,512]{2,1,0:T(8,128)S(1)} %get-tuple-element.46.refs_2_, ...), custom_call_target="tpu_custom_call" | custom-call | flops 2097152 | bytes 3670016 | tf_op jit(solution)/shard_map/pallas_call | solution.py:480
  (10 shorter events, 0.1 us)
Async XLA Ops:
  0.6 5.6 %copy-start = (f32[4,1,16,4096]{3,2,1,0:T(8,128)S(1)}, f32[4,1,16,4096]{3,2,1,0:T(8,128)}, u32[]{:S(2)}) copy-start(f32[4,1,16,4096]{3,2,1,0:T(8,128)} %param.11) | copy-start | bytes 3145732
  2.9 4.4 %collective-permute-start = (f32[4,24,512]{2,1,0:T(8,128)S(1)}, f32[4,24,512]{2,1,0:T(8,128)S(1)}, u32[]{:S(2)}, u32[]{:S(2)}) collective-permute-start(f32[4,24,512]{2,1,0:T(8,128)S(1)} %get-tuple-element.28), channel_id=1, source_target_pairs={{0,32},{32,0},{1,33},{33,1},{2,34},{34,2},{3,35},{35,3},{4,36},{36... | collective-permute-start | bytes 589832 | tf_op jit(solution)/shard_map/ppermute | solution.py:415
  7.4 4.1 %collective-permute-start.1 = (f32[2,24,512]{2,1,0:T(8,128)S(1)}, f32[2,24,512]{2,1,0:T(8,128)S(1)}, u32[]{:S(2)}, u32[]{:S(2)}) collective-permute-start(f32[2,24,512]{2,1,0:T(8,128)S(1)} %pad_maximum_fusion.1), channel_id=1, source_target_pairs={{0,64},{64,0},{128,192},{192,128},{1,65},{65,1},{129,193},{193,129... | collective-permute-start | bytes 294920 | tf_op jit(solution)/shard_map/ppermute | solution.py:418
  7.5 9.3 %copy-start.2 = (f32[16,4096]{1,0:T(8,128)S(1)}, f32[16,4096]{1,0:T(8,128)}, u32[]{:S(2)}) copy-start(f32[16,4096]{1,0:T(8,128)} %refs_2_.3) | copy-start | bytes 786436
  7.5 6.5 %collective-permute-start.2 = (f32[2,24,512]{2,1,0:T(8,128)S(1)}, f32[2,24,512]{2,1,0:T(8,128)S(1)}, u32[]{:S(2)}, u32[]{:S(2)}) collective-permute-start(f32[2,24,512]{2,1,0:T(8,128)S(1)} %pad_maximum_fusion.2), channel_id=1, source_target_pairs={{0,128},{64,192},{128,0},{192,64},{1,129},{65,193},{129,1},{193,65... | collective-permute-start | bytes 294920 | tf_op jit(solution)/shard_map/ppermute | solution.py:418
  9.5 7.3 %collective-permute-start.3 = (f32[2,24,512]{2,1,0:T(8,128)S(1)}, f32[2,24,512]{2,1,0:T(8,128)S(1)}, u32[]{:S(2)}, u32[]{:S(2)}) collective-permute-start(f32[2,24,512]{2,1,0:T(8,128)S(1)} %pad_maximum_fusion.3), channel_id=1, source_target_pairs={{0,192},{64,128},{128,64},{192,0},{1,193},{65,129},{129,65},{193,1... | collective-permute-start | bytes 294920 | tf_op jit(solution)/shard_map/ppermute | solution.py:418
  18.2 14.7 %collective-permute-start.4 = (f32[2,16,512]{2,1,0:T(8,128)S(1)}, f32[2,16,512]{2,1,0:T(8,128)S(1)}, u32[]{:S(2)}, u32[]{:S(2)}) collective-permute-start(f32[2,16,512]{2,1,0:T(8,128)S(1)} %get-tuple-element.37), channel_id=1, source_target_pairs={{0,192},{64,128},{128,64},{192,0},{1,193},{65,129},{129,65},{193,1... | collective-permute-start | bytes 196616 | tf_op jit(solution)/shard_map/ppermute | solution.py:418
  20.2 12.6 %collective-permute-start.5 = (f32[2,16,512]{2,1,0:T(8,128)S(1)}, f32[2,16,512]{2,1,0:T(8,128)S(1)}, u32[]{:S(2)}, u32[]{:S(2)}) collective-permute-start(f32[2,16,512]{2,1,0:T(8,128)S(1)} %get-tuple-element.38), channel_id=1, source_target_pairs={{0,128},{64,192},{128,0},{192,64},{1,129},{65,193},{129,1},{193,65... | collective-permute-start | bytes 196616 | tf_op jit(solution)/shard_map/ppermute | solution.py:418
  20.2 18.9 %all-to-all-start = ((f32[32,8,128]{2,1,0:T(8,128)}), f32[32,8,128]{2,1,0:T(8,128)S(1)}, u32[]{:S(2)}, u32[]{:S(2)}) async-start(f32[32,8,128]{2,1,0:T(8,128)} %get-tuple-element.33), calls=%async_computation | async-start | bytes 262144 | tf_op jit(solution)/shard_map/all_to_all | solution.py:451
  30.0 6.8 %copy-start.1 = (f32[1,16,4096]{2,1,0:T(8,128)S(1)}, f32[1,16,4096]{2,1,0:T(8,128)}, u32[]{:S(2)}) copy-start(f32[1,16,4096]{2,1,0:T(8,128)} %param.9) | copy-start | bytes 786436
  30.0 4.7 %collective-permute-start.7 = (f32[2,16,512]{2,1,0:T(8,128)S(1)}, f32[2,16,512]{2,1,0:T(8,128)S(1)}, u32[]{:S(2)}, u32[]{:S(2)}) collective-permute-start(f32[2,16,512]{2,1,0:T(8,128)S(1)} %get-tuple-element.39), channel_id=1, source_target_pairs={{0,64},{64,0},{128,192},{192,128},{1,65},{65,1},{129,193},{193,129... | collective-permute-start | bytes 196616 | tf_op jit(solution)/shard_map/ppermute | solution.py:418
  32.9 3.8 %copy-start.4 = (f32[1,4096]{1,0:T(1,128)S(1)}, f32[1,4096]{1,0:T(1,128)}, u32[]{:S(2)}) copy-start(f32[1,4096]{1,0:T(1,128)} %refs_3_.3) | copy-start | bytes 49156
  32.9 3.8 %copy-start.5 = (f32[1,4096]{1,0:T(1,128)S(1)}, f32[1,4096]{1,0:T(1,128)}, u32[]{:S(2)}) copy-start(f32[1,4096]{1,0:T(1,128)} %refs_4_.5) | copy-start | bytes 49156
  32.9 4.7 %collective-permute-start.6 = (f32[3,16,512]{2,1,0:T(8,128)S(1)}, f32[3,16,512]{2,1,0:T(8,128)S(1)}, u32[]{:S(2)}, u32[]{:S(2)}) collective-permute-start(f32[3,16,512]{2,1,0:T(8,128)S(1)} %pad_maximum_fusion.4), channel_id=1, source_target_pairs={{0,32},{32,0},{1,33},{33,1},{2,34},{34,2},{3,35},{35,3},{4,36},{36... | collective-permute-start | bytes 294920 | tf_op jit(solution)/shard_map/ppermute | solution.py:415
  34.7 3.0 %collective-permute-start.8 = (f32[1,16,512]{2,1,0:T(8,128)S(1)}, f32[1,16,512]{2,1,0:T(8,128)S(1)}, u32[]{:S(2)}, u32[]{:S(2)}) collective-permute-start(f32[1,16,512]{2,1,0:T(8,128)S(1)} %slice.50), channel_id=1, source_target_pairs={{0,32},{32,0},{1,33},{33,1},{2,34},{34,2},{3,35},{35,3},{4,36},{36... | collective-permute-start | bytes 98312 | tf_op jit(solution)/shard_map/ppermute | solution.py:415
  37.6 25.2 %copy-start.3 = (f32[4,1,16,4096]{3,2,1,0:T(8,128)S(1)}, f32[4,1,16,4096]{3,2,1,0:T(8,128)}, u32[]{:S(2)}) copy-start(f32[4,1,16,4096]{3,2,1,0:T(8,128)} %param.10) | copy-start | bytes 3145732
